TPU v7x, 32 devices: a whole 2x2x4 slice. The times are simulated.
32 devices in a mesh: seq: 8 (over z, y), exp: 4 (over x, core).
Axes of the slice: x: 2, y: 2, z: 4, core: 2. Of those that a mesh axis runs over, the one named last changes fastest.
Arguments:
- tokens: bfloat16 [16384, 1536], P('seq'), may hold values from -6 to 6
- segment_ids: int32 [16384], replicated, may hold values from 0 to 4, as said below
- routes: int32 [16384, 6], P(('seq', 'exp')), may hold values from 0 to 63, all different within a row; in each aligned block of 512 rows (0 to 511, 512 to 1023, ...) at most 96 rows name the same one
- gate_weights: float32 [16384, 6], P(('seq', 'exp')), may hold values from 0.08 to 0.3
- cotangent: bfloat16 [16384, 1536], P(('seq', 'exp')), may hold values from -6 to 6
- norm_in: float32 [1536], replicated, may hold values from 0.5 to 1.5
- proj_z: bfloat16 [1536, 3072], P('seq', 'exp'), may hold values from -0.15625 to 0.15625
- proj_x: bfloat16 [1536, 3072], P('seq', 'exp'), may hold values from -0.15625 to 0.15625
- proj_bc: bfloat16 [1536, 256], replicated, may hold values from -0.15625 to 0.15625
- proj_dt: bfloat16 [1536, 48], P('seq', 'exp'), may hold values from -0.078125 to 0.078125
- conv_weight: float32 [4, 3328], replicated, may hold values from -3 to 3
- conv_bias: float32 [3328], replicated, may hold values from -0.5 to 0.5
- dt_bias: float32 [48], replicated, may hold values from -10 to -3
- decay_log: float32 [48], replicated, may hold values from -1 to 1
- skip_gain: float32 [48], replicated, may hold values from 0.5 to 1.5
- gated_gain: float32 [3072], replicated, may hold values from 0.5 to 1.5
- proj_out: bfloat16 [3072, 1536], P('exp', 'seq'), may hold values from -0.109375 to 0.109375
- norm_mid: float32 [1536], replicated, may hold values from 0.5 to 1.5
- expert_gate: bfloat16 [64, 1536, 512], P('exp', 'seq'), may hold values from -0.15625 to 0.15625
- expert_up: bfloat16 [64, 1536, 512], P('exp', 'seq'), may hold values from -0.15625 to 0.15625
- expert_down: bfloat16 [64, 512, 1536], P('exp', None, 'seq'), may hold values from -1 to 1
- shared_gate: bfloat16 [1536, 1024], replicated, may hold values from -0.15625 to 0.15625
- shared_up: bfloat16 [1536, 1024], replicated, may hold values from -0.15625 to 0.15625
- shared_down: bfloat16 [1024, 1536], replicated, may hold values from -0.375 to 0.375
Outputs:
- block_output: bfloat16 [16384, 1536], P(('seq', 'exp'))
- tokens_grad: float32 [16384, 1536], P(('seq', 'exp'))
- grad_norm_in: float32 [1536], replicated
- grad_proj_z: float32 [1536, 3072], P('seq', 'exp')
- grad_proj_x: float32 [1536, 3072], P('seq', 'exp')
- grad_proj_bc: float32 [1536, 256], replicated
- grad_proj_dt: float32 [1536, 48], P('seq', 'exp')
- grad_conv_weight: float32 [4, 3328], replicated
- grad_conv_bias: float32 [3328], replicated
- grad_dt_bias: float32 [48], replicated
- grad_decay_log: float32 [48], replicated
- grad_skip_gain: float32 [48], replicated
- grad_gated_gain: float32 [3072], replicated
- grad_proj_out: float32 [3072, 1536], P('exp', 'seq')
- grad_norm_mid: float32 [1536], replicated
- grad_expert_gate: float32 [64, 1536, 512], P('exp', 'seq')
- grad_expert_up: float32 [64, 1536, 512], P('exp', 'seq')
- grad_expert_down: float32 [64, 512, 1536], P('exp', None, 'seq')
- grad_shared_gate: float32 [1536, 1024], replicated
- grad_shared_up: float32 [1536, 1024], replicated
- grad_shared_down: float32 [1024, 1536], replicated
Inputs may be any that keep to these rules, and one draw needn't show every extreme that they name: `segment_ids`: segment ids never fall along the tokens; tokens with one id form one document. `routes`: in each aligned block of 512 tokens no expert is named by more than 96 assignments.
All inputs are finite; a program needn't handle non-finite values.
Results may differ from a plain program's by a relative error of at most 0.017.
Values may be sent and summed in bfloat16 or wider, within the bound.
No kernel may reach another device: no remote copies, remote signals or barrier semaphores. Data moves between devices by JAX's collectives and lax.ppermute only.
A program may use at most 512 MiB of HBM per device.

v0:
```python
from functools import partial

import jax
import jax.numpy as jnp
from jax import lax
from jax.sharding import PartitionSpec as P

CONV = 4
SPAN = 256


EPS = 1e-05
HIGH = lax.Precision.HIGHEST
FLOOR = -1e30


def passed_along(block, axis, distance):
    devices = range(lax.axis_size(axis))
    route = [(i - distance, i) for i in devices if i - distance in devices]
    return lax.ppermute(block, axis, route)


def entering(part, axis, combine, identity):
    place = lax.axis_index(axis)
    gathered = jax.tree.map(lambda a: lax.all_gather(a, axis), part)
    state = jax.tree.map(lambda a, e: jnp.zeros_like(a) + jnp.asarray(e, a.dtype), part, identity)

    def entering_one(turn, state):
        return combine(
            state, jax.tree.map(lambda a: lax.dynamic_index_in_dim(a, turn, 0, False), gathered)
        )

    return lax.fori_loop(0, place, entering_one, state)


def carried_in(shard, axis, join, neutral):
    count = lax.axis_size(axis)
    place = lax.axis_index(axis)
    ahead = count - 1 - place
    gathered = jax.tree.map(
        lambda a, kind: lax.all_gather(a.astype(kind), axis),
        shard,
        jax.tree.map(lambda a: jnp.bfloat16 if a.dtype == jnp.float32 else a.dtype, shard),
    )
    state = jax.tree.map(lambda a, e: jnp.zeros_like(a) + jnp.asarray(e, a.dtype), shard, neutral)

    def carried_one(turn, state):
        source = count - 1 - turn
        return join(
            state,
            jax.tree.map(
                lambda a, own: lax.dynamic_index_in_dim(a, source, 0, False).astype(own.dtype),
                gathered,
                shard,
            ),
        )

    return lax.fori_loop(0, ahead, carried_one, state)


def rounded(values):
    return lax.optimization_barrier(values.astype(jnp.bfloat16)).astype(jnp.float32)


def matmul(left, right):
    return jnp.dot(left, right, precision=HIGH, preferred_element_type=jnp.float32)


def low_dot(left, right):
    return jnp.dot(left, right, preferred_element_type=jnp.float32)


def rms_scale(values):
    return lax.rsqrt(jnp.mean(values * values, axis=-1, keepdims=True) + EPS)


def silu_slope(values):
    sigmoid_v = jax.nn.sigmoid(values)
    return sigmoid_v * (1.0 + values * (1.0 - sigmoid_v))


def norm_back(grad_normed, gain, normed, scale):
    weighted = grad_normed * gain[None, :]
    return scale * (weighted - normed * jnp.mean(weighted * normed, axis=-1, keepdims=True))


def same_mask(segs_ext, length):
    return jnp.stack(
        [
            (
                segs_ext[tap_index : tap_index + length] == segs_ext[CONV - 1 : CONV - 1 + length]
            ).astype(jnp.float32)
            for tap_index in range(CONV)
        ],
        axis=1,
    )


def conv_apply(source_ext, kernel, offset, same_seg):
    length = same_seg.shape[0]
    total = jnp.zeros((length, kernel.shape[1]), jnp.float32) + offset[None, :]
    for tap_index in range(kernel.shape[0]):
        total = (
            total
            + source_ext[tap_index : tap_index + length]
            * kernel[tap_index][None, :]
            * same_seg[:, tap_index : tap_index + 1]
        )
    return total


def span_step(decay_rates, carry_state, span_data):
    inputs, b_matrix, c_matrix, step_sizes, segs, seg_prev = span_data
    cum_log = jnp.cumsum(step_sizes * decay_rates[None, :], axis=0)
    positions = jnp.arange(inputs.shape[0], dtype=jnp.int32)
    keep_mask = (segs[:, None] == segs[None, :]) & (positions[:, None] >= positions[None, :])
    spread = cum_log.T[:, :, None] - cum_log.T[:, None, :]
    decay_term = jnp.exp(jnp.where(keep_mask[None], spread, FLOOR))
    scores = matmul(c_matrix, b_matrix.T)
    weights = decay_term * scores[None] * step_sizes.T[:, None, :]
    intra_out = jnp.einsum("hts,shp->thp", weights, inputs, precision=HIGH)
    entry_decay = jnp.exp(cum_log) * (segs == seg_prev).astype(jnp.float32)[:, None]
    carried = (
        jnp.einsum("tn,hpn->thp", c_matrix, carry_state, precision=HIGH) * entry_decay[:, :, None]
    )
    last_seg = segs[-1]
    tail_weight = (
        jnp.exp(cum_log[-1][None, :] - cum_log)
        * (segs == last_seg).astype(jnp.float32)[:, None]
        * step_sizes
    )
    kept_decay = jnp.exp(cum_log[-1]) * (last_seg == seg_prev).astype(jnp.float32)
    new_state = carry_state * kept_decay[:, None, None] + jnp.einsum(
        "sh,shp,sn->hpn", tail_weight, inputs, b_matrix, precision=HIGH
    )
    return (new_state, intra_out + carried)


def ssd_spans(inputs, b_matrix, c_matrix, step_sizes, decay_rates, segs, seg_prev, carry_state):
    length, head_count, head_dim = inputs.shape
    span_count = length // SPAN
    span_prev = jnp.concatenate([jnp.reshape(seg_prev, (1,)), segs[SPAN - 1 : length - 1 : SPAN]])
    span_data = (
        inputs.reshape(span_count, SPAN, head_count, head_dim),
        b_matrix.reshape(span_count, SPAN, -1),
        c_matrix.reshape(span_count, SPAN, -1),
        step_sizes.reshape(span_count, SPAN, head_count),
        segs.reshape(span_count, SPAN),
        span_prev,
    )
    final_state, outputs = lax.scan(
        jax.checkpoint(partial(span_step, decay_rates)), carry_state, span_data
    )
    return (outputs.reshape(length, head_count, head_dim), final_state)


def chain_step(earlier, later):
    return (earlier[0] * later[0], later[1] + later[0][:, None, None] * earlier[1])


def edge_rows(rows, offset_by):
    return passed_along(rows, "seq", offset_by)


def exp_move(rows):
    return lax.all_to_all(rows, "exp", split_axis=0, concat_axis=0, tiled=True)


def per_device(
    tokens,
    segment_ids,
    routes,
    gate_weights,
    cotangent,
    norm_in,
    proj_z,
    proj_x,
    proj_bc,
    proj_dt,
    conv_weight,
    conv_bias,
    dt_bias,
    decay_log,
    skip_gain,
    gated_gain,
    proj_out,
    norm_mid,
    expert_gate,
    expert_up,
    expert_down,
    shared_gate,
    shared_up,
    shared_down,
):
    seq_pos = lax.axis_index("seq")
    exp_pos = lax.axis_index("exp")
    exp_count = lax.axis_size("exp")
    seq_count = lax.axis_size("seq")
    length = tokens.shape[0]
    rows_here = routes.shape[0]
    top_count = routes.shape[1]
    inner_width = gated_gain.shape[0]
    state_dim = proj_bc.shape[1] // 2
    model_width = tokens.shape[1]
    weight_z, weight_x, weight_dt, weight_out = (
        lax.all_gather(proj_z, "seq", axis=0, tiled=True),
        lax.all_gather(proj_x, "seq", axis=0, tiled=True),
        lax.all_gather(proj_dt, "seq", axis=0, tiled=True),
        lax.all_gather(proj_out, "seq", axis=1, tiled=True),
    )
    local_width = weight_z.shape[1]
    head_count = weight_dt.shape[1]
    head_dim = local_width // head_count
    col_start = exp_pos * local_width
    head_start = exp_pos * head_count
    tokens_f = tokens.astype(jnp.float32)
    scale_in = rms_scale(tokens_f)
    normed_in = tokens_f * scale_in
    in_low = (normed_in * norm_in[None, :]).astype(jnp.bfloat16)
    in_float = in_low.astype(jnp.float32)
    gate_z = low_dot(in_low, weight_z)
    raw_x = low_dot(in_low, weight_x)
    raw_dt = low_dot(in_low, weight_dt)
    bc_weight = proj_bc.astype(jnp.float32)
    raw_bc = matmul(in_float, bc_weight)
    source = jnp.concatenate([raw_x, raw_bc], axis=1)
    halo_rows = edge_rows(source[length - (CONV - 1) :], 1)
    source_ext = jnp.concatenate([halo_rows, source], axis=0)
    padded_ids = jnp.concatenate([jnp.full((CONV - 1,), -1, jnp.int32), segment_ids])
    segs_ext = lax.dynamic_slice_in_dim(padded_ids, seq_pos * length, length + CONV - 1)
    same_seg = same_mask(segs_ext, length)
    segs_here = segs_ext[CONV - 1 :]
    seg_prev = segs_ext[CONV - 2]
    kernel = jnp.concatenate(
        [
            lax.dynamic_slice_in_dim(conv_weight, col_start, local_width, 1),
            conv_weight[:, inner_width:],
        ],
        axis=1,
    )
    offset = jnp.concatenate(
        [lax.dynamic_slice_in_dim(conv_bias, col_start, local_width, 0), conv_bias[inner_width:]]
    )
    conv_out = conv_apply(source_ext, kernel, offset, same_seg)
    active = jax.nn.silu(conv_out)
    inputs = rounded(active[:, :local_width]).reshape(length, head_count, head_dim)
    b_matrix = rounded(active[:, local_width : local_width + state_dim])
    c_matrix = rounded(active[:, local_width + state_dim :])
    dt_local = lax.dynamic_slice_in_dim(dt_bias, head_start, head_count)
    step_sizes = jax.nn.softplus(raw_dt + dt_local[None, :])
    decay_rates = -jnp.exp(lax.dynamic_slice_in_dim(decay_log, head_start, head_count))
    zero_state = jnp.zeros((head_count, head_dim, state_dim), jnp.float32)
    local_y, local_state = ssd_spans(
        inputs, b_matrix, c_matrix, step_sizes, decay_rates, segs_here, seg_prev, zero_state
    )
    log_decay = jnp.cumsum(step_sizes * decay_rates[None, :], axis=0)
    same_start = (segs_here == seg_prev).astype(jnp.float32)
    from_start = jnp.exp(log_decay) * same_start[:, None]
    through = jnp.exp(log_decay[-1]) * same_start[-1]
    unused_a, state_in = entering(
        (through, local_state), "seq", chain_step, (jnp.ones_like(through), zero_state)
    )
    scan_y = (
        local_y
        + jnp.einsum("tn,hpn->thp", c_matrix, state_in, precision=HIGH) * from_start[:, :, None]
    )
    skip_local = lax.dynamic_slice_in_dim(skip_gain, head_start, head_count)
    full_y = (scan_y + skip_local[None, :, None] * inputs).reshape(length, local_width)
    gate_act = jax.nn.silu(gate_z)
    gated = full_y * gate_act
    gain_local = lax.dynamic_slice_in_dim(gated_gain, col_start, local_width)
    scaled_low = (gated * gain_local[None, :]).astype(jnp.bfloat16)
    mixer_part = low_dot(scaled_low, weight_out)
    square_part = jnp.sum(gated * gated, axis=1)
    mixer_rows, square_rows = (
        lax.psum_scatter(mixer_part, "exp", scatter_dimension=0, tiled=True),
        lax.psum_scatter(square_part, "exp", scatter_dimension=0, tiled=True),
    )
    scale_mix = lax.rsqrt(square_rows[:, None] / inner_width + EPS)
    residual = (
        lax.dynamic_slice_in_dim(tokens_f, exp_pos * rows_here, rows_here) + scale_mix * mixer_rows
    )
    scale_mid = rms_scale(residual)
    normed_mid = residual * scale_mid
    mid_low = (normed_mid * norm_mid[None, :]).astype(jnp.bfloat16)
    shared_a = low_dot(mid_low, shared_gate)
    shared_b = low_dot(mid_low, shared_up)
    shared_hid = (jax.nn.silu(shared_a) * shared_b).astype(jnp.bfloat16)
    shared_out = low_dot(shared_hid, shared_down)
    experts_here = expert_gate.shape[0]
    experts_all = experts_here * exp_count
    copies = max(1, seq_count // experts_here)
    capacity = 2 * rows_here * top_count // experts_all
    part_cap = capacity // copies
    flat_routes = routes.reshape(-1)
    onehot = (flat_routes[:, None] == jnp.arange(experts_all, dtype=jnp.int32)[None, :]).astype(
        jnp.int32
    )
    slot_number = jnp.sum((jnp.cumsum(onehot, axis=0) - 1) * onehot, axis=1)
    slot_place = flat_routes * capacity + slot_number % copies * part_cap + slot_number // copies
    token_owner = jnp.arange(rows_here * top_count, dtype=jnp.int32) // top_count
    slot_owner = (
        jnp.full((experts_all * capacity,), rows_here, jnp.int32).at[slot_place].set(token_owner)
    )
    mid_pad = jnp.concatenate([mid_low, jnp.zeros((1, model_width), jnp.bfloat16)], axis=0)
    arrived = exp_move(mid_pad[slot_owner])
    gate_full, up_full, down_full = (
        lax.all_gather(expert_gate, "seq", axis=1, tiled=True),
        lax.all_gather(expert_up, "seq", axis=1, tiled=True),
        lax.all_gather(expert_down, "seq", axis=2, tiled=True),
    )
    got = arrived.reshape(exp_count, experts_here, capacity, model_width)
    hidden_a = jnp.einsum("secd,edf->secf", got, gate_full, preferred_element_type=jnp.float32)
    hidden_b = jnp.einsum("secd,edf->secf", got, up_full, preferred_element_type=jnp.float32)
    expert_hid = (jax.nn.silu(hidden_a) * hidden_b).astype(jnp.bfloat16)
    expert_res = jnp.einsum(
        "secf,efd->secd", expert_hid, down_full, preferred_element_type=jnp.float32
    ).astype(jnp.bfloat16)
    returned = exp_move(expert_res.reshape(-1, model_width))
    picked = returned[slot_place].reshape(rows_here, top_count, model_width)
    routed = jnp.zeros_like(residual)
    for pick_index in range(top_count):
        routed = routed + gate_weights[:, pick_index : pick_index + 1] * picked[
            :, pick_index
        ].astype(jnp.float32)
    block_output = (residual + shared_out + routed).astype(jnp.bfloat16)
    grad_out = cotangent.astype(jnp.float32)
    sent_grad = (
        (gate_weights[:, :, None] * grad_out[:, None, :])
        .astype(jnp.bfloat16)
        .reshape(rows_here * top_count, model_width)
    )
    grad_slots = (
        jnp.zeros((experts_all * capacity, model_width), jnp.bfloat16).at[slot_place].set(sent_grad)
    )
    grad_arrived = exp_move(grad_slots)
    grad_got = grad_arrived.reshape(got.shape)
    grad_hid = jnp.einsum("secd,efd->secf", grad_got, down_full, preferred_element_type=jnp.float32)
    grad_down_e = jnp.einsum(
        "secf,secd->efd", expert_hid, grad_got, preferred_element_type=jnp.float32
    )
    grad_a = (grad_hid * hidden_b * silu_slope(hidden_a)).astype(jnp.bfloat16)
    grad_b = (grad_hid * jax.nn.silu(hidden_a)).astype(jnp.bfloat16)
    grad_gate_e = jnp.einsum("secd,secf->edf", got, grad_a, preferred_element_type=jnp.float32)
    grad_up_e = jnp.einsum("secd,secf->edf", got, grad_b, preferred_element_type=jnp.float32)
    grad_rows = (
        jnp.einsum("secf,edf->secd", grad_a, gate_full, preferred_element_type=jnp.float32)
        + jnp.einsum("secf,edf->secd", grad_b, up_full, preferred_element_type=jnp.float32)
    ).astype(jnp.bfloat16)
    grad_back = exp_move(grad_rows.reshape(-1, model_width))
    grad_mid = jnp.sum(
        grad_back[slot_place].reshape(rows_here, top_count, model_width).astype(jnp.float32), axis=1
    )
    grad_shid = low_dot(cotangent, shared_down.T)
    grad_shared_down = low_dot(shared_hid.T, cotangent)
    grad_sa = (grad_shid * shared_b * silu_slope(shared_a)).astype(jnp.bfloat16)
    grad_sb = (grad_shid * jax.nn.silu(shared_a)).astype(jnp.bfloat16)
    grad_shared_gate = low_dot(mid_low.T, grad_sa)
    grad_shared_up = low_dot(mid_low.T, grad_sb)
    grad_mid = grad_mid + low_dot(grad_sa, shared_gate.T) + low_dot(grad_sb, shared_up.T)
    grad_norm_mid = jnp.sum(grad_mid * normed_mid, axis=0)
    grad_resid = grad_out + norm_back(grad_mid, norm_mid, normed_mid, scale_mid)
    grad_part = (scale_mix * grad_resid).astype(jnp.bfloat16)
    grad_square = (
        jnp.sum(grad_resid * mixer_rows, axis=1) * -0.5 * scale_mix[:, 0] ** 3 / inner_width
    ).astype(jnp.bfloat16)
    grad_part_all, grad_square_all = (
        lax.all_gather(grad_part, "exp", axis=0, tiled=True),
        lax.all_gather(grad_square, "exp", axis=0, tiled=True),
    )
    grad_scaled = low_dot(grad_part_all, weight_out.T)
    grad_wout = low_dot(scaled_low.T, grad_part_all)
    grad_gated = (
        grad_scaled * gain_local[None, :]
        + 2.0 * gated * grad_square_all.astype(jnp.float32)[:, None]
    )
    grad_gain_local = jnp.sum(grad_scaled * gated, axis=0)
    grad_full_y = (grad_gated * gate_act).reshape(length, head_count, head_dim)
    grad_z = (grad_gated * full_y * silu_slope(gate_z)).astype(jnp.bfloat16)
    grad_skip_local = jnp.sum(grad_full_y * inputs, axis=(0, 2))
    direct = jnp.einsum("th,thp,tn->hpn", from_start, grad_full_y, c_matrix, precision=HIGH)
    unused_b, state_out_grad = carried_in(
        (through, direct), "seq", chain_step, (jnp.ones_like(through), zero_state)
    )

    def local_scan(scan_inputs, scan_b, scan_c, scan_steps, scan_rates, scan_state):
        return ssd_spans(
            scan_inputs, scan_b, scan_c, scan_steps, scan_rates, segs_here, seg_prev, scan_state
        )

    unused_c, scan_pull = jax.vjp(
        local_scan, inputs, b_matrix, c_matrix, step_sizes, decay_rates, state_in
    )
    grad_inputs, grad_bmat, grad_cmat, grad_steps, grad_rates, unused_d = scan_pull(
        (grad_full_y, state_out_grad)
    )
    grad_inputs = grad_inputs + skip_local[None, :, None] * grad_full_y
    grad_dt_raw = grad_steps * jax.nn.sigmoid(raw_dt + dt_local[None, :])
    grad_dtb_local = jnp.sum(grad_dt_raw, axis=0)
    grad_decay_local = grad_rates * decay_rates
    grad_active = jnp.concatenate(
        [grad_inputs.reshape(length, local_width), grad_bmat, grad_cmat], axis=1
    )
    grad_conv_out = grad_active * silu_slope(conv_out)

    def conv_local(conv_ext, conv_kernel, conv_offset):
        return conv_apply(conv_ext, conv_kernel, conv_offset, same_seg)

    unused_e, conv_pull = jax.vjp(conv_local, source_ext, kernel, offset)
    grad_ext, grad_kernel, grad_offset = conv_pull(grad_conv_out)
    edge_back = edge_rows(grad_ext[: CONV - 1], -1)
    grad_source = grad_ext[CONV - 1 :] + jnp.concatenate(
        [jnp.zeros((length - (CONV - 1), grad_ext.shape[1]), jnp.float32), edge_back], axis=0
    )
    grad_x = grad_source[:, :local_width].astype(jnp.bfloat16)
    grad_bc = grad_source[:, local_width:]
    grad_dt = grad_dt_raw.astype(jnp.bfloat16)
    grad_in = (
        low_dot(grad_z, weight_z.T)
        + low_dot(grad_x, weight_x.T)
        + low_dot(grad_dt, weight_dt.T)
        + matmul(grad_bc, bc_weight.T)
    )
    grad_wz = low_dot(in_low.T, grad_z)
    grad_wx = low_dot(in_low.T, grad_x)
    grad_wdt = low_dot(in_low.T, grad_dt)
    grad_wbc = matmul(in_float.T, grad_bc)
    grad_norm_in = jnp.sum(grad_in * normed_in, axis=0)
    grad_in_part = norm_back(grad_in, norm_in, normed_in, scale_in)
    tokens_grad = grad_resid + lax.psum_scatter(
        grad_in_part.astype(jnp.bfloat16), "exp", scatter_dimension=0, tiled=True
    ).astype(jnp.float32)
    sum_wz, sum_wx, sum_wdt, sum_wout, sum_gate_e, sum_up_e, sum_down_e = (
        lax.psum_scatter(
            grad_wz.astype(jnp.bfloat16), "seq", scatter_dimension=0, tiled=True
        ).astype(jnp.float32),
        lax.psum_scatter(
            grad_wx.astype(jnp.bfloat16), "seq", scatter_dimension=0, tiled=True
        ).astype(jnp.float32),
        lax.psum_scatter(
            grad_wdt.astype(jnp.bfloat16), "seq", scatter_dimension=0, tiled=True
        ).astype(jnp.float32),
        lax.psum_scatter(
            grad_wout.astype(jnp.bfloat16), "seq", scatter_dimension=1, tiled=True
        ).astype(jnp.float32),
        lax.psum_scatter(
            grad_gate_e.astype(jnp.bfloat16), "seq", scatter_dimension=1, tiled=True
        ).astype(jnp.float32),
        lax.psum_scatter(
            grad_up_e.astype(jnp.bfloat16), "seq", scatter_dimension=1, tiled=True
        ).astype(jnp.float32),
        lax.psum_scatter(
            grad_down_e.astype(jnp.bfloat16), "seq", scatter_dimension=2, tiled=True
        ).astype(jnp.float32),
    )
    head_total = dt_bias.shape[0]
    conv_grad_full = jnp.concatenate(
        [
            lax.dynamic_update_slice_in_dim(
                jnp.zeros((kernel.shape[0], inner_width), jnp.float32),
                grad_kernel[:, :local_width],
                col_start,
                1,
            ),
            grad_kernel[:, local_width:],
        ],
        axis=1,
    )
    bias_grad_full = jnp.concatenate(
        [
            lax.dynamic_update_slice_in_dim(
                jnp.zeros((inner_width,), jnp.float32), grad_offset[:local_width], col_start, 0
            ),
            grad_offset[local_width:],
        ]
    )
    dtb_full = lax.dynamic_update_slice_in_dim(
        jnp.zeros((head_total,), jnp.float32), grad_dtb_local, head_start, 0
    )
    decay_full = lax.dynamic_update_slice_in_dim(
        jnp.zeros((head_total,), jnp.float32), grad_decay_local, head_start, 0
    )
    skip_full = lax.dynamic_update_slice_in_dim(
        jnp.zeros((head_total,), jnp.float32), grad_skip_local, head_start, 0
    )
    gain_full = lax.dynamic_update_slice_in_dim(
        jnp.zeros((inner_width,), jnp.float32), grad_gain_local, col_start, 0
    )
    summed = lax.psum(
        (
            grad_norm_in,
            grad_wbc,
            conv_grad_full,
            bias_grad_full,
            dtb_full,
            decay_full,
            skip_full,
            gain_full,
            grad_norm_mid,
            grad_shared_gate,
            grad_shared_up,
            grad_shared_down,
        ),
        ("seq", "exp"),
    )
    return (
        block_output,
        tokens_grad,
        summed[0],
        sum_wz,
        sum_wx,
        summed[1],
        sum_wdt,
        summed[2],
        summed[3],
        summed[4],
        summed[5],
        summed[6],
        summed[7],
        sum_wout,
        summed[8],
        sum_gate_e,
        sum_up_e,
        sum_down_e,
        summed[9],
        summed[10],
        summed[11],
    )


def solution(mesh):
    placed = (
        P("seq", None),
        P(),
        P(("seq", "exp"), None),
        P(("seq", "exp"), None),
        P(("seq", "exp"), None),
        P(),
        P("seq", "exp"),
        P("seq", "exp"),
        P(),
        P("seq", "exp"),
        P(),
        P(),
        P(),
        P(),
        P(),
        P(),
        P("exp", "seq"),
        P(),
        P("exp", "seq", None),
        P("exp", "seq", None),
        P("exp", None, "seq"),
        P(),
        P(),
        P(),
    )
    return jax.shard_map(
        per_device,
        mesh=mesh,
        in_specs=placed,
        out_specs=(
            P(("seq", "exp"), None),
            P(("seq", "exp"), None),
            P(),
            P("seq", "exp"),
            P("seq", "exp"),
            P(),
            P("seq", "exp"),
            P(),
            P(),
            P(),
            P(),
            P(),
            P(),
            P("exp", "seq"),
            P(),
            P("exp", "seq", None),
            P("exp", "seq", None),
            P("exp", None, "seq"),
            P(),
            P(),
            P(),
        ),
        check_vma=False,
    )
```

profile of v0, /device:TPU:0, one launch (start us, length us, event | category | flops | bytes accessed | tf_op | source)
XLA Modules:
  0.0 5812.8 jit_solution(6242888407788059668)
XLA Ops:
  8.9 32.6 all-gather.2
  99.2 21.5 multiply_convert_fusion.4
  138.8 390.3 %while.79 = (s32[]{:T(128)}, f32[12,64,128]{2,1,0:T(8,128)S(1)}, f32[8,256,12,64]{1,0,3,2:T(8,128)}, f32[8,256,12]{1,2,0:T(8,128)}, f32[12]{0:T(128)}, /*index=5...) while((s32[]{:T(128)}, f32[12,64,128]{2,1,0:T(8,128)S(1)}, ...), condition=%wide.region_4.5_spmd.clone, body=%wide.region_1.4_spmd.clone.sunk | while | flops 1313357824 | bytes 9818133 | solution.py:151
  169.4 18.5 dynamic_update_slice.87
  218.2 18.5 dynamic_update_slice.87
  266.9 18.5 dynamic_update_slice.87
  315.7 18.5 dynamic_update_slice.87
  364.4 18.5 dynamic_update_slice.87
  461.9 18.5 dynamic_update_slice.87
  510.6 18.5 dynamic_update_slice.87
  541.3 21.3 all-gather.3
  569.7 23.3 all-gather.30.cloned.1.call-done
  601.4 44.4 all-gather.18.cloned.1.call-done
  658.7 39.9 all-gather.20.cloned.1.call-done
  726.5 34.9 reduce-window.86
  787.2 20.5 reduce-scatter.12.cloned.1.call-done
  815.6 39.1 gather_fusion
  872.5 22.2 mul.1084
  895.0 27.0 scatter_custom_fusion.1
  922.0 145.6 %all-to-all-done = bf16[4,1536,1536]{2,1,0:T(8,128)(2,1)} async-done(((bf16[4,1536,1536]{2,1,0:T(8,128)(2,1)}), bf16[4,1536,1536]{2,1,0:T(8,128)(2,1)}, u32[]{:S(2)}, u32[]{:S(2)}) %all-to-all-start) | async-done | bytes 18874400 | tf_op jit(solution)/shard_map/all_to_all | solution.py:166
  1074.8 214.7 %all-gather.24.cloned.1.call-done = bf16[16,1536,512]{2,1,0:T(8,128)(2,1)} async-done(((bf16[16,192,512]{2,1,0:T(8,128)(2,1)}), bf16[16,1536,512]{2,1,0:T(8,128)(2,1)}) %all-gather.24.cloned.1.call-update) | async-done | bytes 25165840 | tf_op jit(solution)/shard_map/all_gather | solution.py:309
  1289.5 23.9 fusion.100
  1313.5 458.0 %all-gather.22.cloned.1.call-done = bf16[16,1536,512]{2,1,0:T(8,128)(2,1)} async-done(((bf16[16,192,512]{2,1,0:T(8,128)(2,1)}), bf16[16,1536,512]{2,1,0:T(8,128)(2,1)}) %all-gather.22.cloned.1.call-update) | async-done | bytes 25165840 | tf_op jit(solution)/shard_map/all_gather | solution.py:308
  1771.5 24.0 fusion.104
  1795.5 458.0 %all-gather.26.cloned.1.call-done = bf16[16,512,1536]{1,2,0:T(8,128)(2,1)} async-done(((bf16[16,512,192]{1,2,0:T(8,128)(2,1)}), bf16[16,512,1536]{1,2,0:T(8,128)(2,1)}) %all-gather.26.cloned.1.call-update) | async-done | bytes 25165840 | tf_op jit(solution)/shard_map/all_gather | solution.py:310
  2253.5 30.7 fusion.120
  2284.2 27.0 fusion.98
  2311.1 29.2 fusion.110
  2375.5 195.0 %all-to-all-done.3 = bf16[4,1536,1536]{2,1,0:T(8,128)(2,1)} async-done(((bf16[4,1536,1536]{2,1,0:T(8,128)(2,1)}), bf16[4,1536,1536]{2,1,0:T(8,128)(2,1)}, u32[]{:S(2)}, u32[]{:S(2)}) %all-to-all-start.3) | async-done | bytes 18874400 | tf_op jit(solution)/shard_map/all_to_all | solution.py:166
  2570.5 28.5 gather_fusion.2
  2643.4 19.2 all-gather.5
  2687.5 19.5 multiply_reduce_fusion.12
  2713.6 136.4 %while.78 = (s32[]{:T(128)}, f32[12,64,128]{2,1,0:T(8,128)S(1)}, f32[8,12,64,128]{3,2,1,0:T(8,128)}, f32[8,256,12]{1,2,0:T(8,128)}, f32[1,12]{1,0:T(1,128)}, /*i...) while((s32[]{:T(128)}, f32[12,64,128]{2,1,0:T(8,128)S(1)}, ...), condition=%wide.region_26.27_spmd, body=%wide.region_23.26_spmd.sunk | while | flops 302789184 | bytes 2754007 | solution.py:151
  2876.9 829.0 %while.80 = (s32[]{:T(128)}, f32[12]{0:T(128)}, f32[12,64,128]{2,1,0:T(8,128)S(1)}, f32[8,256,12,64]{1,0,3,2:T(8,128)}, f32[8,256,128]{2,1,0:T(8,128)}, /*index=...) while((s32[]{:T(128)}, f32[12]{0:T(128)}, ...), condition=%wide.region_40.41_spmd.clone, body=%wide.region_27.40_spmd.clone.sunk | while | flops 3036491776 | bytes 31978880 | solution.py:151
  2953.0 18.5 dynamic_update_slice.90
  3846.5 28.4 multiply_reduce_fusion.4
  3884.5 22.9 bitcast_convert_fusion.3
  3907.5 22.6 bitcast_convert_fusion.2
  3930.1 25.0 bitcast_convert_fusion.1
  3955.2 22.2 convert_bitcast_fusion
  4032.4 209.0 %all-to-all-done.1 = bf16[4,1536,1536]{2,1,0:T(8,128)(2,1)} async-done(((bf16[4,1536,1536]{2,1,0:T(8,128)(2,1)}), bf16[4,1536,1536]{2,1,0:T(8,128)(2,1)}, u32[]{:S(2)}, u32[]{:S(2)}) %all-to-all-start.1) | async-done | bytes 18874400 | tf_op jit(solution)/shard_map/all_to_all | solution.py:166
  4241.4 28.2 gather_fusion.1
  4284.9 32.0 fusion.196
  4334.9 164.5 %reduce-scatter.22.cloned.1.call-done = bf16[16,192,512]{2,1,0:T(8,128)(2,1)} async-done(((bf16[16,1536,512]{2,1,0:T(8,128)(2,1)}), bf16[16,192,512]{2,1,0:T(8,128)(2,1)}) %reduce-scatter.22.cloned.1.call-update) | async-done | bytes 3145744 | tf_op jit(solution)/shard_map/reduce_scatter | solution.py:446
  4504.8 401.5 %reduce-scatter.24.cloned.1.call-done = bf16[16,192,512]{2,1,0:T(8,128)(2,1)} async-done(((bf16[16,1536,512]{2,1,0:T(8,128)(2,1)}), bf16[16,192,512]{2,1,0:T(8,128)(2,1)}) %reduce-scatter.24.cloned.1.call-update) | async-done | bytes 3145744 | tf_op jit(solution)/shard_map/reduce_scatter | solution.py:449
  4911.8 401.6 %reduce-scatter.26.cloned.1.call-done = bf16[16,512,192]{1,2,0:T(8,128)(2,1)} async-done(((bf16[16,512,1536]{1,2,0:T(8,128)(2,1)}), bf16[16,512,192]{1,2,0:T(8,128)(2,1)}) %reduce-scatter.26.cloned.1.call-update) | async-done | bytes 3145744 | tf_op jit(solution)/shard_map/reduce_scatter | solution.py:452
  5318.9 126.0 %all-reduce.19.cloned.1.call-done = (f32[1536]{0:T(1024)}, f32[4,3328]{1,0:T(4,128)}, f32[3328]{0:T(1024)}, f32[48]{0:T(128)}, f32[48]{0:T(128)}, /*index=5*/f32[48]{0:T(128)}, f32[3072]{0:T(1024)}, f32[1536]{0:T(1024)}) async-done(((f32[1536]{0:T(1024)}, f32[4,3328]{1,0:T(4,128)}, f32[3328]{0:T(1024)}, f32[48]{0:T(128)}, f32[48]{0:T(128)}, /*index=5*/f32[48]{0:T(128)}, f32[3072]{0:T(1024)}, ...) | async-done | bytes 91728 | tf_op jit(solution)/shard_map/psum | solution.py:489
  5444.9 335.5 %all-reduce.21.cloned.1.call-done = (f32[1536,256]{1,0:T(8,128)}, f32[1536,1024]{1,0:T(8,128)}, f32[1536,1024]{1,0:T(8,128)}, f32[1024,1536]{1,0:T(8,128)}) async-done(((f32[1536,256]{1,0:T(8,128)}, f32[1536,1024]{1,0:T(8,128)}, f32[1536,1024]{1,0:T(8,128)}, f32[1024,1536]{1,0:T(8,128)}), (f32[1536,256]{1,0:T(8,128)}, f32[1536,1024]{1,0:T(8,128)}, f32[1536,1024]{1,0:T(8,128)}, ...) | async-done | bytes 20447248 | tf_op jit(solution)/shard_map/psum | solution.py:489
  (1450 shorter events, 1807.4 us)
Async XLA Ops:
  7.2 2364.0 %copy-start = (bf16[1024,1536]{1,0:T(8,128)(2,1)S(1)}, bf16[1024,1536]{1,0:T(8,128)(2,1)}, u32[]{:S(2)}) copy-start(bf16[1024,1536]{1,0:T(8,128)(2,1)} %param.57) | copy-start | bytes 9437188
  7.2 39.6 copy-start.54
  7.2 58.0 all-gather.16.cloned.1.call-start
  8.0 585.0 %all-gather.30.cloned.1.call-start = ((), (), s32[]{:S(2)}) async-start(), calls=%async_computation.28 | async-start | bytes 3538944 | tf_op jit(solution)/shard_map/all_gather | solution.py:25
  58.1 41.1 copy-start.46
  58.1 41.1 copy-start.48
  77.2 12.7 collective-permute-start
  529.9 116.0 %all-gather.18.cloned.1.call-start = ((), (), s32[]{:S(2)}) async-start(), calls=%async_computation.14 | async-start | bytes 2654208 | tf_op jit(solution)/shard_map/all_gather | solution.py:206
  530.6 167.9 %all-gather.20.cloned.1.call-start = ((), (), s32[]{:S(2)}) async-start(), calls=%async_computation.15 | async-start | bytes 2654208 | tf_op jit(solution)/shard_map/all_gather | solution.py:209
  531.2 276.5 %reduce-scatter.12.cloned.1.call-start = ((), (), s32[]{:S(2)}) async-start(), calls=%async_computation.16 | async-start | bytes 15728640 | tf_op jit(solution)/shard_map/reduce_scatter | solution.py:276
  536.2 33.4 copy-start.37
  539.7 53.4 copy-start.93
  540.4 158.1 %copy-start.89 = (f32[768]{0:T(1024)}, f32[768]{0:T(1024)S(1)}, u32[]{:S(2)}) copy-start(f32[768]{0:T(1024)S(1)} %dynamic_slice.168) | copy-start | bytes 9220
  709.6 579.9 %all-gather.24.cloned.1.call-start = ((), (), s32[]{:S(2)}) async-start(), calls=%async_computation.18 | async-start | bytes 28311552 | tf_op jit(solution)/shard_map/all_gather | solution.py:309
  710.2 1061.3 %all-gather.22.cloned.1.call-start = ((), (), s32[]{:S(2)}) async-start(), calls=%async_computation.17 | async-start | bytes 28311552 | tf_op jit(solution)/shard_map/all_gather | solution.py:308
  710.9 1542.6 %all-gather.26.cloned.1.call-start = ((), (), s32[]{:S(2)}) async-start(), calls=%async_computation.19 | async-start | bytes 28311552 | tf_op jit(solution)/shard_map/all_gather | solution.py:310
  711.7 53.8 copy-start.102
  763.7 49.1 copy-start.57
  768.4 126.6 %copy-start.65 = (s32[3072,1]{0,1:T(1,128)}, s32[3072,1]{0,1:T(1,128)S(1)}, u32[]{:S(2)}) copy-start(s32[3072,1]{0,1:T(1,128)S(1)} %compare_select_fusion.2) | copy-start | bytes 36868
  787.1 24.0 copy-start.81
  787.2 26.0 copy-start.83
  811.2 43.5 copy-start.79
  854.7 212.9 %all-to-all-start = ((bf16[4,1536,1536]{2,1,0:T(8,128)(2,1)}), bf16[4,1536,1536]{2,1,0:T(8,128)(2,1)}, u32[]{:S(2)}, u32[]{:S(2)}) async-start(bf16[4,1536,1536]{2,1,0:T(8,128)(2,1)} %bitcast.649), calls=%async_computation.1 | async-start | bytes 37748736 | tf_op jit(solution)/shard_map/all_to_all | solution.py:166
  872.5 22.2 copy-start.62
  1067.5 727.9 %all-to-all-start.2 = ((bf16[4,1536,1536]{2,1,0:T(8,128)(2,1)}), bf16[4,1536,1536]{2,1,0:T(8,128)(2,1)}, u32[]{:S(2)}, u32[]{:S(2)}) async-start(bf16[4,1536,1536]{2,1,0:T(8,128)(2,1)} %bitcast.647), calls=%async_computation.3 | async-start | bytes 37748736 | tf_op jit(solution)/shard_map/all_to_all | solution.py:166
  2357.5 213.0 %all-to-all-start.3 = ((bf16[4,1536,1536]{2,1,0:T(8,128)(2,1)}), bf16[4,1536,1536]{2,1,0:T(8,128)(2,1)}, u32[]{:S(2)}, u32[]{:S(2)}) async-start(bf16[4,1536,1536]{2,1,0:T(8,128)(2,1)} %bitcast.648), calls=%async_computation.4 | async-start | bytes 37748736 | tf_op jit(solution)/shard_map/all_to_all | solution.py:166
  2365.0 322.5 %all-gather.28.cloned.1.call-start = ((), (), s32[]{:S(2)}) async-start(), calls=%async_computation.20 | async-start | bytes 7864320 | tf_op jit(solution)/shard_map/all_gather | solution.py:368
  2365.1 205.4 %copy-start.52 = (s32[3072]{0:T(1024)}, s32[3072]{0:T(1024)S(1)}, u32[]{:S(2)}) copy-start(s32[3072]{0:T(1024)S(1)} %broadcast_clamp_fusion) | copy-start | bytes 36868
  2638.6 24.6 copy-start.100
  2641.8 45.7 copy-start.90
  2641.8 216.7 %all-gather.32.cloned.1.call-start = ((), (), s32[]{:S(2)}) async-start(), calls=%async_computation.29 | async-start | bytes 1769472 | tf_op jit(solution)/shard_map/all_gather | solution.py:41
  2713.6 1609.9 %reduce-scatter.28.cloned.1.call-start = ((), (), s32[]{:S(2)}) async-start(), calls=%async_computation.30 | async-start | bytes 442368
  3713.1 611.9 %reduce-scatter.16.cloned.1.call-start = ((), (), s32[]{:S(2)}) async-start(), calls=%async_computation.22 | async-start | bytes 2654208 | tf_op jit(solution)/shard_map/reduce_scatter | solution.py:434
  3722.4 604.4 %reduce-scatter.20.cloned.1.call-start = ((), (), s32[]{:S(2)}) async-start(), calls=%async_computation.24 | async-start | bytes 2654208 | tf_op jit(solution)/shard_map/reduce_scatter | solution.py:443
  3733.2 595.4 %reduce-scatter.18.cloned.1.call-start = ((), (), s32[]{:S(2)}) async-start(), calls=%async_computation.23 | async-start | bytes 2654208 | tf_op jit(solution)/shard_map/reduce_scatter | solution.py:437
  3796.6 22.8 collective-permute-start.1
  3835.4 495.0 %reduce-scatter.14.cloned.1.call-start = ((), (), s32[]{:S(2)}) async-start(), calls=%async_computation.21 | async-start | bytes 7864320 | tf_op jit(solution)/shard_map/reduce_scatter | solution.py:430
  3835.4 39.5 slice-start.3
  3846.5 28.4 slice-start.4
  3884.5 614.9 %reduce-scatter.22.cloned.1.call-start = ((), (), s32[]{:S(2)}) async-start(), calls=%async_computation.25 | async-start | bytes 28311552 | tf_op jit(solution)/shard_map/reduce_scatter | solution.py:446
  3907.4 998.9 %reduce-scatter.24.cloned.1.call-start = ((), (), s32[]{:S(2)}) async-start(), calls=%async_computation.26 | async-start | bytes 28311552 | tf_op jit(solution)/shard_map/reduce_scatter | solution.py:449
  3930.1 1383.3 %reduce-scatter.26.cloned.1.call-start = ((), (), s32[]{:S(2)}) async-start(), calls=%async_computation.27 | async-start | bytes 28311552 | tf_op jit(solution)/shard_map/reduce_scatter | solution.py:452
  3994.7 246.7 %all-to-all-start.1 = ((bf16[4,1536,1536]{2,1,0:T(8,128)(2,1)}), bf16[4,1536,1536]{2,1,0:T(8,128)(2,1)}, u32[]{:S(2)}, u32[]{:S(2)}) async-start(bf16[4,1536,1536]{2,1,0:T(8,128)(2,1)} %bitcast.646), calls=%async_computation.2 | async-start | bytes 37748736 | tf_op jit(solution)/shard_map/all_to_all | solution.py:166
  4002.2 1442.7 %all-reduce.19.cloned.1.call-start = ((), (), s32[]{:S(2)}) async-start(), calls=%async_computation.31 | async-start | bytes 199680 | tf_op jit(solution)/shard_map/psum | solution.py:489
  4020.8 1759.6 %all-reduce.21.cloned.1.call-start = ((), (), s32[]{:S(2)}) async-start(), calls=%async_computation.32 | async-start | bytes 40894464 | tf_op jit(solution)/shard_map/psum | solution.py:489
  4031.6 209.8 %copy-start.53 = (s32[3072]{0:T(1024)S(1)}, s32[3072]{0:T(1024)}, u32[]{:S(2)}) copy-start(s32[3072]{0:T(1024)} %copy-done.52) | copy-start | bytes 36868
  4284.9 32.0 copy-start.12
  4284.9 32.0 copy-start.104
  (178 other events, 1283.1 us)
Sparse Core Ops, SparseCore 0:
  10.2 54.8 all-gather.15
  530.0 62.9 all-gather.29
  595.2 50.6 all-gather.17
  647.9 50.6 all-gather.19
  709.7 97.9 reduce-scatter.11
  809.1 480.3 all-gather.23
  1291.1 480.3 all-gather.21
  1773.0 480.3 all-gather.25
  2641.9 45.4 all-gather.27
  2713.7 44.1 all-gather.31
  3713.2 57.4 reduce-scatter.27
  3774.7 75.5 reduce-scatter.15
  3853.8 68.0 reduce-scatter.19
  3925.8 68.0 reduce-scatter.17
  3996.9 94.6 reduce-scatter.13
  4095.8 403.5 reduce-scatter.21
  4503.6 402.6 reduce-scatter.23
  4910.6 402.7 reduce-scatter.25
  5322.1 122.7 all-reduce.18
  5454.4 325.9 all-reduce.20
where the time goes:
time: 5850 us; the launch traced here: 5810 us
  waiting for transfers between devices  3260 us (56%)
  local copies, waits for them, and re-layouts  1020 us (17%)
  matrix products  782 us (13%)
  other arithmetic  578 us (10%)
  blocking collectives  85.2 us (1%)
    all_to_all x4, waiting for transfers between devices, exp_move(): return lax.all_to_all(rows, 'exp', split_axis=0, concat_axis=0, tiled=True)  550 us
    psum x2, waiting for transfers between devices, per_device(): lax.psum((grad_norm_in, grad_wbc, conv_grad_full, bias_grad_full, dtb_ful...  462 us
    all_gather x1, waiting for transfers between devices, per_device(): lax.all_gather(expert_gate, 'seq', axis=1, tiled=True)  458 us
    all_gather x1, waiting for transfers between devices, per_device(): lax.all_gather(expert_down, 'seq', axis=2, tiled=True)  458 us
    reduce_scatter x1, waiting for transfers between devices, per_device(): lax.psum_scatter(grad_down_e.astype(jnp.bfloat16), 'seq', scatter_dimensi...  402 us
    reduce_scatter x1, waiting for transfers between devices, per_device(): lax.psum_scatter(grad_up_e.astype(jnp.bfloat16), 'seq', scatter_dimension...  402 us
    dynamic_update_slice x56, local copies, waits for them, and re-layouts, ssd_spans(): lax.scan(jax.checkpoint(partial(span_step, decay_rates)), carry_state, sp...  348 us
    all_gather x1, waiting for transfers between devices, per_device(): lax.all_gather(expert_up, 'seq', axis=1, tiled=True)  215 us
  transfers between devices with their start and end apart: 26, of which 18 were waited for; matrix products, arithmetic and copies ran while one was open for 15% of the time, Pallas kernels for 0%

commit v1 on v0

v1 whole, which is shorter than its diff:
```python
from functools import partial

import jax
import jax.numpy as jnp
from jax import lax
from jax.experimental import pallas as pl
from jax.experimental.pallas import tpu as pltpu
from jax.sharding import PartitionSpec as P

CONV = 4
SPAN = 256
LANES = 128
EPS = 1e-05
FLOOR = -1e30
HIGH = lax.Precision.HIGHEST
VMEM_BYTES = 56 * 1024 * 1024
F32 = jnp.float32
BF16 = jnp.bfloat16


def low_dot(left, right):
    return jnp.dot(left, right, preferred_element_type=F32)


def dot_nt(left, right):
    return lax.dot_general(left, right, (((1,), (1,)), ((), ())), preferred_element_type=F32)


def dot_tn(left, right):
    return lax.dot_general(left, right, (((0,), (0,)), ((), ())), preferred_element_type=F32)


def split_dot(values, table):
    high = values.astype(BF16)
    rest = (values - high.astype(F32)).astype(BF16)
    return low_dot(high, table) + low_dot(rest, table)


def exact_sum(triangle, values):
    high = values.astype(BF16)
    rest = values - high.astype(F32)
    middle = rest.astype(BF16)
    small = (rest - middle.astype(F32)).astype(BF16)
    return low_dot(triangle, high) + low_dot(triangle, middle) + low_dot(triangle, small)


def silu_slope(values):
    sigmoid_v = jax.nn.sigmoid(values)
    return sigmoid_v * (1.0 + values * (1.0 - sigmoid_v))


def rms_scale(values):
    return lax.rsqrt(jnp.mean(values * values, axis=-1, keepdims=True) + EPS)


def norm_back(grad_normed, gain, normed, scale):
    weighted = grad_normed * gain[None, :]
    return scale * (weighted - normed * jnp.mean(weighted * normed, axis=-1, keepdims=True))


def compiler_params(steps=1):
    return pltpu.CompilerParams(
        dimension_semantics=("arbitrary",) * steps, vmem_limit_bytes=VMEM_BYTES
    )


def cost(flops, moved, exps=0):
    return pl.CostEstimate(flops=int(flops), bytes_accessed=int(moved), transcendentals=int(exps))


def causal(span):
    rows = lax.broadcasted_iota(jnp.int32, (span, span), 0)
    cols = lax.broadcasted_iota(jnp.int32, (span, span), 1)
    return rows >= cols


def span_terms(steps, marks, seg_row, rates, b_low, c_low):
    span = steps.shape[0]
    keep = causal(span)
    cum = exact_sum(keep.astype(F32).astype(BF16), steps * rates)
    cum_rows = cum.T
    same = marks[:, 6:7] == seg_row
    bias = jnp.where(keep & same, 0.0, FLOOR)
    scores = dot_nt(c_low, b_low)
    last = cum[span - 1 : span, :]
    entry = jnp.exp(cum) * marks[:, 4:5]
    tail = jnp.exp(last - cum) * marks[:, 5:6]
    return cum, cum_rows, bias, scores, last, entry, tail


def scan_forward(
    raw_x,
    raw_s,
    halo,
    marks,
    seg_row,
    taps,
    steps,
    heads,
    spread,
    conv_out,
    x_out,
    bc_out,
    y_out,
    reach_out,
    entries_out,
    last_out,
    ext,
    state,
    total,
):
    turn = pl.program_id(0)
    span, width = raw_x.shape
    channels = taps.shape[1]

    @pl.when(turn == 0)
    def _():
        ext[0:8, :] = halo[...]
        state[...] = jnp.zeros_like(state)
        total[...] = jnp.zeros_like(total)

    @pl.when(turn > 0)
    def _():
        ext[0:8, :] = ext[span : span + 8, :]

    ext[8 : 8 + span, 0:width] = raw_x[...]
    ext[8 : 8 + span, width:channels] = raw_s[:, 0 : channels - width]
    mark = marks[...]
    for start in range(0, channels, LANES):
        cols = slice(start, start + LANES)
        conv = taps[4:5, cols] + taps[3:4, cols] * ext[8 : 8 + span, cols]
        for tap in range(CONV - 1):
            conv = conv + taps[tap : tap + 1, cols] * (
                ext[5 + tap : 5 + tap + span, cols] * mark[:, tap : tap + 1]
            )
        conv_out[:, cols] = conv
        act = (conv * jax.nn.sigmoid(conv)).astype(BF16)
        if start < width:
            x_out[:, cols] = act
        else:
            bc_out[:, start - width : start - width + LANES] = act
    half = (channels - width) // 2
    b_low = bc_out[:, 0:half]
    c_low = bc_out[:, half:]
    step = steps[...]
    rates = heads[1:2, :]
    cum, cum_rows, bias, scores, last, entry, tail = span_terms(
        step, mark, seg_row[0], rates, b_low, c_low
    )
    reach_out[...] = jnp.exp(cum + total[0:1, :]) * mark[:, 3:4]
    total[0:1, :] = total[0:1, :] + last
    table = spread[...]
    entry_wide = split_dot(entry, table)
    xf = x_out[...].astype(F32)
    fed = (xf * split_dot(step, table)).astype(BF16)
    kept = (xf * split_dot(tail * step, table)).astype(BF16)
    entries_out[0] = state[...]
    state_low = state[...].astype(BF16)
    y_out[...] = entry_wide * low_dot(c_low, state_low)
    left_half = lax.broadcasted_iota(jnp.int32, (span, LANES), 1) < LANES // 2
    for pair in range(width // LANES):
        cols = slice(pair * LANES, (pair + 1) * LANES)
        both = []
        for head in (2 * pair, 2 * pair + 1):
            decay = jnp.exp(cum[:, head : head + 1] - cum_rows[head : head + 1, :] + bias)
            both.append(low_dot((decay * scores).astype(BF16), fed[:, cols]))
        y_out[:, cols] = y_out[:, cols] + jnp.where(left_half, both[0], both[1])
    state[...] = state[...] * entry_wide[span - 1 : span, :] + dot_tn(b_low, kept)

    @pl.when(turn == pl.num_programs(0) - 1)
    def _():
        last_out[...] = state[...]


def gate_forward(
    y_local,
    reach,
    bc,
    state_in,
    x,
    gate,
    rows,
    spread,
    weight,
    full_out,
    low_out,
    mixer_out,
    square_out,
):
    half = bc.shape[1] // 2
    c_low = bc[:, half:]
    far = split_dot(reach[...], spread[...]) * low_dot(c_low, state_in[...].astype(BF16))
    full = y_local[...] + far + rows[0:1, :] * x[...].astype(F32)
    full_out[...] = full
    z = gate[...]
    gated = full * (z * jax.nn.sigmoid(z))
    square_out[...] = jnp.sum(gated * gated, axis=1, keepdims=True)
    low = (gated * rows[1:2, :]).astype(BF16)
    low_out[...] = low
    mixer_out[...] = dot_nt(low, weight[...]).astype(BF16)


def gate_backward(
    part_grad,
    square_grad,
    full_y,
    gate,
    x,
    reach,
    bc,
    rows,
    spread,
    weight,
    grad_y_out,
    grad_z_out,
    sums_out,
    direct_out,
):
    turn = pl.program_id(0)
    z = gate[...]
    sig = jax.nn.sigmoid(z)
    act = z * sig
    full = full_y[...]
    gated = full * act
    scaled_grad = low_dot(part_grad[...], weight[...])
    gated_grad = scaled_grad * rows[1:2, :] + 2.0 * gated * square_grad[...]
    grad_full = gated_grad * act
    grad_y_out[...] = grad_full.astype(BF16)
    grad_z_out[...] = (gated_grad * full * (sig * (1.0 + z * (1.0 - sig)))).astype(BF16)
    half = bc.shape[1] // 2
    seen = (grad_full * split_dot(reach[...], spread[...])).astype(BF16)
    direct = dot_tn(bc[:, half:], seen)
    gain_sum = jnp.sum(scaled_grad * gated, axis=0, keepdims=True)
    skip_sum = jnp.sum(grad_full * x[...].astype(F32), axis=0, keepdims=True)

    @pl.when(turn == 0)
    def _():
        sums_out[...] = jnp.zeros_like(sums_out)
        direct_out[...] = jnp.zeros_like(direct_out)

    sums_out[0:1, :] = sums_out[0:1, :] + gain_sum
    sums_out[1:2, :] = sums_out[1:2, :] + skip_sum
    direct_out[...] = direct_out[...] + direct


def scan_backward(
    conv,
    raw_x,
    raw_s,
    raw_x_before,
    raw_s_before,
    halo,
    marks,
    seg_row,
    taps,
    steps,
    heads,
    spread,
    fold,
    x,
    bc,
    full_y,
    grad_y,
    entries,
    passed,
    state_in,
    state_grad,
    rows,
    grad_x_out,
    grad_bc_out,
    grad_step_out,
    tail_out,
    head_out,
    sums_out,
    rates_out,
    ext,
    later0,
    later1,
    later2,
    back,
    turned,
):
    turn = pl.program_id(0)
    span, width = raw_x.shape
    channels = taps.shape[1]
    half = (channels - width) // 2
    later = (later0, later1, later2)

    @pl.when(turn == 0)
    def _():
        back[...] = state_grad[...]
        sums_out[...] = jnp.zeros_like(sums_out)
        rates_out[...] = jnp.zeros_like(rates_out)
        for kept in later:
            kept[span : span + 8, :] = jnp.zeros((8, channels), F32)

    @pl.when(turn > 0)
    def _():
        for kept in later:
            kept[span : span + 8, :] = kept[0:8, :]

    @pl.when(turn == pl.num_programs(0) - 1)
    def _():
        ext[0:8, :] = halo[...]

    @pl.when(turn < pl.num_programs(0) - 1)
    def _():
        ext[0:8, 0:width] = raw_x_before[...]
        ext[0:8, width:channels] = raw_s_before[:, 0 : channels - width]

    ext[8 : 8 + span, 0:width] = raw_x[...]
    ext[8 : 8 + span, width:channels] = raw_s[:, 0 : channels - width]
    mark = marks[...]
    step = steps[...]
    rates = heads[1:2, :]
    b_low = bc[:, 0:half]
    c_low = bc[:, half:]
    cum, cum_rows, bias, scores, last, entry, tail = span_terms(
        step, mark, seg_row[0], rates, b_low, c_low
    )
    table = spread[...]
    entry_wide = split_dot(entry, table)
    tail_wide = split_dot(tail, table)
    step_wide = split_dot(step, table)
    xf = x[...].astype(F32)
    fed_low = (xf * step_wide).astype(BF16)
    fed = fed_low.astype(F32)
    dy_low = grad_y[...]
    dy = dy_low.astype(F32)
    seen = (dy * entry_wide).astype(BF16)
    entered = entries[0] + split_dot(passed[0], table)[0:1, :] * state_in[...]
    entered_low = entered.astype(BF16)
    back_low = back[...].astype(BF16)
    turned_dy = dy.T.astype(BF16)
    left_half = lax.broadcasted_iota(jnp.int32, (span, LANES), 1) < LANES // 2
    score_grad = jnp.zeros((span, span), F32)
    head_rows = LANES // 2
    for pair in range(width // LANES):
        cols = slice(pair * LANES, (pair + 1) * LANES)
        fed_pair = fed_low[:, cols]
        dy_pair = dy[:, cols]
        for side in (0, 1):
            head = 2 * pair + side
            decay = jnp.exp(cum[:, head : head + 1] - cum_rows[head : head + 1, :] + bias)
            weights = (decay * scores).astype(BF16)
            own = jnp.where(left_half if side == 0 else ~left_half, dy_pair, 0.0).astype(BF16)
            score_grad = score_grad + dot_nt(own, fed_pair) * decay
            lanes = slice(head * head_rows, (head + 1) * head_rows)
            turned[lanes, :] = low_dot(turned_dy[lanes, :], weights)
    score_low = score_grad.astype(BF16)
    inner = turned[...].T
    far = tail_wide * low_dot(b_low, back_low)
    fed_grad = inner + far
    skip = rows[0:1, :]
    scan_y = full_y[...] - skip * xf
    summed = fold[...]
    far_sums = split_dot(fed * far, summed)
    kept_row = jnp.sum(back[...] * entered, axis=0, keepdims=True) * entry_wide[span - 1 : span, :]
    kept_sum = split_dot(jnp.broadcast_to(kept_row, (8, width)), summed)[0:1, :]
    log_grad = split_dot(dy * scan_y - fed * fed_grad, summed)
    ends = jnp.sum(far_sums, axis=0, keepdims=True) + kept_sum
    rows_i = lax.broadcasted_iota(jnp.int32, (span, span), 0)
    cols_i = lax.broadcasted_iota(jnp.int32, (span, span), 1)
    upper = (cols_i >= rows_i).astype(F32).astype(BF16)
    rate_step_grad = exact_sum(upper, log_grad) + ends
    grad_step_out[...] = split_dot(fed_grad * xf, summed) + rates * rate_step_grad
    rates_out[0:1, :] = rates_out[0:1, :] + jnp.sum(rate_step_grad * step, axis=0, keepdims=True)
    c_grad = dot_nt(seen, entered_low) + low_dot(score_low, b_low)
    b_grad = dot_nt((fed * tail_wide).astype(BF16), back_low) + dot_tn(score_low, c_low)
    back[...] = back[...] * entry_wide[span - 1 : span, :] + dot_tn(c_low, seen)
    x_grad = fed_grad * step_wide + skip * dy
    for start in range(0, channels, LANES):
        cols = slice(start, start + LANES)
        if start < width:
            active = x_grad[:, cols]
        elif start < width + half:
            active = b_grad
        else:
            active = c_grad
        grad = active * silu_slope(conv[:, cols])

        @pl.when(turn == pl.num_programs(0) - 1)
        def _():
            head_out[:, cols] = grad[0:8, :]

        source = taps[3:4, cols] * grad
        sums_out[4:5, cols] = sums_out[4:5, cols] + jnp.sum(grad, axis=0, keepdims=True)
        sums_out[3:4, cols] = sums_out[3:4, cols] + jnp.sum(
            grad * ext[8 : 8 + span, cols], axis=0, keepdims=True
        )
        for tap in range(CONV - 1):
            masked = grad * mark[:, tap : tap + 1]
            later[tap][0:span, cols] = masked
            sums_out[tap : tap + 1, cols] = sums_out[tap : tap + 1, cols] + jnp.sum(
                masked * ext[5 + tap : 5 + tap + span, cols], axis=0, keepdims=True
            )
            shift = CONV - 1 - tap
            source = source + taps[tap : tap + 1, cols] * later[tap][shift : shift + span, cols]
        if start < width:
            grad_x_out[:, cols] = source.astype(BF16)
        else:
            grad_bc_out[:, start - width : start - width + LANES] = source.astype(BF16)

        @pl.when(turn == 0)
        def _():
            tail_out[:, cols] = source[span - 8 : span, :]


def dispatch_kernel(weighted, *refs):
    if weighted:
        rows, places, gates, out = refs
    else:
        rows, places, out = refs
    experts, _, slots, _ = out.shape
    count = rows.shape[0]
    slot = lax.broadcasted_iota(jnp.int32, (slots, count), 0)
    hits = [slot == places[0, e : e + 1, :] for e in range(experts)]
    chosen = jnp.concatenate([hit.astype(F32).astype(BF16) for hit in hits], axis=0)
    taken = low_dot(chosen, rows[...])
    for e in range(experts):
        part = taken[e * slots : (e + 1) * slots, :]
        if weighted:
            part = part * jnp.sum(
                jnp.where(hits[e], gates[0, e : e + 1, :], 0.0), axis=1, keepdims=True
            )
        out[e, 0] = part.astype(BF16)


def dispatch(rows, places, slots, gates=None):
    blocks, experts, count = places.shape
    width = rows.shape[1]
    arrays = (rows, places) if gates is None else (rows, places, gates)
    small = pl.BlockSpec((1, experts, count), lambda b: (b, 0, 0))
    return pl.pallas_call(
        partial(dispatch_kernel, gates is not None),
        grid=(blocks,),
        in_specs=[pl.BlockSpec((count, width), lambda b: (b, 0))] + [small] * (len(arrays) - 1),
        out_specs=pl.BlockSpec((experts, 1, slots, width), lambda b: (0, b, 0, 0)),
        out_shape=jax.ShapeDtypeStruct((experts, blocks, slots, width), BF16),
        compiler_params=compiler_params(),
        cost_estimate=cost(
            2 * blocks * experts * slots * count * width,
            2 * rows.size + 2 * experts * blocks * slots * width,
        ),
        name="dispatch",
    )(*arrays)


def expert_kernel(pieces, me, got, grad_got, *refs):
    weights = refs[: 3 * pieces]
    hid_out, a_out, b_out, res_out, row_out, gate, up, down = refs[3 * pieces :]
    part = weights[0].shape[1]
    for kind, full in enumerate((gate, up, down)):
        for piece in range(pieces):
            start = pl.multiple_of((me[0] ^ piece) * part, part)
            full[pl.ds(start, part), :] = weights[kind * pieces + piece][0]
    blocks, slots, width = got.shape[1:]
    step = max(1, min(blocks, 384 // slots))
    for first in range(0, blocks, step):
        rows = slice(first * slots, (first + step) * slots)
        taken = got[0, first : first + step].reshape(step * slots, width)
        taken_grad = grad_got[0, first : first + step].reshape(step * slots, width)
        a = low_dot(taken, gate[...])
        b = low_dot(taken, up[...])
        hid_grad = low_dot(taken_grad, down[...])
        sig = jax.nn.sigmoid(a)
        act = a * sig
        hid = (act * b).astype(BF16)
        a_grad = (hid_grad * b * (sig * (1.0 + a * (1.0 - sig)))).astype(BF16)
        b_grad = (hid_grad * act).astype(BF16)
        hid_out[0, rows, :] = hid
        a_out[0, rows, :] = a_grad
        b_out[0, rows, :] = b_grad
        res = dot_nt(hid, down[...]).astype(BF16)
        row = (dot_nt(a_grad, gate[...]) + dot_nt(b_grad, up[...])).astype(BF16)
        res_out[0, first : first + step] = res.reshape(step, slots, width)
        row_out[0, first : first + step] = row.reshape(step, slots, width)


def run_experts(me, got, grad_got, gate, up, down):
    experts, blocks, slots, width = got.shape
    pieces = len(gate)
    part, hidden = gate[0].shape[1:]
    total = blocks * slots
    wide = pl.BlockSpec((1, blocks, slots, width), lambda e, me: (e, 0, 0, 0))
    narrow = pl.BlockSpec((1, total, hidden), lambda e, me: (e, 0, 0))
    piece = pl.BlockSpec((1, part, hidden), lambda e, me: (e, 0, 0))
    hid_shape = jax.ShapeDtypeStruct((experts, total, hidden), BF16)
    row_shape = jax.ShapeDtypeStruct(got.shape, BF16)
    return pl.pallas_call(
        partial(expert_kernel, pieces),
        grid_spec=pltpu.PrefetchScalarGridSpec(
            num_scalar_prefetch=1,
            grid=(experts,),
            in_specs=[wide, wide] + [piece] * (3 * pieces),
            out_specs=[narrow] * 3 + [wide] * 2,
            scratch_shapes=[pltpu.VMEM((width, hidden), BF16)] * 3,
        ),
        out_shape=[hid_shape] * 3 + [row_shape] * 2,
        compiler_params=compiler_params(),
        cost_estimate=cost(
            12 * experts * total * width * hidden,
            8 * got.size + 6 * experts * width * hidden,
            experts * total * hidden,
        ),
        name="experts",
    )(me, got, grad_got, *gate, *up, *down)


def expert_grad_kernel(pieces, me, got, grad_got, hid, a_grad, b_grad, *refs):
    outs, (gate, up, down) = refs[: 3 * pieces], refs[3 * pieces :]
    blocks, slots, width = got.shape[1:]
    part = outs[0].shape[1]
    total = blocks * slots
    step = 256
    for start in range(0, width, step):
        cols = slice(start, start + step)
        taken = got[0, :, :, cols].reshape(total, step)
        taken_grad = grad_got[0, :, :, cols].reshape(total, step)
        gate[cols, :] = dot_tn(taken, a_grad[0]).astype(BF16)
        up[cols, :] = dot_tn(taken, b_grad[0]).astype(BF16)
        down[cols, :] = dot_tn(taken_grad, hid[0]).astype(BF16)
    for kind, full in enumerate((gate, up, down)):
        for piece in range(pieces):
            start = pl.multiple_of((me[0] ^ piece) * part, part)
            outs[kind * pieces + piece][0] = full[pl.ds(start, part), :]


def expert_grads(me, got, grad_got, hid, a_grad, b_grad, pieces):
    experts, blocks, slots, width = got.shape
    total, hidden = hid.shape[1:]
    part = width // pieces
    wide = pl.BlockSpec((1, blocks, slots, width), lambda e, me: (e, 0, 0, 0))
    narrow = pl.BlockSpec((1, total, hidden), lambda e, me: (e, 0, 0))
    piece = pl.BlockSpec((1, part, hidden), lambda e, me: (e, 0, 0))
    outs = pl.pallas_call(
        partial(expert_grad_kernel, pieces),
        grid_spec=pltpu.PrefetchScalarGridSpec(
            num_scalar_prefetch=1,
            grid=(experts,),
            in_specs=[wide] * 2 + [narrow] * 3,
            out_specs=[piece] * (3 * pieces),
            scratch_shapes=[pltpu.VMEM((width, hidden), BF16)] * 3,
        ),
        out_shape=[jax.ShapeDtypeStruct((experts, part, hidden), BF16)] * (3 * pieces),
        compiler_params=compiler_params(),
        cost_estimate=cost(
            6 * experts * total * width * hidden, 4 * got.size + 6 * experts * width * hidden
        ),
        name="expert_grads",
    )(me, got, grad_got, hid, a_grad, b_grad)
    return [outs[kind * pieces : (kind + 1) * pieces] for kind in range(3)]


def combine_kernel(weighted, turned, *refs):
    if weighted:
        rows, places, table, number, gates, hidden, weight, out = refs
    else:
        rows, places, table, number, hidden, weight, out = refs
    experts, _, slots, width = rows.shape
    wide = low_dot(places[0], table[...])
    factor = low_dot(gates[0], table[...]) if weighted else 1.0
    chosen = jnp.where(wide == number[...], factor, 0.0).astype(BF16)
    total = low_dot(chosen, rows[:, 0].reshape(experts * slots, width))
    dense = dot_nt if turned else low_dot
    out[...] = (total + dense(hidden[...], weight[...])).astype(BF16)


def combine(rows, places, hidden, weight, turned, gates=None):
    experts, blocks, slots, width = rows.shape
    count = places.shape[1]
    expert_of = jnp.arange(experts * slots, dtype=jnp.int32) // slots
    table = (jnp.arange(experts, dtype=jnp.int32)[:, None] == expert_of[None, :]).astype(BF16)
    number = (jnp.arange(experts * slots, dtype=jnp.int32) % slots).astype(F32)[None, :]
    small = pl.BlockSpec((1, count, experts), lambda b: (b, 0, 0))
    arrays = [rows, places, table, number]
    specs = [
        pl.BlockSpec((experts, 1, slots, width), lambda b: (0, b, 0, 0)),
        small,
        pl.BlockSpec(table.shape, lambda b: (0, 0)),
        pl.BlockSpec(number.shape, lambda b: (0, 0)),
    ]
    if gates is not None:
        arrays.append(gates)
        specs.append(small)
    arrays += [hidden, weight]
    specs += [
        pl.BlockSpec((count, hidden.shape[1]), lambda b: (b, 0)),
        pl.BlockSpec(weight.shape, lambda b: (0, 0)),
    ]
    return pl.pallas_call(
        partial(combine_kernel, gates is not None, turned),
        grid=(blocks,),
        in_specs=specs,
        out_specs=pl.BlockSpec((count, width), lambda b: (b, 0)),
        out_shape=jax.ShapeDtypeStruct((blocks * count, width), BF16),
        compiler_params=compiler_params(),
        cost_estimate=cost(
            2 * blocks * count * width * (experts * slots + hidden.shape[1]),
            2 * rows.size + 2 * blocks * count * width,
        ),
        name="combine",
    )(*arrays)


def swap(block, axis, stride):
    return lax.ppermute(
        block, axis, [(i, i ^ stride) for i in range(lax.axis_size(axis))]
    )


def bits(count):
    return [1 << i for i in range(count.bit_length() - 1)]


def bit_of(axis, stride):
    return (lax.axis_index(axis) // stride) % 2


def gather_rows(block, axis, strides):
    for stride in strides:
        other = swap(block, axis, stride)
        mine = jnp.concatenate([block, other], axis=0)
        theirs = jnp.concatenate([other, block], axis=0)
        block = jnp.where(bit_of(axis, stride) == 0, mine, theirs)
    return block


def scatter_rows(block, axis, strides):
    for stride in reversed(strides):
        half = block.shape[0] // 2
        place = bit_of(axis, stride)
        kept = lax.dynamic_slice_in_dim(block, place * half, half, 0)
        sent = lax.dynamic_slice_in_dim(block, (1 - place) * half, half, 0)
        block = (kept.astype(F32) + swap(sent, axis, stride).astype(F32)).astype(block.dtype)
    return block


def gather_group(block, steps):
    cols = block.shape[1] // 2
    halves = []
    for part, order in ((block[:, :cols], (0, 1)), (block[:, cols:], (1, 0))):
        known = {0: part}
        numbers = list(order) + list(range(2, len(steps)))
        for number in numbers:
            axis, stride = steps[number]
            got = {place | 1 << number: swap(v, axis, stride) for place, v in known.items()}
            known.update(got)
        halves.append(jnp.concatenate([known[place] for place in range(len(known))], axis=0))
    return jnp.concatenate(halves, axis=1)


def scatter_group(block, steps):
    count = 1 << len(steps)
    rows, width = block.shape[0] // count, block.shape[1]
    cols = width // 2
    halves = []
    for start, order in ((0, (0, 1)), (cols, (1, 0))):
        known = {
            place: lax.slice(block, (place * rows, start), ((place + 1) * rows, start + cols))
            for place in range(count)
        }
        for number in list(reversed(range(2, len(steps)))) + list(reversed(order)):
            axis, stride = steps[number]
            flag = 1 << number
            known = {
                place: (
                    v.astype(F32) + swap(known[place | flag], axis, stride).astype(F32)
                ).astype(BF16 if len(known) > 2 else F32)
                for place, v in known.items()
                if not place & flag
            }
        halves.append(known[0])
    return jnp.concatenate(halves, axis=1)


def spread_weights(shard, low_z, other_strides):
    half = shard.shape[0] // 2
    place = bit_of("seq", low_z)
    kept = lax.dynamic_slice_in_dim(shard, place * half, half, 0)
    sent = lax.dynamic_slice_in_dim(shard, (1 - place) * half, half, 0)
    known = {0: kept, low_z: swap(sent, "seq", low_z)}
    for stride in other_strides:
        known.update({at | stride: swap(v, "seq", stride) for at, v in known.items()})
    return [known[at] for at in range(len(known))]


def collect_weights(pieces, low_z, other_strides):
    known = dict(enumerate(pieces))
    for stride in reversed(other_strides):
        known = {
            at: (v.astype(F32) + swap(known[at | stride], "seq", stride).astype(F32)).astype(BF16)
            for at, v in known.items()
            if not at & stride
        }
    mine, other = known[0], swap(known[low_z], "seq", low_z)
    first = bit_of("seq", low_z) == 0
    return jnp.concatenate(
        [jnp.where(first, mine, other), jnp.where(first, other, mine)], axis=0
    ).astype(F32)


def gather_exp(block, strides):
    known = {0: block}
    for stride in strides:
        known.update({at | stride: swap(v, "exp", stride) for at, v in known.items()})
    for stride in strides:
        flipped = bit_of("exp", stride) == 1
        known = {at: jnp.where(flipped, known[at ^ stride], v) for at, v in known.items()}
    return jnp.concatenate([known[at] for at in range(len(known))], axis=0)


def scatter_exp(blocks, strides):
    place = lax.axis_index("exp")
    known = {
        at: lax.dynamic_index_in_dim(blocks, place ^ at, 0, False) for at in range(blocks.shape[0])
    }
    for stride in reversed(strides):
        known = {
            at: (v.astype(F32) + swap(known[at | stride], "exp", stride).astype(F32)).astype(
                F32 if len(known) == 2 else v.dtype
            )
            for at, v in known.items()
            if not at & stride
        }
    return known[0]


def earlier_states(through, state, strides):
    before = jnp.zeros_like(state)
    whole, decay = state, through
    reach = jnp.ones_like(through)
    for stride in strides:
        other = swap(whole.astype(BF16), "seq", stride).astype(F32)
        other_decay = swap(decay, "seq", stride)
        high = bit_of("seq", stride) == 1
        before = jnp.where(high, before + reach * other, before)
        reach = jnp.where(high, reach * other_decay, reach)
        whole = jnp.where(high, whole + decay * other, other + other_decay * whole)
        decay = decay * other_decay
    return before


def later_grads(through, direct, strides):
    after = jnp.zeros_like(direct)
    whole, decay = direct, through
    reach = jnp.ones_like(through)
    for stride in strides:
        other = swap(whole.astype(BF16), "seq", stride).astype(F32)
        other_decay = swap(decay, "seq", stride)
        low = bit_of("seq", stride) == 0
        after = jnp.where(low, after + reach * other, after)
        reach = jnp.where(low, reach * other_decay, reach)
        whole = jnp.where(low, whole + decay * other, other + other_decay * whole)
        decay = decay * other_decay
    return after


def per_device(
    tokens,
    segment_ids,
    routes,
    gate_weights,
    cotangent,
    norm_in,
    proj_z,
    proj_x,
    proj_bc,
    proj_dt,
    conv_weight,
    conv_bias,
    dt_bias,
    decay_log,
    skip_gain,
    gated_gain,
    proj_out,
    norm_mid,
    expert_gate,
    expert_up,
    expert_down,
    shared_gate,
    shared_up,
    shared_down,
):
    seq_pos = lax.axis_index("seq")
    exp_pos = lax.axis_index("exp")
    exp_count = lax.axis_size("exp")
    seq_count = lax.axis_size("seq")
    length, model_width = tokens.shape
    rows_here, top_count = routes.shape
    inner_width = gated_gain.shape[0]
    head_total = dt_bias.shape[0]
    pair_width = proj_bc.shape[1]
    state_dim = pair_width // 2
    local_width = proj_x.shape[1]
    head_count = proj_dt.shape[1]
    channels = local_width + pair_width
    col_start = exp_pos * local_width
    head_start = exp_pos * head_count
    low_z = seq_count // 4
    seq_strides = bits(seq_count)
    weight_strides = [2 * low_z] + bits(low_z)
    exp_strides = list(reversed(bits(exp_count)))
    steps_group = [("seq", low_z)] + [("exp", stride) for stride in exp_strides]
    span_count = length // SPAN

    pad_dt = jnp.pad(proj_dt, ((0, 0), (0, LANES - head_count)))
    weight_xdt = lax.all_gather(
        jnp.concatenate([proj_x, pad_dt], axis=1), "seq", axis=0, tiled=True
    )
    weight_z = lax.all_gather(proj_z, "seq", axis=0, tiled=True)
    weight_out = lax.all_gather(proj_out.T, "seq", axis=0, tiled=True)
    weight_x, weight_dt = weight_xdt[:, :local_width], weight_xdt[:, local_width:]

    half_experts = expert_gate.shape[0] // 2
    down_pieces = spread_weights(expert_down.transpose(0, 2, 1), low_z, weight_strides)
    gate_pieces = spread_weights(expert_gate, low_z, weight_strides)
    up_pieces = spread_weights(expert_up, low_z, weight_strides)

    def small_group(block):
        known = {0: block}
        for number, (axis, stride) in enumerate(steps_group):
            known.update({at | 1 << number: swap(v, axis, stride) for at, v in known.items()})
        return jnp.concatenate([known[at] for at in range(len(known))], axis=0)

    block_count = 1 << len(steps_group)
    routes_all = small_group(routes).reshape(block_count, rows_here, top_count)
    gates_all = small_group(gate_weights).reshape(block_count, rows_here, top_count)
    cot_all = gather_group(cotangent, steps_group)
    experts_here = expert_gate.shape[0]
    capacity = 2 * rows_here * top_count // (experts_here * exp_count)
    first_expert = exp_pos * experts_here + bit_of("seq", low_z) * half_experts
    expert_ids = first_expert + jnp.arange(half_experts, dtype=jnp.int32)
    named = routes_all[:, :, :, None] == expert_ids
    hit = jnp.any(named, axis=2)
    gate_of = jnp.sum(jnp.where(named, gates_all[:, :, :, None], 0.0), axis=2)
    order = jnp.tril(jnp.ones((rows_here, rows_here), BF16))
    rank = jnp.einsum("ts,bse->bte", order, hit.astype(BF16), preferred_element_type=F32)
    places = jnp.where(hit, rank - 1.0, -1.0)
    place_cols = places.astype(BF16)
    place_rows = places.transpose(0, 2, 1).astype(jnp.int32)
    gate_cols = gate_of.astype(BF16)
    gate_rows = gate_of.transpose(0, 2, 1)
    grad_got = dispatch(cot_all, place_rows, capacity, gate_rows)

    hidden_part = shared_gate.shape[1] // block_count
    group_pos = bit_of("seq", low_z) * exp_count + exp_pos
    hidden_start = group_pos * hidden_part
    shared_in = jnp.concatenate(
        [
            lax.dynamic_slice_in_dim(shared_gate, hidden_start, hidden_part, 1),
            lax.dynamic_slice_in_dim(shared_up, hidden_start, hidden_part, 1),
        ],
        axis=1,
    )
    shared_back = lax.dynamic_slice_in_dim(shared_down, hidden_start, hidden_part, 0)
    grad_shid = dot_nt(cot_all, shared_back)

    tokens_f = tokens.astype(F32)
    scale_in = rms_scale(tokens_f)
    in_low = (tokens_f * scale_in * norm_in[None, :]).astype(BF16)
    raw_x = low_dot(in_low, weight_x)
    raw_s = low_dot(in_low, jnp.concatenate([proj_bc, weight_dt], axis=1))
    gate_z = low_dot(in_low, weight_z)
    last_rows = jnp.concatenate([raw_x[length - 8 :], raw_s[length - 8 :, :pair_width]], axis=1)
    halo = lax.ppermute(last_rows, "seq", [(i, i + 1) for i in range(seq_count - 1)])
    padded_ids = jnp.concatenate([jnp.full((CONV - 1,), -1, jnp.int32), segment_ids])
    segs_ext = lax.dynamic_slice_in_dim(padded_ids, seq_pos * length, length + CONV - 1)
    segs = segs_ext[CONV - 1 :]
    spans = segs.reshape(span_count, SPAN)
    before = jnp.concatenate([segs_ext[CONV - 2 : CONV - 1], spans[:-1, -1]])
    marks = jnp.stack(
        [(segs_ext[tap : tap + length] == segs).astype(F32) for tap in range(CONV - 1)]
        + [
            (segs == segs_ext[CONV - 2]).astype(F32),
            (spans == before[:, None]).astype(F32).reshape(length),
            (spans == spans[:, -1:]).astype(F32).reshape(length),
            segs.astype(F32),
            jnp.zeros((length,), F32),
        ],
        axis=1,
    )
    seg_rows = segs.astype(F32).reshape(span_count, 1, SPAN)

    def local_cols(values):
        mine = lax.dynamic_slice_in_dim(values, col_start, local_width, values.ndim - 1)
        return jnp.concatenate([mine, values[..., inner_width:]], axis=-1)

    taps = jnp.concatenate(
        [
            local_cols(conv_weight),
            local_cols(conv_bias)[None, :],
            jnp.zeros((3, channels), F32),
        ],
        axis=0,
    )
    pad_heads = (0, LANES - head_count)
    dt_local = jnp.pad(lax.dynamic_slice_in_dim(dt_bias, head_start, head_count), pad_heads)
    rates_local = jnp.pad(
        -jnp.exp(lax.dynamic_slice_in_dim(decay_log, head_start, head_count)), pad_heads
    )
    lane_on = jnp.arange(LANES) < head_count
    raw_dt = raw_s[:, pair_width:] + dt_local[None, :]
    step_sizes = jnp.where(lane_on[None, :], jax.nn.softplus(raw_dt), 0.0)
    heads = jnp.concatenate(
        [dt_local[None, :], rates_local[None, :], jnp.zeros((6, LANES), F32)], axis=0
    )
    head_dim = local_width // head_count
    spread_f = (
        jnp.arange(LANES)[:, None] == (jnp.arange(local_width) // head_dim)[None, :]
    ).astype(F32)
    spread = spread_f.astype(BF16)

    def tile(cols, turn=lambda i: i):
        return pl.BlockSpec((SPAN, cols), lambda i: (turn(i), 0))

    def whole(*shape):
        return pl.BlockSpec(shape, lambda i: (0,) * len(shape))

    def seg_tile(turn=lambda i: i):
        return pl.BlockSpec((1, 1, SPAN), lambda i: (turn(i), 0, 0))

    shape = jax.ShapeDtypeStruct
    elements = length * SPAN * head_count
    scan_cost = cost(
        4 * elements * LANES, length * (channels * 8 + local_width * 8 + 4096), elements
    )
    conv_out, inputs, bc_low, local_y, reach, entries, last_state = pl.pallas_call(
        scan_forward,
        grid=(span_count,),
        in_specs=[
            tile(local_width),
            tile(raw_s.shape[1]),
            whole(8, channels),
            tile(8),
            seg_tile(),
            whole(8, channels),
            tile(LANES),
            whole(8, LANES),
            whole(LANES, local_width),
        ],
        out_specs=[
            tile(channels),
            tile(local_width),
            tile(pair_width),
            tile(local_width),
            tile(LANES),
            pl.BlockSpec((1, state_dim, local_width), lambda i: (i, 0, 0)),
            whole(state_dim, local_width),
        ],
        out_shape=[
            shape((length, channels), F32),
            shape((length, local_width), BF16),
            shape((length, pair_width), BF16),
            shape((length, local_width), F32),
            shape((length, LANES), F32),
            shape((span_count, state_dim, local_width), F32),
            shape((state_dim, local_width), F32),
        ],
        scratch_shapes=[
            pltpu.VMEM((SPAN + 8, channels), F32),
            pltpu.VMEM((state_dim, local_width), F32),
            pltpu.VMEM((8, LANES), F32),
        ],
        compiler_params=compiler_params(),
        cost_estimate=scan_cost,
        name="scan_forward",
    )(raw_x, raw_s, halo, marks, seg_rows, taps, step_sizes, heads, spread)

    through = jnp.dot(reach[length - 1 :], spread_f, precision=HIGH)
    state_in = earlier_states(through, last_state, seq_strides)
    skip_wide = jnp.dot(
        jnp.pad(lax.dynamic_slice_in_dim(skip_gain, head_start, head_count), pad_heads)[None, :],
        spread_f,
        precision=HIGH,
    )
    gain_local = lax.dynamic_slice_in_dim(gated_gain, col_start, local_width)
    rows_wide = jnp.concatenate(
        [skip_wide, gain_local[None, :], jnp.zeros((6, local_width), F32)], axis=0
    )
    full_y, scaled_low, mixer_part, squares = pl.pallas_call(
        gate_forward,
        grid=(span_count,),
        in_specs=[
            tile(local_width),
            tile(LANES),
            tile(pair_width),
            whole(state_dim, local_width),
            tile(local_width),
            tile(local_width),
            whole(8, local_width),
            whole(LANES, local_width),
            whole(model_width, local_width),
        ],
        out_specs=[tile(local_width), tile(local_width), tile(model_width), tile(1)],
        out_shape=[
            shape((length, local_width), F32),
            shape((length, local_width), BF16),
            shape((length, model_width), BF16),
            shape((length, 1), F32),
        ],
        compiler_params=compiler_params(),
        cost_estimate=cost(
            2 * length * local_width * (model_width + 3 * LANES),
            length * (local_width * 16 + model_width * 2),
        ),
        name="gate_forward",
    )(local_y, reach, bc_low, state_in, inputs, gate_z, rows_wide, spread, weight_out)

    mixer_rows = scatter_exp(mixer_part.reshape(exp_count, rows_here, model_width), exp_strides)
    square_rows = scatter_exp(squares.reshape(exp_count, 1, rows_here), exp_strides)
    square_rows = square_rows.reshape(rows_here, 1)
    scale_mix = lax.rsqrt(square_rows / inner_width + EPS)
    residual = (
        lax.dynamic_slice_in_dim(tokens, exp_pos * rows_here, rows_here).astype(F32)
        + scale_mix * mixer_rows
    )
    scale_mid = rms_scale(residual)
    normed_mid = residual * scale_mid
    mid_low = (normed_mid * norm_mid[None, :]).astype(BF16)
    mid_all = gather_group(mid_low, steps_group)

    got = dispatch(mid_all, place_rows, capacity)
    place_here = jnp.reshape(seq_pos, (1,)).astype(jnp.int32)
    expert_hid, grad_a, grad_b, expert_res, grad_rows = run_experts(
        place_here, got, grad_got, gate_pieces, up_pieces, down_pieces
    )
    shared_ab = low_dot(mid_all, shared_in)
    shared_a, shared_b = shared_ab[:, :hidden_part], shared_ab[:, hidden_part:]
    shared_hid = (jax.nn.silu(shared_a) * shared_b).astype(BF16)
    grad_ab = jnp.concatenate(
        [grad_shid * shared_b * silu_slope(shared_a), grad_shid * jax.nn.silu(shared_a)], axis=1
    ).astype(BF16)
    grad_mid = scatter_group(
        combine(grad_rows, place_cols, grad_ab, shared_in, True), steps_group
    )
    routed = scatter_group(
        combine(expert_res, place_cols, shared_hid, shared_back, False, gate_cols), steps_group
    )
    block_output = (residual + routed).astype(BF16)
    grad_pieces = expert_grads(
        place_here, got, grad_got, expert_hid, grad_a, grad_b, seq_count
    )
    sum_gate_e, sum_up_e, sum_down_e = [
        collect_weights(pieces, low_z, weight_strides) for pieces in grad_pieces
    ]
    sum_down_e = sum_down_e.transpose(0, 2, 1)
    shared_grads = jnp.concatenate(
        [dot_tn(grad_ab, mid_all), dot_tn(shared_hid, cot_all)], axis=0
    ).astype(BF16)

    grad_norm_mid = jnp.sum(grad_mid * normed_mid, axis=0)
    grad_resid = cotangent.astype(F32) + norm_back(grad_mid, norm_mid, normed_mid, scale_mid)
    grad_part = (scale_mix * grad_resid).astype(BF16)
    grad_square = (
        jnp.sum(grad_resid * mixer_rows, axis=1, keepdims=True) * -0.5 * scale_mix**3 / inner_width
    ).astype(BF16)
    grad_part_all = gather_exp(grad_part, exp_strides)
    grad_square_all = gather_exp(grad_square.reshape(1, rows_here), exp_strides)
    grad_square_all = grad_square_all.astype(F32).reshape(length, 1)

    grad_y, grad_z, gate_sums, direct = pl.pallas_call(
        gate_backward,
        grid=(span_count,),
        in_specs=[
            tile(model_width),
            tile(1),
            tile(local_width),
            tile(local_width),
            tile(local_width),
            tile(LANES),
            tile(pair_width),
            whole(8, local_width),
            whole(LANES, local_width),
            whole(model_width, local_width),
        ],
        out_specs=[
            tile(local_width),
            tile(local_width),
            whole(8, local_width),
            whole(state_dim, local_width),
        ],
        out_shape=[
            shape((length, local_width), BF16),
            shape((length, local_width), BF16),
            shape((8, local_width), F32),
            shape((state_dim, local_width), F32),
        ],
        compiler_params=compiler_params(),
        cost_estimate=cost(
            2 * length * local_width * (model_width + 3 * LANES),
            length * (local_width * 16 + model_width * 2),
        ),
        name="gate_backward",
    )(
        grad_part_all,
        grad_square_all,
        full_y,
        gate_z,
        inputs,
        reach,
        bc_low,
        rows_wide,
        spread,
        weight_out,
    )
    state_grad = later_grads(through, direct, seq_strides)
    sum_wout = lax.psum_scatter(
        dot_tn(grad_part_all, scaled_low).astype(BF16), "seq", scatter_dimension=0, tiled=True
    ).astype(F32).T
    sum_wz = lax.psum_scatter(
        dot_tn(in_low, grad_z).astype(BF16), "seq", scatter_dimension=0, tiled=True
    ).astype(F32)

    passed = jnp.concatenate([jnp.ones((1, LANES), F32), reach[SPAN - 1 : length - 1 : SPAN]])
    passed = jnp.broadcast_to(passed[:, None, :], (span_count, 8, LANES))
    turn = lambda i: span_count - 1 - i
    ahead = SPAN // 8
    before_tile = lambda cols: pl.BlockSpec(
        (8, cols), lambda i: (jnp.maximum(turn(i) * ahead - 1, 0), 0)
    )
    grad_x, grad_bc, grad_steps, tail_rows, head_rows, conv_sums, rate_sums = pl.pallas_call(
        scan_backward,
        grid=(span_count,),
        in_specs=[
            tile(channels, turn),
            tile(local_width, turn),
            tile(raw_s.shape[1], turn),
            before_tile(local_width),
            before_tile(raw_s.shape[1]),
            whole(8, channels),
            tile(8, turn),
            seg_tile(turn),
            whole(8, channels),
            tile(LANES, turn),
            whole(8, LANES),
            whole(LANES, local_width),
            whole(local_width, LANES),
            tile(local_width, turn),
            tile(pair_width, turn),
            tile(local_width, turn),
            tile(local_width, turn),
            pl.BlockSpec((1, state_dim, local_width), lambda i: (turn(i), 0, 0)),
            pl.BlockSpec((1, 8, LANES), lambda i: (turn(i), 0, 0)),
            whole(state_dim, local_width),
            whole(state_dim, local_width),
            whole(8, local_width),
        ],
        out_specs=[
            tile(local_width, turn),
            tile(pair_width, turn),
            tile(LANES, turn),
            whole(8, channels),
            whole(8, channels),
            whole(8, channels),
            whole(8, LANES),
        ],
        out_shape=[
            shape((length, local_width), BF16),
            shape((length, pair_width), BF16),
            shape((length, LANES), F32),
            shape((8, channels), F32),
            shape((8, channels), F32),
            shape((8, channels), F32),
            shape((8, LANES), F32),
        ],
        scratch_shapes=[pltpu.VMEM((SPAN + 8, channels), F32)] * 4
        + [pltpu.VMEM((state_dim, local_width), F32), pltpu.VMEM((local_width, SPAN), F32)],
        compiler_params=compiler_params(),
        cost_estimate=cost(
            10 * elements * LANES, length * (channels * 16 + local_width * 16 + 4096), elements
        ),
        name="scan_backward",
    )(
        conv_out,
        raw_x,
        raw_s,
        raw_x,
        raw_s,
        halo,
        marks,
        seg_rows,
        taps,
        step_sizes,
        heads,
        spread,
        spread.T,
        inputs,
        bc_low,
        full_y,
        grad_y,
        entries,
        passed,
        state_in,
        state_grad,
        rows_wide,
    )
    edge = jnp.stack(
        [
            sum(
                taps[tap] * marks[at - tap, tap] * head_rows[at - tap]
                for tap in range(at + 1)
            )
            for at in range(CONV - 1)
        ]
    )
    edge_back = lax.ppermute(edge, "seq", [(i + 1, i) for i in range(seq_count - 1)])
    tail_fixed = tail_rows + jnp.pad(edge_back, ((8 - (CONV - 1), 0), (0, 0)))
    grad_x = grad_x.at[length - 8 :].set(tail_fixed[:, :local_width].astype(BF16))
    grad_bc = grad_bc.at[length - 8 :].set(tail_fixed[:, local_width:].astype(BF16))
    grad_dt_raw = grad_steps * jax.nn.sigmoid(raw_dt) * lane_on.astype(F32)[None, :]
    grad_dt = grad_dt_raw.astype(BF16)
    grad_in = (
        dot_nt(grad_z, weight_z)
        + dot_nt(grad_x, weight_x)
        + dot_nt(grad_dt, weight_dt)
        + dot_nt(grad_bc, proj_bc)
    )
    grad_wxdt = jnp.concatenate([dot_tn(in_low, grad_x), dot_tn(in_low, grad_dt)], axis=1)
    sum_wxdt = lax.psum_scatter(
        grad_wxdt.astype(BF16), "seq", scatter_dimension=0, tiled=True
    ).astype(F32)
    grad_wbc = dot_tn(in_low, grad_bc)
    normed_in = tokens_f * scale_in
    grad_norm_in = jnp.sum(grad_in * normed_in, axis=0)
    grad_in_part = norm_back(grad_in, norm_in, normed_in, scale_in).astype(BF16)
    tokens_grad = grad_resid + scatter_exp(
        grad_in_part.reshape(exp_count, rows_here, model_width), exp_strides
    )

    quarter = scatter_rows(shared_grads, "seq", bits(low_z) + [2 * low_z])
    pieces = lax.all_gather(quarter, ("seq", "exp"), axis=0, tiled=True)
    part_rows = quarter.shape[0]
    pieces = pieces.reshape(2, 2, low_z, exp_count, part_rows, model_width)
    pieces = pieces.transpose(1, 3, 0, 2, 4, 5).reshape(
        block_count, 3, hidden_part, model_width
    )
    pieces = pieces.transpose(1, 0, 2, 3).reshape(3, block_count * hidden_part, model_width)
    pieces = pieces.astype(F32)

    def placed_cols(values, total, start):
        blank = jnp.zeros(values.shape[:-1] + (total,), F32)
        return lax.dynamic_update_slice_in_dim(blank, values, start, values.ndim - 1)

    def placed_conv(values):
        mine = placed_cols(values[..., :local_width], inner_width, col_start)
        return jnp.concatenate([mine, values[..., local_width:]], axis=-1)

    def placed_heads(values):
        return placed_cols(values[:head_count], head_total, head_start)

    skip_sums = jnp.dot(gate_sums[1:2], spread_f.T, precision=HIGH)[0]
    summed = lax.psum(
        (
            grad_norm_in,
            grad_wbc,
            placed_conv(conv_sums[:CONV]),
            placed_conv(conv_sums[CONV]),
            placed_heads(jnp.sum(grad_dt_raw, axis=0)),
            placed_heads(rate_sums[0] * rates_local),
            placed_heads(skip_sums),
            placed_cols(gate_sums[0], inner_width, col_start),
            grad_norm_mid,
        ),
        ("seq", "exp"),
    )
    return (
        block_output,
        tokens_grad,
        summed[0],
        sum_wz,
        sum_wxdt[:, :local_width],
        summed[1],
        sum_wxdt[:, local_width : local_width + head_count],
        summed[2],
        summed[3],
        summed[4],
        summed[5],
        summed[6],
        summed[7],
        sum_wout,
        summed[8],
        sum_gate_e,
        sum_up_e,
        sum_down_e,
        pieces[0].T,
        pieces[1].T,
        pieces[2],
    )


def solution(mesh):
    placed = (
        P("seq", None),
        P(),
        P(("seq", "exp"), None),
        P(("seq", "exp"), None),
        P(("seq", "exp"), None),
        P(),
        P("seq", "exp"),
        P("seq", "exp"),
        P(),
        P("seq", "exp"),
        P(),
        P(),
        P(),
        P(),
        P(),
        P(),
        P("exp", "seq"),
        P(),
        P("exp", "seq", None),
        P("exp", "seq", None),
        P("exp", None, "seq"),
        P(),
        P(),
        P(),
    )
    return jax.shard_map(
        per_device,
        mesh=mesh,
        in_specs=placed,
        out_specs=(
            P(("seq", "exp"), None),
            P(("seq", "exp"), None),
            P(),
            P("seq", "exp"),
            P("seq", "exp"),
            P(),
            P("seq", "exp"),
            P(),
            P(),
            P(),
            P(),
            P(),
            P(),
            P("exp", "seq"),
            P(),
            P("exp", "seq", None),
            P("exp", "seq", None),
            P("exp", None, "seq"),
            P(),
            P(),
            P(),
        ),
        check_vma=False,
    )
```

time: 5850 us -> 2350 us (0.40)
  waiting for transfers between devices: 3260 us -> 1490 us
  local copies, waits for them, and re-layouts: 1020 us -> 162 us
  matrix products: 782 us -> 133 us
  other arithmetic: 578 us -> 132 us
  Pallas kernels: 0 us -> 299 us
  blocking collectives: 85.2 us -> 0 us
  starting transfers between devices: 35.8 us -> 103 us
    ppermute x2 -> x139, waiting for transfers between devices: 4.54 us -> 1270 us  [the longest x137 1270 us: swap(): lax.ppermute(block, axis, [(i, i ^ stride) for i in range(lax.axis_size(a...]
    all_gather x9 -> x4, waiting for transfers between devices: 1250 us -> 39.3 us  [the longest x1 28 us: per_device(): weight_out = lax.all_gather(proj_out.T, 'seq', axis=0, tiled=True)]
    reduce_scatter x8 -> x2, waiting for transfers between devices: 988 us -> 0.01 us  [the longest x1 0.01 us: per_device(): lax.psum_scatter(dot_tn(in_low, grad_z).astype(BF16), 'seq', scatter_dime...]
    dot_general x155 -> x20, matrix products: 782 us -> 133 us  [the longest x7 50.4 us: dot_tn(): lax.dot_general(left, right, (((0,), (0,)), ((), ())), preferred_element_...]
    all_to_all x4 -> x0, waiting for transfers between devices: 550 us -> none  [exp_move(): return lax.all_to_all(rows, 'exp', split_axis=0, concat_axis=0, tiled=True)]
    dynamic_update_slice x61 -> x6, local copies, waits for them, and re-layouts: 349 us -> 1.09 us  [placed_cols(): lax.dynamic_update_slice_in_dim(blank, values, start, values.ndim - 1)]
    pallas_call x0 -> x10, Pallas kernels: none -> 299 us  [the longest x1 70.6 us: run_experts(): pl.pallas_call(partial(expert_kernel, pieces), grid_spec=pltpu.PrefetchSc...]
    psum x2, waiting for transfers between devices: 462 us -> 186 us  [per_device(): lax.psum((grad_norm_in, grad_wbc, placed_conv(conv_sums[:CONV]), placed_c...]
  transfers between devices with their start and end apart: 26 -> 148, of which waited for: 18 -> 65; matrix products, arithmetic and copies ran while one was open for 15% -> 16% of each run, Pallas kernels for 0% -> 9%
where the time goes in v1:
time: 2350 us; the launch traced here: 2340 us
  waiting for transfers between devices  1490 us (63%)
  Pallas kernels  299 us (13%)
  local copies, waits for them, and re-layouts  162 us (7%)
  matrix products  133 us (6%)
  other arithmetic  132 us (6%)
  starting transfers between devices  103 us (4%)
    ppermute x137, waiting for transfers between devices, swap(): lax.ppermute(block, axis, [(i, i ^ stride) for i in range(lax.axis_size(a...  1270 us
    psum x2, waiting for transfers between devices, per_device(): lax.psum((grad_norm_in, grad_wbc, placed_conv(conv_sums[:CONV]), placed_c...  186 us
    ppermute x137, starting transfers between devices, swap(): lax.ppermute(block, axis, [(i, i ^ stride) for i in range(lax.axis_size(a...  98 us
    unnamed x380, local copies, waits for them, and re-layouts  73.1 us
    pallas_call x1, Pallas kernels, run_experts(): pl.pallas_call(partial(expert_kernel, pieces), grid_spec=pltpu.PrefetchSc...  70.6 us
    pallas_call x1, Pallas kernels, per_device(): pl.pallas_call(scan_backward, grid=(span_count,), in_specs=[tile(channels...  53.8 us
    dot_general x7, matrix products, dot_tn(): lax.dot_general(left, right, (((0,), (0,)), ((), ())), preferred_element_...  50.4 us
    dot_general x5, matrix products, dot_nt(): lax.dot_general(left, right, (((1,), (1,)), ((), ())), preferred_element_...  49.6 us
  transfers between devices with their start and end apart: 148, of which 65 were waited for; matrix products, arithmetic and copies ran while one was open for 16% of the time, Pallas kernels for 9%

profile of v1, /device:TPU:0, one launch (start us, length us, event | category | flops | bytes accessed | tf_op | source)
XLA Modules:
  0.0 2337.9 jit_solution(9023242317838577374)
XLA Ops:
  86.7 24.4 %scan_forward.1 = (f32[2048,1024]{1,0:T(8,128)}, bf16[2048,768]{1,0:T(8,128)(2,1)}, bf16[2048,256]{1,0:T(8,128)(2,1)}, f32[2048,768]{1,0:T(8,128)}, f32[2048,128...) custom-call(f32[2048,768]{1,0:T(8,128)} %copy-done.6, f32[2048,384]{1,0:T(8,128)} %copy-done.8, ...), custom_call_target="tpu_custom_call" | custom-call | flops 3221225472 | bytes 37748736 | tf_op jit(solution)/shard_map/scan_forward/pallas_call | solution.py:928
  154.0 28.0 %all-gather.9.cloned.1.call-done.weight = bf16[1536,768]{1,0:T(8,128)(2,1)} async-done(((bf16[192,768]{1,0:T(8,128)(2,1)}), bf16[1536,768]{1,0:T(8,128)(2,1)}) %all-gather.9.cloned.1.call-update) | async-done | bytes 2359312 | tf_op jit(solution)/shard_map/all_gather | solution.py:812
  182.0 17.8 gate_forward.1
  263.4 38.8 %collective-permute-done.42 = bf16[512,768]{1,0:T(8,128)(2,1)} collective-permute-done((bf16[512,768]{1,0:T(8,128)(2,1)}, bf16[512,768]{1,0:T(8,128)(2,1)}, u32[]{:S(2)}, u32[]{:S(2)}) %collective-permute-start.42) | collective-permute-done | bytes 786464 | tf_op jit(solution)/shard_map/ppermute | solution.py:607
  316.0 17.1 collective-permute-done.55.refs_2_
  352.4 18.1 collective-permute-done.62.refs_10_
  372.1 15.2 collective-permute-done.12
  395.1 16.4 collective-permute-done.19
  412.9 17.6 dispatch.3.grad_got
  477.5 52.7 %collective-permute-done.69.refs_18_ = bf16[8,192,512]{2,1,0:T(8,128)(2,1)} collective-permute-done((bf16[8,192,512]{2,1,0:T(8,128)(2,1)S(1)}, bf16[8,192,512]{2,1,0:T(8,128)(2,1)}, u32[]{:S(2)}, u32[]{:S(2)}) %collective-permute-start.69) | collective-permute-done | bytes 1572896 | tf_op jit(solution)/shard_map/ppermute | solution.py:607
  535.4 96.3 %collective-permute-done.59.refs_6_ = bf16[8,192,512]{2,1,0:T(8,128)(2,1)S(1)} collective-permute-done((bf16[8,192,512]{2,1,0:T(8,128)(2,1)}, bf16[8,192,512]{2,1,0:T(8,128)(2,1)S(1)}, u32[]{:S(2)}, u32[]{:S(2)}) %collective-permute-start.59) | collective-permute-done | bytes 1572896 | tf_op jit(solution)/shard_map/ppermute | solution.py:607
  641.4 57.8 %collective-permute-done.66.refs_14_ = bf16[8,192,512]{2,1,0:T(8,128)(2,1)} collective-permute-done((bf16[8,192,512]{2,1,0:T(8,128)(2,1)}, bf16[8,192,512]{2,1,0:T(8,128)(2,1)}, u32[]{:S(2)}, u32[]{:S(2)}) %collective-permute-start.66) | collective-permute-done | bytes 1572896 | tf_op jit(solution)/shard_map/ppermute | solution.py:607
  701.9 30.3 %collective-permute-done.73.refs_22_ = bf16[8,192,512]{2,1,0:T(8,128)(2,1)} collective-permute-done((bf16[8,192,512]{2,1,0:T(8,128)(2,1)}, bf16[8,192,512]{2,1,0:T(8,128)(2,1)}, u32[]{:S(2)}, u32[]{:S(2)}) %collective-permute-start.73) | collective-permute-done | bytes 1572896 | tf_op jit(solution)/shard_map/ppermute | solution.py:607
  742.7 17.0 dispatch.2.got
  770.4 33.7 %collective-permute-done.67.refs_15_ = bf16[8,192,512]{2,1,0:T(8,128)(2,1)} collective-permute-done((bf16[8,192,512]{2,1,0:T(8,128)(2,1)}, bf16[8,192,512]{2,1,0:T(8,128)(2,1)}, u32[]{:S(2)}, u32[]{:S(2)}) %collective-permute-start.67) | collective-permute-done | bytes 1572896 | tf_op jit(solution)/shard_map/ppermute | solution.py:607
  804.1 31.6 %collective-permute-done.74.refs_23_ = bf16[8,192,512]{2,1,0:T(8,128)(2,1)} collective-permute-done((bf16[8,192,512]{2,1,0:T(8,128)(2,1)}, bf16[8,192,512]{2,1,0:T(8,128)(2,1)}, u32[]{:S(2)}, u32[]{:S(2)}) %collective-permute-start.74) | collective-permute-done | bytes 1572896 | tf_op jit(solution)/shard_map/ppermute | solution.py:607
  835.7 70.6 %experts.1 = (bf16[8,768,512]{2,1,0:T(8,128)(2,1)}, bf16[8,768,512]{2,1,0:T(8,128)(2,1)}, bf16[8,768,512]{2,1,0:T(8,128)(2,1)}, bf16[8,8,96,1536]{3,2,1,0:T(8,128)(2,1)}, bf16[8,8,96,1536]{3,2,1,0:T(8,128)(2,1)}) custom-call(s32[1]{0:T(128)} %bitcast.26.me, bf16[8,8,96,1536]{3,2,1,0:T(8,128)(2,1)} %dispatch.2.got, ...), custom_call_target="tpu_custom_call" | custom-call | flops 57982058496 | bytes 113246208 | tf_op jit(solution)/shard_map/experts/pallas_call | solution.py:490
  906.3 20.1 combine.3
  931.0 21.0 combine.2
  962.3 17.3 collective-permute-done.94
  997.4 15.1 collective-permute-done.91
  1037.3 13.9 collective-permute-done.101
  1053.3 14.8 collective-permute-done.87
  1069.1 15.9 collective-permute-done.98
  1106.7 33.8 %collective-permute-done.103 = bf16[512,1536]{1,0:T(8,128)(2,1)S(1)} collective-permute-done((bf16[512,1536]{1,0:T(8,128)(2,1)S(1)}, bf16[512,1536]{1,0:T(8,128)(2,1)S(1)}, u32[]{:S(2)}, u32[]{:S(2)}) %collective-permute-start.103) | collective-permute-done | bytes 1572896 | tf_op jit(solution)/shard_map/ppermute | solution.py:607
  1167.4 18.0 gate_backward.1
  1227.1 53.8 %scan_backward.1 = (bf16[2048,768]{1,0:T(8,128)(2,1)}, bf16[2048,256]{1,0:T(8,128)(2,1)}, f32[2048,128]{1,0:T(8,128)}, f32[8,1024]{1,0:T(8,128)}, f32[8,1024]{1,...) custom-call(f32[2048,1024]{1,0:T(8,128)} %get-tuple-element.107.conv, f32[2048,768]{1,0:T(8,128)} %copy-done.6, ...), custom_call_target="tpu_custom_call" | custom-call | flops 8053063680 | bytes 67108864 | tf_op jit(solution)/shard_map/scan_backward/pallas_call | solution.py:1122
  1317.8 44.1 %collective-permute-done.137 = bf16[192,1536]{1,0:T(8,128)(2,1)S(1)} collective-permute-done((bf16[192,1536]{1,0:T(8,128)(2,1)S(1)}, bf16[192,1536]{1,0:T(8,128)(2,1)S(1)}, u32[]{:S(2)}, u32[]{:S(2)}) %collective-permute-start.137) | collective-permute-done | bytes 589856 | tf_op jit(solution)/shard_map/ppermute | solution.py:607
  1365.0 38.9 %expert_grads.1 = (bf16[8,192,512]{2,1,0:T(8,128)(2,1)}, bf16[8,192,512]{2,1,0:T(8,128)(2,1)}, bf16[8,192,512]{2,1,0:T(8,128)(2,1)}, bf16[8,192,512]{2,1,0:T(8,1...) custom-call(s32[1]{0:T(128)} %bitcast.26.me, ...), custom_call_target="tpu_custom_call" | custom-call | flops 28991029248 | bytes 75497472 | tf_op jit(solution)/shard_map/expert_grads/pallas_call | solution.py:536
  1408.9 38.9 %collective-permute-done.116 = bf16[8,192,512]{2,1,0:T(8,128)(2,1)} collective-permute-done((bf16[8,192,512]{2,1,0:T(8,128)(2,1)}, bf16[8,192,512]{2,1,0:T(8,128)(2,1)}, u32[]{:S(2)}, u32[]{:S(2)}) %collective-permute-start.116) | collective-permute-done | bytes 1572896 | tf_op jit(solution)/shard_map/ppermute | solution.py:607
  1447.9 50.4 %collective-permute-done.117 = bf16[8,192,512]{2,1,0:T(8,128)(2,1)S(1)} collective-permute-done((bf16[8,192,512]{2,1,0:T(8,128)(2,1)}, bf16[8,192,512]{2,1,0:T(8,128)(2,1)S(1)}, u32[]{:S(2)}, u32[]{:S(2)}) %collective-permute-start.117) | collective-permute-done | bytes 1572896 | tf_op jit(solution)/shard_map/ppermute | solution.py:607
  1498.3 33.7 %collective-permute-done.134 = bf16[8,192,512]{2,1,0:T(8,128)(2,1)S(1)} collective-permute-done((bf16[8,192,512]{2,1,0:T(8,128)(2,1)}, bf16[8,192,512]{2,1,0:T(8,128)(2,1)S(1)}, u32[]{:S(2)}, u32[]{:S(2)}) %collective-permute-start.134) | collective-permute-done | bytes 1572896 | tf_op jit(solution)/shard_map/ppermute | solution.py:607
  1533.9 31.8 %collective-permute-done.120 = bf16[8,192,512]{2,1,0:T(8,128)(2,1)S(1)} collective-permute-done((bf16[8,192,512]{2,1,0:T(8,128)(2,1)}, bf16[8,192,512]{2,1,0:T(8,128)(2,1)S(1)}, u32[]{:S(2)}, u32[]{:S(2)}) %collective-permute-start.120) | collective-permute-done | bytes 1572896 | tf_op jit(solution)/shard_map/ppermute | solution.py:607
  1566.2 33.2 %collective-permute-done.119 = bf16[8,192,512]{2,1,0:T(8,128)(2,1)S(1)} collective-permute-done((bf16[8,192,512]{2,1,0:T(8,128)(2,1)}, bf16[8,192,512]{2,1,0:T(8,128)(2,1)S(1)}, u32[]{:S(2)}, u32[]{:S(2)}) %collective-permute-start.119) | collective-permute-done | bytes 1572896 | tf_op jit(solution)/shard_map/ppermute | solution.py:607
  1599.4 33.7 %collective-permute-done.127 = bf16[8,192,512]{2,1,0:T(8,128)(2,1)S(1)} collective-permute-done((bf16[8,192,512]{2,1,0:T(8,128)(2,1)}, bf16[8,192,512]{2,1,0:T(8,128)(2,1)S(1)}, u32[]{:S(2)}, u32[]{:S(2)}) %collective-permute-start.127) | collective-permute-done | bytes 1572896 | tf_op jit(solution)/shard_map/ppermute | solution.py:607
  1633.6 33.2 %collective-permute-done.131 = bf16[8,192,512]{2,1,0:T(8,128)(2,1)S(1)} collective-permute-done((bf16[8,192,512]{2,1,0:T(8,128)(2,1)}, bf16[8,192,512]{2,1,0:T(8,128)(2,1)S(1)}, u32[]{:S(2)}, u32[]{:S(2)}) %collective-permute-start.131) | collective-permute-done | bytes 1572896 | tf_op jit(solution)/shard_map/ppermute | solution.py:607
  1666.8 33.7 %collective-permute-done.133 = bf16[8,192,512]{2,1,0:T(8,128)(2,1)S(1)} collective-permute-done((bf16[8,192,512]{2,1,0:T(8,128)(2,1)}, bf16[8,192,512]{2,1,0:T(8,128)(2,1)S(1)}, u32[]{:S(2)}, u32[]{:S(2)}) %collective-permute-start.133) | collective-permute-done | bytes 1572896 | tf_op jit(solution)/shard_map/ppermute | solution.py:607
  1701.8 32.4 %collective-permute-done.124 = bf16[8,192,512]{2,1,0:T(8,128)(2,1)S(1)} collective-permute-done((bf16[8,192,512]{2,1,0:T(8,128)(2,1)S(1)}, bf16[8,192,512]{2,1,0:T(8,128)(2,1)S(1)}, u32[]{:S(2)}, u32[]{:S(2)}) %collective-permute-start.124) | collective-permute-done | bytes 1572896 | tf_op jit(solution)/shard_map/ppermute | solution.py:607
  1737.4 30.5 %collective-permute-done.126 = bf16[8,192,512]{2,1,0:T(8,128)(2,1)S(1)} collective-permute-done((bf16[8,192,512]{2,1,0:T(8,128)(2,1)S(1)}, bf16[8,192,512]{2,1,0:T(8,128)(2,1)S(1)}, u32[]{:S(2)}, u32[]{:S(2)}) %collective-permute-start.126) | collective-permute-done | bytes 1572896 | tf_op jit(solution)/shard_map/ppermute | solution.py:607
  1767.9 36.8 %collective-permute-done.128 = bf16[8,192,512]{2,1,0:T(8,128)(2,1)S(1)} collective-permute-done((bf16[8,192,512]{2,1,0:T(8,128)(2,1)S(1)}, bf16[8,192,512]{2,1,0:T(8,128)(2,1)S(1)}, u32[]{:S(2)}, u32[]{:S(2)}) %collective-permute-start.128) | collective-permute-done | bytes 1572896 | tf_op jit(solution)/shard_map/ppermute | solution.py:607
  1806.7 61.9 %collective-permute-done.132 = bf16[8,192,512]{2,1,0:T(8,128)(2,1)S(1)} collective-permute-done((bf16[8,192,512]{2,1,0:T(8,128)(2,1)S(1)}, bf16[8,192,512]{2,1,0:T(8,128)(2,1)S(1)}, u32[]{:S(2)}, u32[]{:S(2)}) %collective-permute-start.132) | collective-permute-done | bytes 1572896 | tf_op jit(solution)/shard_map/ppermute | solution.py:607
  1876.3 59.8 %collective-permute-done.118 = bf16[8,192,512]{2,1,0:T(8,128)(2,1)S(1)} collective-permute-done((bf16[8,192,512]{2,1,0:T(8,128)(2,1)S(1)}, bf16[8,192,512]{2,1,0:T(8,128)(2,1)S(1)}, u32[]{:S(2)}, u32[]{:S(2)}) %collective-permute-start.118) | collective-permute-done | bytes 1572896 | tf_op jit(solution)/shard_map/ppermute | solution.py:607
  1938.7 31.0 %collective-permute-done.125 = bf16[8,192,512]{2,1,0:T(8,128)(2,1)S(1)} collective-permute-done((bf16[8,192,512]{2,1,0:T(8,128)(2,1)S(1)}, bf16[8,192,512]{2,1,0:T(8,128)(2,1)S(1)}, u32[]{:S(2)}, u32[]{:S(2)}) %collective-permute-start.125) | collective-permute-done | bytes 1572896 | tf_op jit(solution)/shard_map/ppermute | solution.py:607
  2002.9 20.3 fusion.9
  2056.6 28.2 %collective-permute-done.115 = bf16[512,1536]{1,0:T(8,128)(2,1)} collective-permute-done((bf16[512,1536]{1,0:T(8,128)(2,1)}, bf16[512,1536]{1,0:T(8,128)(2,1)}, u32[]{:S(2)}, u32[]{:S(2)}) %collective-permute-start.115) | collective-permute-done | bytes 1572896 | tf_op jit(solution)/shard_map/ppermute | solution.py:607
  2109.8 13.8 fusion.110
  2136.9 45.9 %all-reduce.13.cloned.1.call-done = (f32[1536]{0:T(1024)}, f32[4,3328]{1,0:T(4,128)}, f32[3328]{0:T(1024)}, f32[48]{0:T(128)}, f32[48]{0:T(128)}, /*index=5*/f32[48]{0:T(128)}, f32[3072]{0:T(1024)}, f32[1536]{0:T(1024)}) async-done(((f32[1536]{0:T(1024)}, f32[4,3328]{1,0:T(4,128)}, f32[3328]{0:T(1024)}, f32[48]{0:T(128)}, f32[48]{0:T(128)}, /*index=5*/f32[48]{0:T(128)}, f32[3072]{0:T(1024)}, ...) | async-done | bytes 91728 | tf_op jit(solution)/shard_map/psum | solution.py:1253
  2182.8 140.5 %all-reduce.11.cloned.1.call-done = f32[1536,256]{1,0:T(8,128)} async-done(((f32[1536,256]{1,0:T(8,128)}), f32[1536,256]{1,0:T(8,128)}) %all-reduce.11.cloned.1.call-update) | async-done | bytes 1572880 | tf_op jit(solution)/shard_map/psum | solution.py:1253
  (850 shorter events, 641.7 us)
Async XLA Ops:
  10.0 126.8 %all-gather.7.cloned.1.call-start = ((), (), s32[]{:S(2)}) async-start(), calls=%async_computation.4 | async-start | bytes 2654208 | tf_op jit(solution)/shard_map/all_gather | solution.py:811
  10.7 171.3 %all-gather.9.cloned.1.call-start = ((), (), s32[]{:S(2)}) async-start(), calls=%async_computation.5 | async-start | bytes 2654208 | tf_op jit(solution)/shard_map/all_gather | solution.py:812
  10.8 101.2 %collective-permute-start.27 = (s32[512,6]{0,1:T(8,128)}, s32[512,6]{0,1:T(8,128)}, u32[]{:S(2)}, u32[]{:S(2)}) collective-permute-start(s32[512,6]{0,1:T(8,128)} %param.30), channel_id=1, source_target_pairs={{0,2},{1,3},{2,0},{3,1},{4,6},{5,7},{6,4},{7,5},{8,10},{9,11},{10,... | collective-permute-start | bytes 36872 | tf_op jit(solution)/shard_map/ppermute | solution.py:607
  15.4 188.3 %collective-permute-start.29 = (s32[512,6]{0,1:T(8,128)}, s32[512,6]{0,1:T(8,128)}, u32[]{:S(2)}, u32[]{:S(2)}) collective-permute-start(s32[512,6]{0,1:T(8,128)} %param.30), channel_id=1, source_target_pairs={{0,1},{1,0},{2,3},{3,2},{4,5},{5,4},{6,7},{7,6},{8,9},{9,8},{10,11... | collective-permute-start | bytes 36872 | tf_op jit(solution)/shard_map/ppermute | solution.py:607
  15.4 110.5 %collective-permute-start.48 = (f32[512,6]{0,1:T(8,128)}, f32[512,6]{0,1:T(8,128)}, u32[]{:S(2)}, u32[]{:S(2)}) collective-permute-start(f32[512,6]{0,1:T(8,128)} %param.31), channel_id=1, source_target_pairs={{0,2},{1,3},{2,0},{3,1},{4,6},{5,7},{6,4},{7,5},{8,10},{9,11},{10,... | collective-permute-start | bytes 36872 | tf_op jit(solution)/shard_map/ppermute | solution.py:607
  15.9 102.2 %collective-permute-start.47 = (f32[512,6]{0,1:T(8,128)}, f32[512,6]{0,1:T(8,128)}, u32[]{:S(2)}, u32[]{:S(2)}) collective-permute-start(f32[512,6]{0,1:T(8,128)} %param.31), channel_id=1, source_target_pairs={{0,8},{4,12},{8,0},{12,4},{16,24},{20,28},{24,16},{28,20},{1,9},{5... | collective-permute-start | bytes 36872 | tf_op jit(solution)/shard_map/ppermute | solution.py:607
  15.9 2073.6 %reduce-scatter.8.cloned.1.call-start = ((), (), s32[]{:S(2)}) async-start(), calls=%async_computation.8 | async-start | bytes 2654208 | tf_op jit(solution)/shard_map/reduce_scatter | solution.py:1108
  86.1 126.6 %collective-permute-start.50 = (f32[512,6]{0,1:T(8,128)}, f32[512,6]{0,1:T(8,128)}, u32[]{:S(2)}, u32[]{:S(2)}) collective-permute-start(f32[512,6]{0,1:T(8,128)} %param.31), channel_id=1, source_target_pairs={{0,1},{1,0},{2,3},{3,2},{4,5},{5,4},{6,7},{7,6},{8,9},{9,8},{10,11... | collective-permute-start | bytes 36872 | tf_op jit(solution)/shard_map/ppermute | solution.py:607
  122.5 112.4 %collective-permute-start.36 = (bf16[512,768]{1,0:T(8,128)(2,1)}, bf16[512,768]{1,0:T(8,128)(2,1)}, u32[]{:S(2)}, u32[]{:S(2)}) collective-permute-start(bf16[512,768]{1,0:T(8,128)(2,1)} %get-tuple-element.354), channel_id=1, source_target_pairs={{0,1},{1,0},{2,3},{3,2},{4,5},{5,4},{6,7},{7,6},{8,9},{9,8},{10,11... | collective-permute-start | bytes 2359304 | tf_op jit(solution)/shard_map/ppermute | solution.py:607
  129.9 106.5 %collective-permute-start.34 = (bf16[512,768]{1,0:T(8,128)(2,1)}, bf16[512,768]{1,0:T(8,128)(2,1)}, u32[]{:S(2)}, u32[]{:S(2)}) collective-permute-start(bf16[512,768]{1,0:T(8,128)(2,1)} %get-tuple-element.354), channel_id=1, source_target_pairs={{0,2},{1,3},{2,0},{3,1},{4,6},{5,7},{6,4},{7,5},{8,10},{9,11},{10,... | collective-permute-start | bytes 2359304 | tf_op jit(solution)/shard_map/ppermute | solution.py:607
  236.4 73.2 %collective-permute-start.9 = (bf16[512,1536]{1,0:T(8,128)(2,1)}, bf16[512,1536]{1,0:T(8,128)(2,1)S(1)}, u32[]{:S(2)}, u32[]{:S(2)}) collective-permute-start(bf16[512,1536]{1,0:T(8,128)(2,1)} %get-tuple-element.344), channel_id=1, source_target_pairs={{0,1},{1,0},{2,3},{3,2},{4,5},{5,4},{6,7},{7,6},{8,9},{9,8},{10,11... | collective-permute-start | bytes 4718600 | tf_op jit(solution)/shard_map/ppermute | solution.py:607
  256.3 76.8 %collective-permute-start.55 = (bf16[8,192,512]{2,1,0:T(8,128)(2,1)}, bf16[8,192,512]{2,1,0:T(8,128)(2,1)}, u32[]{:S(2)}, u32[]{:S(2)}) collective-permute-start(bf16[8,192,512]{2,1,0:T(8,128)(2,1)} %get-tuple-element.352), channel_id=1, source_target_pairs={{0,8},{4,12},{8,0},{12,4},{16,24},{20,28},{24,16},{28,20},{1,9},{5... | collective-permute-start | bytes 4718600 | tf_op jit(solution)/shard_map/ppermute | solution.py:607
  257.0 76.2 %collective-permute-start.57 = (bf16[8,192,512]{2,1,0:T(8,128)(2,1)}, bf16[8,192,512]{2,1,0:T(8,128)(2,1)}, u32[]{:S(2)}, u32[]{:S(2)}) collective-permute-start(bf16[8,192,512]{2,1,0:T(8,128)(2,1)} %get-tuple-element.353.refs_0_), channel_id=1, source_target_pairs={{0,16},{4,20},{8,24},{12,28},{16,0},{20,4},{24,8},{28,12},{1,17},{... | collective-permute-start | bytes 4718600 | tf_op jit(solution)/shard_map/ppermute | solution.py:607
  458.7 74.6 %collective-permute-start.71 = (bf16[8,192,512]{2,1,0:T(8,128)(2,1)S(1)}, bf16[8,192,512]{2,1,0:T(8,128)(2,1)S(1)}, u32[]{:S(2)}, u32[]{:S(2)}) collective-permute-start(bf16[8,192,512]{2,1,0:T(8,128)(2,1)S(1)} %copy-done.45), channel_id=1, source_target_pairs={{0,16},{4,20},{8,24},{12,28},{16,0},{20,4},{24,8},{28,12},{1,17},{... | collective-permute-start | bytes 4718600 | tf_op jit(solution)/shard_map/ppermute | solution.py:607
  462.3 169.4 %collective-permute-start.59 = (bf16[8,192,512]{2,1,0:T(8,128)(2,1)}, bf16[8,192,512]{2,1,0:T(8,128)(2,1)S(1)}, u32[]{:S(2)}, u32[]{:S(2)}) collective-permute-start(bf16[8,192,512]{2,1,0:T(8,128)(2,1)} %collective-permute-done.55.refs_2_), channel_id=1, source_target_pairs={{0,16},{4,20},{8,24},{12,28},{16,0},{20,4},{24,8},{28,12},{1,17},{... | collective-permute-start | bytes 4718600 | tf_op jit(solution)/shard_map/ppermute | solution.py:607
  464.9 167.5 %collective-permute-start.56 = (bf16[8,192,512]{2,1,0:T(8,128)(2,1)}, bf16[8,192,512]{2,1,0:T(8,128)(2,1)S(1)}, u32[]{:S(2)}, u32[]{:S(2)}) collective-permute-start(bf16[8,192,512]{2,1,0:T(8,128)(2,1)} %collective-permute-done.55.refs_2_), channel_id=1, source_target_pairs={{0,4},{4,0},{8,12},{12,8},{16,20},{20,16},{24,28},{28,24},{1,5},{5... | collective-permute-start | bytes 4718600 | tf_op jit(solution)/shard_map/ppermute | solution.py:607
  530.2 169.0 %collective-permute-start.66 = (bf16[8,192,512]{2,1,0:T(8,128)(2,1)}, bf16[8,192,512]{2,1,0:T(8,128)(2,1)}, u32[]{:S(2)}, u32[]{:S(2)}) collective-permute-start(bf16[8,192,512]{2,1,0:T(8,128)(2,1)} %collective-permute-done.62.refs_10_), channel_id=1, source_target_pairs={{0,16},{4,20},{8,24},{12,28},{16,0},{20,4},{24,8},{28,12},{1,17},{... | collective-permute-start | bytes 4718600 | tf_op jit(solution)/shard_map/ppermute | solution.py:607
  533.3 166.5 %collective-permute-start.63 = (bf16[8,192,512]{2,1,0:T(8,128)(2,1)}, bf16[8,192,512]{2,1,0:T(8,128)(2,1)S(1)}, u32[]{:S(2)}, u32[]{:S(2)}) collective-permute-start(bf16[8,192,512]{2,1,0:T(8,128)(2,1)} %collective-permute-done.62.refs_10_), channel_id=1, source_target_pairs={{0,4},{4,0},{8,12},{12,8},{16,20},{20,16},{24,28},{28,24},{1,5},{5... | collective-permute-start | bytes 4718600 | tf_op jit(solution)/shard_map/ppermute | solution.py:607
  533.9 106.4 %collective-permute-start.58 = (bf16[8,192,512]{2,1,0:T(8,128)(2,1)}, bf16[8,192,512]{2,1,0:T(8,128)(2,1)S(1)}, u32[]{:S(2)}, u32[]{:S(2)}) collective-permute-start(bf16[8,192,512]{2,1,0:T(8,128)(2,1)} %collective-permute-done.57.refs_4_), channel_id=1, source_target_pairs={{0,4},{4,0},{8,12},{12,8},{16,20},{20,16},{24,28},{28,24},{1,5},{5... | collective-permute-start | bytes 4718600 | tf_op jit(solution)/shard_map/ppermute | solution.py:607
  634.0 98.3 %collective-permute-start.73 = (bf16[8,192,512]{2,1,0:T(8,128)(2,1)}, bf16[8,192,512]{2,1,0:T(8,128)(2,1)}, u32[]{:S(2)}, u32[]{:S(2)}) collective-permute-start(bf16[8,192,512]{2,1,0:T(8,128)(2,1)} %collective-permute-done.69.refs_18_), channel_id=1, source_target_pairs={{0,16},{4,20},{8,24},{12,28},{16,0},{20,4},{24,8},{28,12},{1,17},{... | collective-permute-start | bytes 4718600 | tf_op jit(solution)/shard_map/ppermute | solution.py:607
  640.4 119.4 %collective-permute-start.70 = (bf16[8,192,512]{2,1,0:T(8,128)(2,1)}, bf16[8,192,512]{2,1,0:T(8,128)(2,1)}, u32[]{:S(2)}, u32[]{:S(2)}) collective-permute-start(bf16[8,192,512]{2,1,0:T(8,128)(2,1)} %collective-permute-done.69.refs_18_), channel_id=1, source_target_pairs={{0,4},{4,0},{8,12},{12,8},{16,20},{20,16},{24,28},{28,24},{1,5},{5... | collective-permute-start | bytes 4718600 | tf_op jit(solution)/shard_map/ppermute | solution.py:607
  701.3 102.8 %collective-permute-start.67 = (bf16[8,192,512]{2,1,0:T(8,128)(2,1)}, bf16[8,192,512]{2,1,0:T(8,128)(2,1)}, u32[]{:S(2)}, u32[]{:S(2)}) collective-permute-start(bf16[8,192,512]{2,1,0:T(8,128)(2,1)} %collective-permute-done.66.refs_14_), channel_id=1, source_target_pairs={{0,4},{4,0},{8,12},{12,8},{16,20},{20,16},{24,28},{28,24},{1,5},{5... | collective-permute-start | bytes 4718600 | tf_op jit(solution)/shard_map/ppermute | solution.py:607
  732.3 103.4 %collective-permute-start.74 = (bf16[8,192,512]{2,1,0:T(8,128)(2,1)}, bf16[8,192,512]{2,1,0:T(8,128)(2,1)}, u32[]{:S(2)}, u32[]{:S(2)}) collective-permute-start(bf16[8,192,512]{2,1,0:T(8,128)(2,1)} %collective-permute-done.73.refs_22_), channel_id=1, source_target_pairs={{0,4},{4,0},{8,12},{12,8},{16,20},{20,16},{24,28},{28,24},{1,5},{5... | collective-permute-start | bytes 4718600 | tf_op jit(solution)/shard_map/ppermute | solution.py:607
  1156.2 935.2 %reduce-scatter.6.cloned.1.call-start = ((), (), s32[]{:S(2)}) async-start(), calls=%async_computation.6 | async-start | bytes 2654208 | tf_op jit(solution)/shard_map/reduce_scatter | solution.py:1111
  1215.7 877.5 %reduce-scatter.10.cloned.1.call-start = ((), (), s32[]{:S(2)}) async-start(), calls=%async_computation.10 | async-start | bytes 3096576
  1307.5 789.6 %all-gather.11.cloned.1.call-start = ((), (), s32[]{:S(2)}) async-start(), calls=%async_computation.9 | async-start | bytes 9732096 | tf_op jit(solution)/shard_map/all_gather | solution.py:1232
  1404.8 778.0 %all-reduce.13.cloned.1.call-start = ((), (), s32[]{:S(2)}) async-start(), calls=%async_computation.11 | async-start | bytes 199680 | tf_op jit(solution)/shard_map/psum | solution.py:1253
  1404.8 93.5 %collective-permute-start.117 = (bf16[8,192,512]{2,1,0:T(8,128)(2,1)}, bf16[8,192,512]{2,1,0:T(8,128)(2,1)S(1)}, u32[]{:S(2)}, u32[]{:S(2)}) collective-permute-start(bf16[8,192,512]{2,1,0:T(8,128)(2,1)} %get-tuple-element.126), channel_id=1, source_target_pairs={{0,4},{4,0},{8,12},{12,8},{16,20},{20,16},{24,28},{28,24},{1,5},{5... | collective-permute-start | bytes 4718600 | tf_op jit(solution)/shard_map/ppermute | solution.py:607
  1406.8 125.2 %collective-permute-start.134 = (bf16[8,192,512]{2,1,0:T(8,128)(2,1)}, bf16[8,192,512]{2,1,0:T(8,128)(2,1)S(1)}, u32[]{:S(2)}, u32[]{:S(2)}) collective-permute-start(bf16[8,192,512]{2,1,0:T(8,128)(2,1)} %get-tuple-element.146), channel_id=1, source_target_pairs={{0,4},{4,0},{8,12},{12,8},{16,20},{20,16},{24,28},{28,24},{1,5},{5... | collective-permute-start | bytes 4718600 | tf_op jit(solution)/shard_map/ppermute | solution.py:607
  1406.9 158.8 %collective-permute-start.120 = (bf16[8,192,512]{2,1,0:T(8,128)(2,1)}, bf16[8,192,512]{2,1,0:T(8,128)(2,1)S(1)}, u32[]{:S(2)}, u32[]{:S(2)}) collective-permute-start(bf16[8,192,512]{2,1,0:T(8,128)(2,1)} %get-tuple-element.130), channel_id=1, source_target_pairs={{0,4},{4,0},{8,12},{12,8},{16,20},{20,16},{24,28},{28,24},{1,5},{5... | collective-permute-start | bytes 4718600 | tf_op jit(solution)/shard_map/ppermute | solution.py:607
  1408.9 190.5 %collective-permute-start.119 = (bf16[8,192,512]{2,1,0:T(8,128)(2,1)}, bf16[8,192,512]{2,1,0:T(8,128)(2,1)S(1)}, u32[]{:S(2)}, u32[]{:S(2)}) collective-permute-start(bf16[8,192,512]{2,1,0:T(8,128)(2,1)} %get-tuple-element.128), channel_id=1, source_target_pairs={{0,4},{4,0},{8,12},{12,8},{16,20},{20,16},{24,28},{28,24},{1,5},{5... | collective-permute-start | bytes 4718600 | tf_op jit(solution)/shard_map/ppermute | solution.py:607
  1447.8 185.3 %collective-permute-start.127 = (bf16[8,192,512]{2,1,0:T(8,128)(2,1)}, bf16[8,192,512]{2,1,0:T(8,128)(2,1)S(1)}, u32[]{:S(2)}, u32[]{:S(2)}) collective-permute-start(bf16[8,192,512]{2,1,0:T(8,128)(2,1)} %get-tuple-element.138), channel_id=1, source_target_pairs={{0,4},{4,0},{8,12},{12,8},{16,20},{20,16},{24,28},{28,24},{1,5},{5... | collective-permute-start | bytes 4718600 | tf_op jit(solution)/shard_map/ppermute | solution.py:607
  1498.3 168.5 %collective-permute-start.131 = (bf16[8,192,512]{2,1,0:T(8,128)(2,1)}, bf16[8,192,512]{2,1,0:T(8,128)(2,1)S(1)}, u32[]{:S(2)}, u32[]{:S(2)}) collective-permute-start(bf16[8,192,512]{2,1,0:T(8,128)(2,1)} %get-tuple-element.142), channel_id=1, source_target_pairs={{0,4},{4,0},{8,12},{12,8},{16,20},{20,16},{24,28},{28,24},{1,5},{5... | collective-permute-start | bytes 4718600 | tf_op jit(solution)/shard_map/ppermute | solution.py:607
  1532.0 168.5 %collective-permute-start.133 = (bf16[8,192,512]{2,1,0:T(8,128)(2,1)}, bf16[8,192,512]{2,1,0:T(8,128)(2,1)S(1)}, u32[]{:S(2)}, u32[]{:S(2)}) collective-permute-start(bf16[8,192,512]{2,1,0:T(8,128)(2,1)} %get-tuple-element.144), channel_id=1, source_target_pairs={{0,4},{4,0},{8,12},{12,8},{16,20},{20,16},{24,28},{28,24},{1,5},{5... | collective-permute-start | bytes 4718600 | tf_op jit(solution)/shard_map/ppermute | solution.py:607
  1565.7 135.3 %collective-permute-start.135 = (bf16[8,192,512]{2,1,0:T(8,128)(2,1)S(1)}, bf16[8,192,512]{2,1,0:T(8,128)(2,1)S(1)}, u32[]{:S(2)}, u32[]{:S(2)}) collective-permute-start(bf16[8,192,512]{2,1,0:T(8,128)(2,1)S(1)} %add_convert_fusion.1), channel_id=1, source_target_pairs={{0,16},{4,20},{8,24},{12,28},{16,0},{20,4},{24,8},{28,12},{1,17},{... | collective-permute-start | bytes 4718600 | tf_op jit(solution)/shard_map/ppermute | solution.py:607
  1599.4 134.8 %collective-permute-start.124 = (bf16[8,192,512]{2,1,0:T(8,128)(2,1)S(1)}, bf16[8,192,512]{2,1,0:T(8,128)(2,1)S(1)}, u32[]{:S(2)}, u32[]{:S(2)}) collective-permute-start(bf16[8,192,512]{2,1,0:T(8,128)(2,1)S(1)} %copy-done.137), channel_id=1, source_target_pairs={{0,4},{4,0},{8,12},{12,8},{16,20},{20,16},{24,28},{28,24},{1,5},{5... | collective-permute-start | bytes 4718600 | tf_op jit(solution)/shard_map/ppermute | solution.py:607
  1633.1 101.1 %collective-permute-start.121 = (bf16[8,192,512]{2,1,0:T(8,128)(2,1)S(1)}, bf16[8,192,512]{2,1,0:T(8,128)(2,1)S(1)}, u32[]{:S(2)}, u32[]{:S(2)}) collective-permute-start(bf16[8,192,512]{2,1,0:T(8,128)(2,1)S(1)} %add_convert_fusion.13), channel_id=1, source_target_pairs={{0,16},{4,20},{8,24},{12,28},{16,0},{20,4},{24,8},{28,12},{1,17},{... | collective-permute-start | bytes 4718600 | tf_op jit(solution)/shard_map/ppermute | solution.py:607
  1666.8 101.1 %collective-permute-start.126 = (bf16[8,192,512]{2,1,0:T(8,128)(2,1)S(1)}, bf16[8,192,512]{2,1,0:T(8,128)(2,1)S(1)}, u32[]{:S(2)}, u32[]{:S(2)}) collective-permute-start(bf16[8,192,512]{2,1,0:T(8,128)(2,1)S(1)} %copy-done.133), channel_id=1, source_target_pairs={{0,4},{4,0},{8,12},{12,8},{16,20},{20,16},{24,28},{28,24},{1,5},{5... | collective-permute-start | bytes 4718600 | tf_op jit(solution)/shard_map/ppermute | solution.py:607
  1700.5 104.2 %collective-permute-start.128 = (bf16[8,192,512]{2,1,0:T(8,128)(2,1)S(1)}, bf16[8,192,512]{2,1,0:T(8,128)(2,1)S(1)}, u32[]{:S(2)}, u32[]{:S(2)}) collective-permute-start(bf16[8,192,512]{2,1,0:T(8,128)(2,1)S(1)} %add_convert_fusion.7), channel_id=1, source_target_pairs={{0,16},{4,20},{8,24},{12,28},{16,0},{20,4},{24,8},{28,12},{1,17},{... | collective-permute-start | bytes 4718600 | tf_op jit(solution)/shard_map/ppermute | solution.py:607
  1701.0 105.0 %collective-permute-start.130 = (bf16[8,192,512]{2,1,0:T(8,128)(2,1)S(1)}, bf16[8,192,512]{2,1,0:T(8,128)(2,1)S(1)}, u32[]{:S(2)}, u32[]{:S(2)}) collective-permute-start(bf16[8,192,512]{2,1,0:T(8,128)(2,1)S(1)} %copy-done.132), channel_id=1, source_target_pairs={{0,4},{4,0},{8,12},{12,8},{16,20},{20,16},{24,28},{28,24},{1,5},{5... | collective-permute-start | bytes 4718600 | tf_op jit(solution)/shard_map/ppermute | solution.py:607
  1734.2 134.4 %collective-permute-start.132 = (bf16[8,192,512]{2,1,0:T(8,128)(2,1)S(1)}, bf16[8,192,512]{2,1,0:T(8,128)(2,1)S(1)}, u32[]{:S(2)}, u32[]{:S(2)}) collective-permute-start(bf16[8,192,512]{2,1,0:T(8,128)(2,1)S(1)} %add_convert_fusion.4), channel_id=1, source_target_pairs={{0,16},{4,20},{8,24},{12,28},{16,0},{20,4},{24,8},{28,12},{1,17},{... | collective-permute-start | bytes 4718600 | tf_op jit(solution)/shard_map/ppermute | solution.py:607
  1734.2 134.4 %collective-permute-start.136 = (bf16[8,192,512]{2,1,0:T(8,128)(2,1)S(1)}, bf16[8,192,512]{2,1,0:T(8,128)(2,1)S(1)}, u32[]{:S(2)}, u32[]{:S(2)}) collective-permute-start(bf16[8,192,512]{2,1,0:T(8,128)(2,1)S(1)} %add_convert_fusion), channel_id=1, source_target_pairs={{0,8},{4,12},{8,0},{12,4},{16,24},{20,28},{24,16},{28,20},{1,9},{5... | collective-permute-start | bytes 4718600 | tf_op jit(solution)/shard_map/ppermute | solution.py:607
  1767.9 168.1 %collective-permute-start.118 = (bf16[8,192,512]{2,1,0:T(8,128)(2,1)S(1)}, bf16[8,192,512]{2,1,0:T(8,128)(2,1)S(1)}, u32[]{:S(2)}, u32[]{:S(2)}) collective-permute-start(bf16[8,192,512]{2,1,0:T(8,128)(2,1)S(1)} %add_convert_fusion.16), channel_id=1, source_target_pairs={{0,16},{4,20},{8,24},{12,28},{16,0},{20,4},{24,8},{28,12},{1,17},{... | collective-permute-start | bytes 4718600 | tf_op jit(solution)/shard_map/ppermute | solution.py:607
  1804.7 131.3 %collective-permute-start.122 = (bf16[8,192,512]{2,1,0:T(8,128)(2,1)S(1)}, bf16[8,192,512]{2,1,0:T(8,128)(2,1)S(1)}, u32[]{:S(2)}, u32[]{:S(2)}) collective-permute-start(bf16[8,192,512]{2,1,0:T(8,128)(2,1)S(1)} %add_convert_fusion.12), channel_id=1, source_target_pairs={{0,8},{4,12},{8,0},{12,4},{16,24},{20,28},{24,16},{28,20},{1,9},{5... | collective-permute-start | bytes 4718600 | tf_op jit(solution)/shard_map/ppermute | solution.py:607
  1806.6 132.1 %collective-permute-start.123 = (bf16[8,192,512]{2,1,0:T(8,128)(2,1)S(1)}, bf16[8,192,512]{2,1,0:T(8,128)(2,1)S(1)}, u32[]{:S(2)}, u32[]{:S(2)}) collective-permute-start(bf16[8,192,512]{2,1,0:T(8,128)(2,1)S(1)} %copy-done.131), channel_id=1, source_target_pairs={{0,4},{4,0},{8,12},{12,8},{16,20},{20,16},{24,28},{28,24},{1,5},{5... | collective-permute-start | bytes 4718600 | tf_op jit(solution)/shard_map/ppermute | solution.py:607
  1868.6 101.1 %collective-permute-start.125 = (bf16[8,192,512]{2,1,0:T(8,128)(2,1)S(1)}, bf16[8,192,512]{2,1,0:T(8,128)(2,1)S(1)}, u32[]{:S(2)}, u32[]{:S(2)}) collective-permute-start(bf16[8,192,512]{2,1,0:T(8,128)(2,1)S(1)} %add_convert_fusion.10), channel_id=1, source_target_pairs={{0,16},{4,20},{8,24},{12,28},{16,0},{20,4},{24,8},{28,12},{1,17},{... | collective-permute-start | bytes 4718600 | tf_op jit(solution)/shard_map/ppermute | solution.py:607
  1868.6 106.9 %collective-permute-start.129 = (bf16[8,192,512]{2,1,0:T(8,128)(2,1)S(1)}, bf16[8,192,512]{2,1,0:T(8,128)(2,1)S(1)}, u32[]{:S(2)}, u32[]{:S(2)}) collective-permute-start(bf16[8,192,512]{2,1,0:T(8,128)(2,1)S(1)} %add_convert_fusion.6), channel_id=1, source_target_pairs={{0,8},{4,12},{8,0},{12,4},{16,24},{20,28},{24,16},{28,20},{1,9},{5... | collective-permute-start | bytes 4718600 | tf_op jit(solution)/shard_map/ppermute | solution.py:607
  2049.8 273.5 %all-reduce.11.cloned.1.call-start = ((), (), s32[]{:S(2)}) async-start(), calls=%async_computation.7 | async-start | bytes 3145728 | tf_op jit(solution)/shard_map/psum | solution.py:1253
  (263 other events, 8062.6 us)
Sparse Core Ops, SparseCore 0:
  10.8 58.7 all-gather.4
  71.8 50.7 all-gather.6
  124.7 57.2 all-gather.8
  1156.3 72.2 reduce-scatter.7
  1232.5 67.6 reduce-scatter.5
  1307.6 92.8 reduce-scatter.9
  1404.9 101.4 all-gather.10
  2049.9 132.7 all-reduce.12
  2190.2 133.0 all-reduce.10

commit v2 on v1

--- a/solution.py
+++ b/solution.py
@@ -5,6 +5,7 @@
 from jax import lax
 from jax.experimental import pallas as pl
 from jax.experimental.pallas import tpu as pltpu
+from jax.sharding import Mesh
 from jax.sharding import PartitionSpec as P
 
 CONV = 4
@@ -13,6 +14,9 @@
 EPS = 1e-05
 FLOOR = -1e30
 HIGH = lax.Precision.HIGHEST
+SEQ = ("far", "near", "low")
+GROUP = ("far", "exp")
+ALL = SEQ + ("exp",)
 VMEM_BYTES = 56 * 1024 * 1024
 F32 = jnp.float32
 BF16 = jnp.bfloat16
@@ -426,130 +430,179 @@
         out[e, 0] = part.astype(BF16)
 
 
-def dispatch(rows, places, slots, gates=None):
+def dispatch(rows, places, slots, width, gates=None, here=None):
     blocks, experts, count = places.shape
-    width = rows.shape[1]
     arrays = (rows, places) if gates is None else (rows, places, gates)
-    small = pl.BlockSpec((1, experts, count), lambda b: (b, 0, 0))
+    kernel = partial(dispatch_kernel, gates is not None)
+    here = jnp.zeros((1,), jnp.int32) if here is None else here
+    small = pl.BlockSpec((1, experts, count), lambda b, here: (b, 0, 0))
     return pl.pallas_call(
-        partial(dispatch_kernel, gates is not None),
-        grid=(blocks,),
-        in_specs=[pl.BlockSpec((count, width), lambda b: (b, 0))] + [small] * (len(arrays) - 1),
-        out_specs=pl.BlockSpec((experts, 1, slots, width), lambda b: (0, b, 0, 0)),
+        lambda here, *refs: kernel(*refs),
+        grid_spec=pltpu.PrefetchScalarGridSpec(
+            num_scalar_prefetch=1,
+            grid=(blocks,),
+            in_specs=[pl.BlockSpec((count, width), lambda b, here: (b ^ here[0], 0))]
+            + [small] * (len(arrays) - 1),
+            out_specs=pl.BlockSpec(
+                (experts, 1, slots, width), lambda b, here: (0, b, 0, 0)
+            ),
+        ),
         out_shape=jax.ShapeDtypeStruct((experts, blocks, slots, width), BF16),
         compiler_params=compiler_params(),
         cost_estimate=cost(
             2 * blocks * experts * slots * count * width,
-            2 * rows.size + 2 * experts * blocks * slots * width,
+            2 * blocks * count * width + 2 * experts * blocks * slots * width,
         ),
         name="dispatch",
-    )(*arrays)
+    )(here, *arrays)
 
 
 def expert_kernel(pieces, me, got, grad_got, *refs):
-    weights = refs[: 3 * pieces]
-    hid_out, a_out, b_out, res_out, row_out, gate, up, down = refs[3 * pieces :]
-    part = weights[0].shape[1]
-    for kind, full in enumerate((gate, up, down)):
-        for piece in range(pieces):
-            start = pl.multiple_of((me[0] ^ piece) * part, part)
-            full[pl.ds(start, part), :] = weights[kind * pieces + piece][0]
+    weights = refs[:pieces]
+    hid_out, grads_out, res_out, row_out, full = refs[pieces:]
+    part = weights[0].shape[-2]
+    hidden = hid_out.shape[2]
+    for piece, ref in enumerate(weights):
+        start = pl.multiple_of((me[0] ^ piece) * part, part)
+        full[pl.ds(start, part), :] = ref[0]
+    gate, up, down = (slice(kind * hidden, (kind + 1) * hidden) for kind in range(3))
     blocks, slots, width = got.shape[1:]
     step = max(1, min(blocks, 384 // slots))
     for first in range(0, blocks, step):
         rows = slice(first * slots, (first + step) * slots)
         taken = got[0, first : first + step].reshape(step * slots, width)
         taken_grad = grad_got[0, first : first + step].reshape(step * slots, width)
-        a = low_dot(taken, gate[...])
-        b = low_dot(taken, up[...])
-        hid_grad = low_dot(taken_grad, down[...])
+        a = low_dot(taken, full[:, gate])
+        b = low_dot(taken, full[:, up])
+        hid_grad = low_dot(taken_grad, full[:, down])
         sig = jax.nn.sigmoid(a)
         act = a * sig
         hid = (act * b).astype(BF16)
         a_grad = (hid_grad * b * (sig * (1.0 + a * (1.0 - sig)))).astype(BF16)
         b_grad = (hid_grad * act).astype(BF16)
         hid_out[0, rows, :] = hid
-        a_out[0, rows, :] = a_grad
-        b_out[0, rows, :] = b_grad
-        res = dot_nt(hid, down[...]).astype(BF16)
-        row = (dot_nt(a_grad, gate[...]) + dot_nt(b_grad, up[...])).astype(BF16)
+        grads_out[0, rows, 0:hidden] = a_grad
+        grads_out[0, rows, hidden:] = b_grad
+        res = dot_nt(hid, full[:, down]).astype(BF16)
+        row = (dot_nt(a_grad, full[:, gate]) + dot_nt(b_grad, full[:, up])).astype(BF16)
         res_out[0, first : first + step] = res.reshape(step, slots, width)
         row_out[0, first : first + step] = row.reshape(step, slots, width)
 
 
-def run_experts(me, got, grad_got, gate, up, down):
-    experts, blocks, slots, width = got.shape
-    pieces = len(gate)
-    part, hidden = gate[0].shape[1:]
+def run_experts(me, got, grad_got, pieces):
+    count, blocks, slots, width = got.shape
+    part, packed = pieces[0].shape[1:]
+    hidden = packed // 3
     total = blocks * slots
     wide = pl.BlockSpec((1, blocks, slots, width), lambda e, me: (e, 0, 0, 0))
     narrow = pl.BlockSpec((1, total, hidden), lambda e, me: (e, 0, 0))
-    piece = pl.BlockSpec((1, part, hidden), lambda e, me: (e, 0, 0))
-    hid_shape = jax.ShapeDtypeStruct((experts, total, hidden), BF16)
-    row_shape = jax.ShapeDtypeStruct(got.shape, BF16)
+    double = pl.BlockSpec((1, total, 2 * hidden), lambda e, me: (e, 0, 0))
+    piece = pl.BlockSpec((1, part, packed), lambda e, me: (e, 0, 0))
+    shape = jax.ShapeDtypeStruct
+    row_shape = shape((count, blocks, slots, width), BF16)
     return pl.pallas_call(
-        partial(expert_kernel, pieces),
+        partial(expert_kernel, len(pieces)),
         grid_spec=pltpu.PrefetchScalarGridSpec(
             num_scalar_prefetch=1,
-            grid=(experts,),
-            in_specs=[wide, wide] + [piece] * (3 * pieces),
-            out_specs=[narrow] * 3 + [wide] * 2,
-            scratch_shapes=[pltpu.VMEM((width, hidden), BF16)] * 3,
+            grid=(count,),
+            in_specs=[wide, wide] + [piece] * len(pieces),
+            out_specs=[narrow, double, wide, wide],
+            scratch_shapes=[pltpu.VMEM((width, packed), BF16)],
         ),
-        out_shape=[hid_shape] * 3 + [row_shape] * 2,
+        out_shape=[
+            shape((count, total, hidden), BF16),
+            shape((count, total, 2 * hidden), BF16),
+            row_shape,
+            row_shape,
+        ],
         compiler_params=compiler_params(),
         cost_estimate=cost(
-            12 * experts * total * width * hidden,
-            8 * got.size + 6 * experts * width * hidden,
-            experts * total * hidden,
+            12 * count * total * width * hidden,
+            count * (8 * total * width + 6 * width * hidden),
+            count * total * hidden,
         ),
         name="experts",
-    )(me, got, grad_got, *gate, *up, *down)
-
-
-def expert_grad_kernel(pieces, me, got, grad_got, hid, a_grad, b_grad, *refs):
-    outs, (gate, up, down) = refs[: 3 * pieces], refs[3 * pieces :]
+    )(me, got, grad_got, *pieces)
+
+
+def expert_grad_kernel(pieces, me, got, grad_got, hid, grads, *refs):
+    outs, full = refs[:pieces], refs[pieces]
     blocks, slots, width = got.shape[1:]
     part = outs[0].shape[1]
+    hidden = hid.shape[2]
     total = blocks * slots
     step = 256
     for start in range(0, width, step):
         cols = slice(start, start + step)
         taken = got[0, :, :, cols].reshape(total, step)
         taken_grad = grad_got[0, :, :, cols].reshape(total, step)
-        gate[cols, :] = dot_tn(taken, a_grad[0]).astype(BF16)
-        up[cols, :] = dot_tn(taken, b_grad[0]).astype(BF16)
-        down[cols, :] = dot_tn(taken_grad, hid[0]).astype(BF16)
-    for kind, full in enumerate((gate, up, down)):
-        for piece in range(pieces):
-            start = pl.multiple_of((me[0] ^ piece) * part, part)
-            outs[kind * pieces + piece][0] = full[pl.ds(start, part), :]
-
-
-def expert_grads(me, got, grad_got, hid, a_grad, b_grad, pieces):
-    experts, blocks, slots, width = got.shape
+        full[cols, 0 : 2 * hidden] = dot_tn(taken, grads[0]).astype(BF16)
+        full[cols, 2 * hidden :] = dot_tn(taken_grad, hid[0]).astype(BF16)
+    for piece in range(pieces):
+        start = pl.multiple_of((me[0] ^ piece) * part, part)
+        outs[piece][0] = full[pl.ds(start, part), :]
+
+
+def expert_grads(me, got, grad_got, hid, grads, pieces):
+    count, blocks, slots, width = got.shape
     total, hidden = hid.shape[1:]
     part = width // pieces
+    packed = 3 * hidden
     wide = pl.BlockSpec((1, blocks, slots, width), lambda e, me: (e, 0, 0, 0))
     narrow = pl.BlockSpec((1, total, hidden), lambda e, me: (e, 0, 0))
-    piece = pl.BlockSpec((1, part, hidden), lambda e, me: (e, 0, 0))
-    outs = pl.pallas_call(
+    double = pl.BlockSpec((1, total, 2 * hidden), lambda e, me: (e, 0, 0))
+    piece = pl.BlockSpec((1, part, packed), lambda e, me: (e, 0, 0))
+    return pl.pallas_call(
         partial(expert_grad_kernel, pieces),
         grid_spec=pltpu.PrefetchScalarGridSpec(
             num_scalar_prefetch=1,
-            grid=(experts,),
-            in_specs=[wide] * 2 + [narrow] * 3,
-            out_specs=[piece] * (3 * pieces),
-            scratch_shapes=[pltpu.VMEM((width, hidden), BF16)] * 3,
+            grid=(count,),
+            in_specs=[wide] * 2 + [narrow, double],
+            out_specs=[piece] * pieces,
+            scratch_shapes=[pltpu.VMEM((width, packed), BF16)],
         ),
-        out_shape=[jax.ShapeDtypeStruct((experts, part, hidden), BF16)] * (3 * pieces),
+        out_shape=[jax.ShapeDtypeStruct((count, part, packed), BF16)] * pieces,
         compiler_params=compiler_params(),
         cost_estimate=cost(
-            6 * experts * total * width * hidden, 4 * got.size + 6 * experts * width * hidden
+            6 * count * total * width * hidden, count * (4 * total * width + 6 * width * hidden)
         ),
         name="expert_grads",
-    )(me, got, grad_got, hid, a_grad, b_grad)
-    return [outs[kind * pieces : (kind + 1) * pieces] for kind in range(3)]
+    )(me, got, grad_got, hid, grads)
+
+
+def owner_kernel(count, me, *refs):
+    arrived, outs = refs[:2], refs[2:]
+    hidden = arrived[0].shape[2] // 3
+    turn = pl.program_id(0)
+    for place, values in enumerate(arrived):
+
+        @pl.when(turn // count == me[0] ^ place)
+        def _():
+            full = values[0].astype(F32)
+            outs[0][0] = full[:, :hidden]
+            outs[1][0] = full[:, hidden : 2 * hidden]
+            outs[2][0] = full[:, 2 * hidden :].T
+
+
+def owner_grads(me, arrived):
+    count, part, packed = arrived[0].shape
+    hidden = packed // 3
+    shape = jax.ShapeDtypeStruct
+    one = lambda rows, cols: pl.BlockSpec((1, rows, cols), lambda e, me: (e, 0, 0))
+    return pl.pallas_call(
+        partial(owner_kernel, count),
+        grid_spec=pltpu.PrefetchScalarGridSpec(
+            num_scalar_prefetch=1,
+            grid=(2 * count,),
+            in_specs=[pl.BlockSpec((1, part, packed), lambda e, me: (e % count, 0, 0))] * 2,
+            out_specs=[one(part, hidden), one(part, hidden), one(hidden, part)],
+        ),
+        out_shape=[shape((2 * count, part, hidden), F32)] * 2
+        + [shape((2 * count, hidden, part), F32)],
+        compiler_params=compiler_params(),
+        cost_estimate=cost(0, 12 * count * part * packed),
+        name="owner_grads",
+    )(me, *arrived)
 
 
 def combine_kernel(weighted, turned, *refs):
@@ -597,7 +650,7 @@
         compiler_params=compiler_params(),
         cost_estimate=cost(
             2 * blocks * count * width * (experts * slots + hidden.shape[1]),
-            2 * rows.size + 2 * blocks * count * width,
+            2 * blocks * experts * slots * width + 2 * blocks * count * width,
         ),
         name="combine",
     )(*arrays)
@@ -617,87 +670,31 @@
     return (lax.axis_index(axis) // stride) % 2
 
 
-def gather_rows(block, axis, strides):
+def after(value, *earlier):
+    return lax.optimization_barrier((value, earlier))[0]
+
+
+def scatter_step(block, stride, left):
+    left = list(reversed(bits(lax.axis_size(SEQ)))) if left is None else list(left)
+    cols = block.shape[1]
+    axis = left.index(stride)
+    left.remove(stride)
+    block = block.reshape((1 << axis, 2, -1, cols))
+    place = bit_of(SEQ, stride)
+    kept = lax.dynamic_index_in_dim(block, place, 1, False)
+    sent = lax.dynamic_index_in_dim(block, 1 - place, 1, False)
+    block = (kept.astype(F32) + swap(sent, SEQ, stride).astype(F32)).astype(block.dtype)
+    return block.reshape(-1, cols), left
+
+
+def sum_all(block, axis, strides):
     for stride in strides:
-        other = swap(block, axis, stride)
-        mine = jnp.concatenate([block, other], axis=0)
-        theirs = jnp.concatenate([other, block], axis=0)
-        block = jnp.where(bit_of(axis, stride) == 0, mine, theirs)
+        block = block + swap(block, axis, stride)
     return block
 
 
-def scatter_rows(block, axis, strides):
-    for stride in reversed(strides):
-        half = block.shape[0] // 2
-        place = bit_of(axis, stride)
-        kept = lax.dynamic_slice_in_dim(block, place * half, half, 0)
-        sent = lax.dynamic_slice_in_dim(block, (1 - place) * half, half, 0)
-        block = (kept.astype(F32) + swap(sent, axis, stride).astype(F32)).astype(block.dtype)
-    return block
-
-
-def gather_group(block, steps):
-    cols = block.shape[1] // 2
-    halves = []
-    for part, order in ((block[:, :cols], (0, 1)), (block[:, cols:], (1, 0))):
-        known = {0: part}
-        numbers = list(order) + list(range(2, len(steps)))
-        for number in numbers:
-            axis, stride = steps[number]
-            got = {place | 1 << number: swap(v, axis, stride) for place, v in known.items()}
-            known.update(got)
-        halves.append(jnp.concatenate([known[place] for place in range(len(known))], axis=0))
-    return jnp.concatenate(halves, axis=1)
-
-
-def scatter_group(block, steps):
-    count = 1 << len(steps)
-    rows, width = block.shape[0] // count, block.shape[1]
-    cols = width // 2
-    halves = []
-    for start, order in ((0, (0, 1)), (cols, (1, 0))):
-        known = {
-            place: lax.slice(block, (place * rows, start), ((place + 1) * rows, start + cols))
-            for place in range(count)
-        }
-        for number in list(reversed(range(2, len(steps)))) + list(reversed(order)):
-            axis, stride = steps[number]
-            flag = 1 << number
-            known = {
-                place: (
-                    v.astype(F32) + swap(known[place | flag], axis, stride).astype(F32)
-                ).astype(BF16 if len(known) > 2 else F32)
-                for place, v in known.items()
-                if not place & flag
-            }
-        halves.append(known[0])
-    return jnp.concatenate(halves, axis=1)
-
-
-def spread_weights(shard, low_z, other_strides):
-    half = shard.shape[0] // 2
-    place = bit_of("seq", low_z)
-    kept = lax.dynamic_slice_in_dim(shard, place * half, half, 0)
-    sent = lax.dynamic_slice_in_dim(shard, (1 - place) * half, half, 0)
-    known = {0: kept, low_z: swap(sent, "seq", low_z)}
-    for stride in other_strides:
-        known.update({at | stride: swap(v, "seq", stride) for at, v in known.items()})
-    return [known[at] for at in range(len(known))]
-
-
-def collect_weights(pieces, low_z, other_strides):
-    known = dict(enumerate(pieces))
-    for stride in reversed(other_strides):
-        known = {
-            at: (v.astype(F32) + swap(known[at | stride], "seq", stride).astype(F32)).astype(BF16)
-            for at, v in known.items()
-            if not at & stride
-        }
-    mine, other = known[0], swap(known[low_z], "seq", low_z)
-    first = bit_of("seq", low_z) == 0
-    return jnp.concatenate(
-        [jnp.where(first, mine, other), jnp.where(first, other, mine)], axis=0
-    ).astype(F32)
+def added(one, two):
+    return (one.astype(F32) + two.astype(F32)).astype(BF16)
 
 
 def gather_exp(block, strides):
@@ -726,34 +723,37 @@
     return known[0]
 
 
-def earlier_states(through, state, strides):
-    before = jnp.zeros_like(state)
-    whole, decay = state, through
-    reach = jnp.ones_like(through)
-    for stride in strides:
-        other = swap(whole.astype(BF16), "seq", stride).astype(F32)
-        other_decay = swap(decay, "seq", stride)
-        high = bit_of("seq", stride) == 1
-        before = jnp.where(high, before + reach * other, before)
-        reach = jnp.where(high, reach * other_decay, reach)
-        whole = jnp.where(high, whole + decay * other, other + other_decay * whole)
-        decay = decay * other_decay
-    return before
-
-
-def later_grads(through, direct, strides):
-    after = jnp.zeros_like(direct)
-    whole, decay = direct, through
-    reach = jnp.ones_like(through)
-    for stride in strides:
-        other = swap(whole.astype(BF16), "seq", stride).astype(F32)
-        other_decay = swap(decay, "seq", stride)
-        low = bit_of("seq", stride) == 0
-        after = jnp.where(low, after + reach * other, after)
-        reach = jnp.where(low, reach * other_decay, reach)
-        whole = jnp.where(low, whole + decay * other, other + other_decay * whole)
-        decay = decay * other_decay
-    return after
+def split_rows(row):
+    high = row.astype(BF16)
+    rest = row - high.astype(F32)
+    middle = rest.astype(BF16)
+    return [high, middle, (rest - middle.astype(F32)).astype(BF16)]
+
+
+def gather_states(through, state):
+    rows = jnp.concatenate(split_rows(through), axis=0)
+    packed = jnp.concatenate(
+        [state.astype(BF16), jnp.pad(rows, ((0, 16 - rows.shape[0]), (0, 0)))], axis=0
+    )
+    gathered = lax.all_gather(packed, SEQ, axis=0).astype(F32)
+    size = state.shape[0]
+    return gathered[:, :size], jnp.sum(gathered[:, size : size + 3], axis=1, keepdims=True)
+
+
+def earlier_states(states, decays):
+    place = lax.axis_index(SEQ)
+    total = jnp.zeros_like(states[0])
+    for at in range(states.shape[0] - 1):
+        total = jnp.where(at < place, states[at] + decays[at] * total, total)
+    return total
+
+
+def later_grads(grads, decays):
+    place = lax.axis_index(SEQ)
+    total = jnp.zeros_like(grads[0])
+    for at in reversed(range(1, grads.shape[0])):
+        total = jnp.where(at > place, grads[at] + decays[at] * total, total)
+    return total
 
 
 def per_device(
@@ -782,10 +782,10 @@
     shared_up,
     shared_down,
 ):
-    seq_pos = lax.axis_index("seq")
+    seq_pos = lax.axis_index(SEQ)
     exp_pos = lax.axis_index("exp")
     exp_count = lax.axis_size("exp")
-    seq_count = lax.axis_size("seq")
+    seq_count = lax.axis_size(SEQ)
     length, model_width = tokens.shape
     rows_here, top_count = routes.shape
     inner_width = gated_gain.shape[0]
@@ -799,52 +799,37 @@
     head_start = exp_pos * head_count
     low_z = seq_count // 4
     seq_strides = bits(seq_count)
-    weight_strides = [2 * low_z] + bits(low_z)
+    y_strides = bits(low_z)
+    far_z = 2 * low_z
     exp_strides = list(reversed(bits(exp_count)))
-    steps_group = [("seq", low_z)] + [("exp", stride) for stride in exp_strides]
+    far_bit = bit_of(SEQ, far_z)
+    block_count = 2 * exp_count
     span_count = length // SPAN
 
     pad_dt = jnp.pad(proj_dt, ((0, 0), (0, LANES - head_count)))
-    weight_xdt = lax.all_gather(
-        jnp.concatenate([proj_x, pad_dt], axis=1), "seq", axis=0, tiled=True
-    )
-    weight_z = lax.all_gather(proj_z, "seq", axis=0, tiled=True)
-    weight_out = lax.all_gather(proj_out.T, "seq", axis=0, tiled=True)
+    projections = lax.all_gather(
+        jnp.concatenate([proj_x, pad_dt, proj_z, proj_out.T], axis=1), SEQ, axis=0, tiled=True
+    )
+    weight_xdt = projections[:, : local_width + LANES]
+    both = projections[:, local_width + LANES :]
     weight_x, weight_dt = weight_xdt[:, :local_width], weight_xdt[:, local_width:]
-
-    half_experts = expert_gate.shape[0] // 2
-    down_pieces = spread_weights(expert_down.transpose(0, 2, 1), low_z, weight_strides)
-    gate_pieces = spread_weights(expert_gate, low_z, weight_strides)
-    up_pieces = spread_weights(expert_up, low_z, weight_strides)
-
-    def small_group(block):
-        known = {0: block}
-        for number, (axis, stride) in enumerate(steps_group):
-            known.update({at | 1 << number: swap(v, axis, stride) for at, v in known.items()})
-        return jnp.concatenate([known[at] for at in range(len(known))], axis=0)
-
-    block_count = 1 << len(steps_group)
-    routes_all = small_group(routes).reshape(block_count, rows_here, top_count)
-    gates_all = small_group(gate_weights).reshape(block_count, rows_here, top_count)
-    cot_all = gather_group(cotangent, steps_group)
+    halo_tokens = lax.ppermute(
+        tokens[length - 8 :], SEQ, [(i, i + 1) for i in range(seq_count - 1)]
+    )
     experts_here = expert_gate.shape[0]
-    capacity = 2 * rows_here * top_count // (experts_here * exp_count)
-    first_expert = exp_pos * experts_here + bit_of("seq", low_z) * half_experts
-    expert_ids = first_expert + jnp.arange(half_experts, dtype=jnp.int32)
-    named = routes_all[:, :, :, None] == expert_ids
-    hit = jnp.any(named, axis=2)
-    gate_of = jnp.sum(jnp.where(named, gates_all[:, :, :, None], 0.0), axis=2)
-    order = jnp.tril(jnp.ones((rows_here, rows_here), BF16))
-    rank = jnp.einsum("ts,bse->bte", order, hit.astype(BF16), preferred_element_type=F32)
-    places = jnp.where(hit, rank - 1.0, -1.0)
-    place_cols = places.astype(BF16)
-    place_rows = places.transpose(0, 2, 1).astype(jnp.int32)
-    gate_cols = gate_of.astype(BF16)
-    gate_rows = gate_of.transpose(0, 2, 1)
-    grad_got = dispatch(cot_all, place_rows, capacity, gate_rows)
+    experts_half = experts_here // 2
+    packed = jnp.concatenate(
+        [expert_gate, expert_up, expert_down.transpose(0, 2, 1)], axis=2
+    )
+    kept = lax.dynamic_slice_in_dim(packed, far_bit * experts_half, experts_half, 0)
+    sent = lax.dynamic_slice_in_dim(packed, (1 - far_bit) * experts_half, experts_half, 0)
+    middle = experts_half // 2 if experts_half > 1 else experts_half
+    low_0 = swap(kept, SEQ, 1)
+    near_0 = swap(kept, SEQ, low_z)
+    got_far = [swap(sent[:middle], SEQ, far_z)]
 
     hidden_part = shared_gate.shape[1] // block_count
-    group_pos = bit_of("seq", low_z) * exp_count + exp_pos
+    group_pos = far_bit * exp_count + exp_pos
     hidden_start = group_pos * hidden_part
     shared_in = jnp.concatenate(
         [
@@ -854,16 +839,15 @@
         axis=1,
     )
     shared_back = lax.dynamic_slice_in_dim(shared_down, hidden_start, hidden_part, 0)
-    grad_shid = dot_nt(cot_all, shared_back)
 
     tokens_f = tokens.astype(F32)
     scale_in = rms_scale(tokens_f)
     in_low = (tokens_f * scale_in * norm_in[None, :]).astype(BF16)
+    halo_f = halo_tokens.astype(F32)
+    halo_low = (halo_f * rms_scale(halo_f) * norm_in[None, :]).astype(BF16)
     raw_x = low_dot(in_low, weight_x)
     raw_s = low_dot(in_low, jnp.concatenate([proj_bc, weight_dt], axis=1))
-    gate_z = low_dot(in_low, weight_z)
-    last_rows = jnp.concatenate([raw_x[length - 8 :], raw_s[length - 8 :, :pair_width]], axis=1)
-    halo = lax.ppermute(last_rows, "seq", [(i, i + 1) for i in range(seq_count - 1)])
+    halo = jnp.concatenate([low_dot(halo_low, weight_x), low_dot(halo_low, proj_bc)], axis=1)
     padded_ids = jnp.concatenate([jnp.full((CONV - 1,), -1, jnp.int32), segment_ids])
     segs_ext = lax.dynamic_slice_in_dim(padded_ids, seq_pos * length, length + CONV - 1)
     segs = segs_ext[CONV - 1 :]
@@ -911,6 +895,17 @@
     ).astype(F32)
     spread = spread_f.astype(BF16)
 
+    raw_x, low_0, near_0, got_far[0] = lax.optimization_barrier(
+        (raw_x, low_0, near_0, got_far[0])
+    )
+    if middle < experts_half:
+        got_far.append(swap(after(sent[middle:], raw_x), SEQ, far_z))
+    low_far = [swap(got_far[0], SEQ, 1)]
+    route_cols = split_rows(gate_weights)
+    route_cols = jnp.concatenate([routes.astype(BF16)] + route_cols, axis=1)
+    route_cols = jnp.pad(route_cols, ((0, 0), (0, LANES - route_cols.shape[1])))
+    cot_one = jnp.concatenate([cotangent, route_cols], axis=1)
+
     def tile(cols, turn=lambda i: i):
         return pl.BlockSpec((SPAN, cols), lambda i: (turn(i), 0))
 
@@ -967,8 +962,24 @@
         name="scan_forward",
     )(raw_x, raw_s, halo, marks, seg_rows, taps, step_sizes, heads, spread)
 
+    last_state, got_far, low_far[0] = lax.optimization_barrier(
+        (last_state, got_far, low_far[0])
+    )
+    got_far = [after(part, last_state) for part in got_far]
+    cot_far = swap(after(cot_one, last_state), SEQ, far_z)
+    low_near = swap(after(near_0, last_state), SEQ, 1)
+    low_far_rest = got_far[1:]
+    got_far = jnp.concatenate(got_far, axis=0)
+    near_far = swap(got_far, SEQ, low_z)
     through = jnp.dot(reach[length - 1 :], spread_f, precision=HIGH)
-    state_in = earlier_states(through, last_state, seq_strides)
+    block_states, block_decays = gather_states(through, last_state)
+    state_in = earlier_states(block_states, block_decays)
+    local_y, state_in, cot_far, near_far, low_near = lax.optimization_barrier(
+        (local_y, state_in, cot_far, near_far, low_near)
+    )
+    low_far = low_far + [swap(after(part, local_y), SEQ, 1) for part in low_far_rest]
+    weight_z, weight_out = both[:, :local_width], both[:, local_width:]
+    gate_z = low_dot(in_low, weight_z)
     skip_wide = jnp.dot(
         jnp.pad(lax.dynamic_slice_in_dim(skip_gain, head_start, head_count), pad_heads)[None, :],
         spread_f,
@@ -1018,36 +1029,120 @@
     scale_mid = rms_scale(residual)
     normed_mid = residual * scale_mid
     mid_low = (normed_mid * norm_mid[None, :]).astype(BF16)
-    mid_all = gather_group(mid_low, steps_group)
-
-    got = dispatch(mid_all, place_rows, capacity)
+    known = {0: after(cot_one, mixer_rows), exp_count: cot_far}
+    for stride in exp_strides[:-1]:
+        keys = list(known)
+        far = swap(jnp.concatenate([known[at] for at in keys], axis=0), "exp", stride)
+        for number, at in enumerate(keys):
+            known[at | stride] = far[number * rows_here : (number + 1) * rows_here]
+    mid_low, known, *low_far = lax.optimization_barrier((mid_low, known, *low_far))
+    mid_all = lax.all_gather(mid_low, GROUP, axis=0, tiled=True)
+    low_far_near = swap(near_far, SEQ, 1)
+    low_far = jnp.concatenate(low_far, axis=0)
+    keys = list(known)
+    far = swap(jnp.concatenate([known[at] for at in keys], axis=0), "exp", 1)
+    for number, at in enumerate(keys):
+        known[at | 1] = far[number * rows_here : (number + 1) * rows_here]
+    cot_all = jnp.concatenate([known[at] for at in range(block_count)], axis=0)
+
+    def natural(values):
+        return jnp.stack(
+            [
+                lax.dynamic_index_in_dim(values, at ^ group_pos, 0, False)
+                for at in range(block_count)
+            ]
+        )
+
+    capacity = 2 * rows_here * top_count // (experts_here * exp_count)
+    first_expert = exp_pos * experts_here + far_bit * experts_half
+    expert_ids = first_expert + jnp.arange(experts_half, dtype=jnp.int32)
+    tables = cot_all[:, model_width:].reshape(block_count, rows_here, LANES)
+    tables = natural(tables).astype(F32).transpose(0, 2, 1)
+    routes_all = tables[:, :top_count].astype(jnp.int32)
+    gates_all = sum(
+        tables[:, at * top_count : (at + 1) * top_count] for at in range(1, 4)
+    )
+    named = routes_all[:, :, None, :] == expert_ids[None, None, :, None]
+    hit = jnp.any(named, axis=1)
+    gate_rows = jnp.sum(jnp.where(named, gates_all[:, :, None, :], 0.0), axis=1)
+    order = jnp.triu(jnp.ones((rows_here, rows_here), BF16))
+    rank = jnp.einsum("bes,st->bet", hit.astype(BF16), order, preferred_element_type=F32)
+    places = jnp.where(hit, rank - 1.0, -1.0)
+    place_rows = places.astype(jnp.int32)
+    place_cols = places.transpose(0, 2, 1).astype(BF16)
+    gate_cols = gate_rows.transpose(0, 2, 1).astype(BF16)
+    group_here = jnp.reshape(group_pos, (1,)).astype(jnp.int32)
+    grad_got = dispatch(
+        cot_all, place_rows, capacity, model_width, gate_rows, group_here
+    )
+    cot_rows = cot_all[:, :model_width]
+    grad_shid = dot_nt(cot_rows, shared_back).reshape(block_count, rows_here, hidden_part)
+    grad_shid = natural(grad_shid).reshape(-1, hidden_part)
+    sets = {
+        0: kept,
+        1: low_0,
+        low_z: near_0,
+        1 | low_z: low_near,
+        far_z: got_far,
+        1 | far_z: low_far,
+        far_z | low_z: near_far,
+        1 | far_z | low_z: low_far_near,
+    }
+    for stride in y_strides[1:]:
+        sets.update({at | stride: swap(v, SEQ, stride) for at, v in sets.items()})
+    mid_all, grad_got, grad_shid, *sets = lax.optimization_barrier(
+        (mid_all, grad_got, grad_shid, *[sets[at] for at in range(seq_count)])
+    )
+
+    got = dispatch(mid_all, place_rows, capacity, model_width)
     place_here = jnp.reshape(seq_pos, (1,)).astype(jnp.int32)
-    expert_hid, grad_a, grad_b, expert_res, grad_rows = run_experts(
-        place_here, got, grad_got, gate_pieces, up_pieces, down_pieces
-    )
+    expert_hid, expert_back, expert_res, grad_rows = run_experts(place_here, got, grad_got, sets)
     shared_ab = low_dot(mid_all, shared_in)
     shared_a, shared_b = shared_ab[:, :hidden_part], shared_ab[:, hidden_part:]
     shared_hid = (jax.nn.silu(shared_a) * shared_b).astype(BF16)
     grad_ab = jnp.concatenate(
         [grad_shid * shared_b * silu_slope(shared_a), grad_shid * jax.nn.silu(shared_a)], axis=1
     ).astype(BF16)
-    grad_mid = scatter_group(
-        combine(grad_rows, place_cols, grad_ab, shared_in, True), steps_group
-    )
-    routed = scatter_group(
-        combine(expert_res, place_cols, shared_hid, shared_back, False, gate_cols), steps_group
-    )
-    block_output = (residual + routed).astype(BF16)
-    grad_pieces = expert_grads(
-        place_here, got, grad_got, expert_hid, grad_a, grad_b, seq_count
-    )
-    sum_gate_e, sum_up_e, sum_down_e = [
-        collect_weights(pieces, low_z, weight_strides) for pieces in grad_pieces
-    ]
-    sum_down_e = sum_down_e.transpose(0, 2, 1)
+    row_part = combine(grad_rows, place_cols, grad_ab, shared_in, True)
+    grad_mid = lax.psum_scatter(row_part, GROUP, scatter_dimension=0, tiled=True)
+    known = dict(
+        enumerate(
+            expert_grads(
+                place_here, got, grad_got, after(expert_hid, row_part), expert_back, seq_count
+            )
+        )
+    )
+
+    def reduced(at, stride, *wait):
+        sent = after(known[at | stride], *wait) if wait else known[at | stride]
+        known[at] = added(known[at], swap(sent, SEQ, stride))
+        return known[at]
+
+    for stride in reversed(y_strides[1:]):
+        for at in [at for at in known if at & stride]:
+            reduced(at ^ stride, stride)
+            del known[at]
+    grad_ab = after(grad_ab, known[0])
     shared_grads = jnp.concatenate(
-        [dot_tn(grad_ab, mid_all), dot_tn(shared_hid, cot_all)], axis=0
+        [
+            dot_tn(grad_ab, mid_all),
+            dot_tn(
+                natural(shared_hid.reshape(block_count, rows_here, -1)).reshape(
+                    shared_hid.shape
+                ),
+                cot_rows,
+            ),
+        ],
+        axis=0,
     ).astype(BF16)
+    first_sum = reduced(low_z | far_z, 1)
+    grad_mid, shared_grads = lax.optimization_barrier((grad_mid, shared_grads))
+    grad_mid = grad_mid.astype(F32)
+    second_sum = reduced(far_z, 1)
+    shard = lax.psum_scatter(
+        shared_grads, ("near", "low"), scatter_dimension=0, tiled=True
+    )
+    pieces = lax.all_gather(shard, ALL, axis=0, tiled=True)
 
     grad_norm_mid = jnp.sum(grad_mid * normed_mid, axis=0)
     grad_resid = cotangent.astype(F32) + norm_back(grad_mid, norm_mid, normed_mid, scale_mid)
@@ -1058,6 +1153,14 @@
     grad_part_all = gather_exp(grad_part, exp_strides)
     grad_square_all = gather_exp(grad_square.reshape(1, rows_here), exp_strides)
     grad_square_all = grad_square_all.astype(F32).reshape(length, 1)
+
+    grad_part_all, known[far_z], known[low_z | far_z], expert_res = lax.optimization_barrier(
+        (grad_part_all, known[far_z], known[low_z | far_z], expert_res)
+    )
+    out_part = combine(
+        expert_res, place_cols, shared_hid, shared_back, False, gate_cols
+    )
+    third_sum = reduced(far_z, low_z)
 
     grad_y, grad_z, gate_sums, direct = pl.pallas_call(
         gate_backward,
@@ -1104,14 +1207,24 @@
         spread,
         weight_out,
     )
-    state_grad = later_grads(through, direct, seq_strides)
-    sum_wout = lax.psum_scatter(
-        dot_tn(grad_part_all, scaled_low).astype(BF16), "seq", scatter_dimension=0, tiled=True
-    ).astype(F32).T
-    sum_wz = lax.psum_scatter(
-        dot_tn(in_low, grad_z).astype(BF16), "seq", scatter_dimension=0, tiled=True
-    ).astype(F32)
-
+    fourth_sum = reduced(low_z, 1)
+    state_grad = later_grads(
+        lax.all_gather(direct.astype(BF16), SEQ, axis=0).astype(F32), block_decays
+    )
+
+    small_first = y_strides + [low_z, far_z]
+    sent = jnp.concatenate([dot_tn(in_low, grad_z), dot_tn(grad_part_all, scaled_low)], axis=1)
+    sent, third_sum, fourth_sum, known[1] = lax.optimization_barrier(
+        (sent.astype(BF16), third_sum, fourth_sum, known[1])
+    )
+    far_back = [swap(third_sum[:middle], SEQ, far_z)]
+    low_sent = swap(known[1], SEQ, 1)
+    sent, sent_left = scatter_step(sent, small_first[0], None)
+    grad_y, state_grad, out_part, sent = lax.optimization_barrier(
+        (grad_y, state_grad, out_part, sent)
+    )
+    near_sent = swap(fourth_sum, SEQ, low_z)
+    routed = lax.psum_scatter(out_part, GROUP, scatter_dimension=0, tiled=True).astype(F32)
     passed = jnp.concatenate([jnp.ones((1, LANES), F32), reach[SPAN - 1 : length - 1 : SPAN]])
     passed = jnp.broadcast_to(passed[:, None, :], (span_count, 8, LANES))
     turn = lambda i: span_count - 1 - i
@@ -1195,6 +1308,35 @@
         state_grad,
         rows_wide,
     )
+    (
+        grad_x,
+        grad_bc,
+        grad_steps,
+        tail_rows,
+        head_rows,
+        conv_sums,
+        rate_sums,
+        far_back[0],
+        third_sum,
+        low_sent,
+        near_sent,
+    ) = lax.optimization_barrier(
+        (
+            grad_x,
+            grad_bc,
+            grad_steps,
+            tail_rows,
+            head_rows,
+            conv_sums,
+            rate_sums,
+            far_back[0],
+            third_sum,
+            low_sent,
+            near_sent,
+        )
+    )
+    if middle < experts_half:
+        far_back.append(swap(third_sum[middle:], SEQ, far_z))
     edge = jnp.stack(
         [
             sum(
@@ -1204,141 +1346,193 @@
             for at in range(CONV - 1)
         ]
     )
-    edge_back = lax.ppermute(edge, "seq", [(i + 1, i) for i in range(seq_count - 1)])
-    tail_fixed = tail_rows + jnp.pad(edge_back, ((8 - (CONV - 1), 0), (0, 0)))
-    grad_x = grad_x.at[length - 8 :].set(tail_fixed[:, :local_width].astype(BF16))
-    grad_bc = grad_bc.at[length - 8 :].set(tail_fixed[:, local_width:].astype(BF16))
+    block_output = (residual + routed).astype(BF16)
+
+    edge = jnp.pad(edge, ((8 - (CONV - 1), 0), (0, 0))).astype(BF16)
+    edge_x, edge_bc = edge[:, :local_width], edge[:, local_width:]
     grad_dt_raw = grad_steps * jax.nn.sigmoid(raw_dt) * lane_on.astype(F32)[None, :]
     grad_dt = grad_dt_raw.astype(BF16)
+    grad_late = jnp.concatenate(
+        [
+            dot_tn(in_low, grad_x) + dot_tn(halo_low, edge_x),
+            dot_tn(in_low, grad_dt),
+            dot_tn(in_low, grad_bc) + dot_tn(halo_low, edge_bc),
+        ],
+        axis=1,
+    ).astype(BF16)
+    late_sum, late_left = scatter_step(grad_late, small_first[0], None)
+    grad_x, late_sum, sent, far_back = lax.optimization_barrier(
+        (grad_x, late_sum, sent, far_back)
+    )
+    for stride in small_first[1:]:
+        sent, sent_left = scatter_step(sent, stride, sent_left)
+    sent = sent.astype(F32)
+    sum_wz, sum_wout = sent[:, :local_width], sent[:, local_width:].T
+    last_sum = added(added(known[0], low_sent), near_sent)
+    owned = owner_grads(
+        jnp.reshape(far_bit, (1,)).astype(jnp.int32),
+        [last_sum, jnp.concatenate(far_back, axis=0)],
+    )
     grad_in = (
         dot_nt(grad_z, weight_z)
         + dot_nt(grad_x, weight_x)
         + dot_nt(grad_dt, weight_dt)
         + dot_nt(grad_bc, proj_bc)
     )
-    grad_wxdt = jnp.concatenate([dot_tn(in_low, grad_x), dot_tn(in_low, grad_dt)], axis=1)
-    sum_wxdt = lax.psum_scatter(
-        grad_wxdt.astype(BF16), "seq", scatter_dimension=0, tiled=True
-    ).astype(F32)
-    grad_wbc = dot_tn(in_low, grad_bc)
+    for stride in small_first[1:]:
+        late_sum, late_left = scatter_step(late_sum, stride, late_left)
+        if stride == low_z:
+            late_sum, owned = lax.optimization_barrier((late_sum, owned))
+    sum_gate_e, sum_up_e, sum_down_e = owned
+    late_sum, conv_sums, rate_sums, gate_sums, grad_norm_mid = lax.optimization_barrier(
+        (late_sum, conv_sums, rate_sums, gate_sums, grad_norm_mid)
+    )
+    late_sum = late_sum.astype(F32)
+    sum_wxdt = late_sum[:, : local_width + LANES]
+    sum_wbc = sum_all(late_sum[:, local_width + LANES :], "exp", exp_strides).astype(BF16)
+    for stride in seq_strides:
+        other = swap(sum_wbc, SEQ, stride)
+        low = bit_of(SEQ, stride) == 0
+        sum_wbc = jnp.where(
+            low,
+            jnp.concatenate([sum_wbc, other], axis=0),
+            jnp.concatenate([other, sum_wbc], axis=0),
+        )
     normed_in = tokens_f * scale_in
-    grad_norm_in = jnp.sum(grad_in * normed_in, axis=0)
+    halo_scale = rms_scale(halo_f)
+    halo_normed = halo_f * halo_scale
+    edge_in = dot_nt(edge_x, weight_x) + dot_nt(edge_bc, proj_bc)
+    grad_norm_in = jnp.sum(grad_in * normed_in, axis=0) + jnp.sum(edge_in * halo_normed, axis=0)
+    edge_part = lax.ppermute(
+        norm_back(edge_in, norm_in, halo_normed, halo_scale),
+        SEQ,
+        [(i + 1, i) for i in range(seq_count - 1)],
+    )
     grad_in_part = norm_back(grad_in, norm_in, normed_in, scale_in).astype(BF16)
+    grad_in_part = grad_in_part.at[length - 8 :].set(
+        (grad_in_part[length - 8 :].astype(F32) + edge_part).astype(BF16)
+    )
     tokens_grad = grad_resid + scatter_exp(
         grad_in_part.reshape(exp_count, rows_here, model_width), exp_strides
     )
 
-    quarter = scatter_rows(shared_grads, "seq", bits(low_z) + [2 * low_z])
-    pieces = lax.all_gather(quarter, ("seq", "exp"), axis=0, tiled=True)
-    part_rows = quarter.shape[0]
-    pieces = pieces.reshape(2, 2, low_z, exp_count, part_rows, model_width)
-    pieces = pieces.transpose(1, 3, 0, 2, 4, 5).reshape(
-        block_count, 3, hidden_part, model_width
-    )
-    pieces = pieces.transpose(1, 0, 2, 3).reshape(3, block_count * hidden_part, model_width)
-    pieces = pieces.astype(F32)
-
-    def placed_cols(values, total, start):
-        blank = jnp.zeros(values.shape[:-1] + (total,), F32)
-        return lax.dynamic_update_slice_in_dim(blank, values, start, values.ndim - 1)
-
-    def placed_conv(values):
-        mine = placed_cols(values[..., :local_width], inner_width, col_start)
-        return jnp.concatenate([mine, values[..., local_width:]], axis=-1)
-
-    def placed_heads(values):
-        return placed_cols(values[:head_count], head_total, head_start)
-
-    skip_sums = jnp.dot(gate_sums[1:2], spread_f.T, precision=HIGH)[0]
-    summed = lax.psum(
-        (
-            grad_norm_in,
-            grad_wbc,
-            placed_conv(conv_sums[:CONV]),
-            placed_conv(conv_sums[CONV]),
-            placed_heads(jnp.sum(grad_dt_raw, axis=0)),
-            placed_heads(rate_sums[0] * rates_local),
-            placed_heads(skip_sums),
-            placed_cols(gate_sums[0], inner_width, col_start),
-            grad_norm_mid,
-        ),
-        ("seq", "exp"),
-    )
+    pieces = pieces.reshape(
+        2, 2, low_z, exp_count, shard.shape[0], model_width
+    ).transpose(0, 3, 1, 2, 4, 5)
+    pieces = pieces.reshape(block_count, 3, hidden_part, model_width).transpose(1, 0, 2, 3)
+    pieces = pieces.reshape(3, block_count * hidden_part, model_width)
+
+    def rows_of(values):
+        flat = values.reshape(-1)
+        count = -(-flat.shape[0] // local_width)
+        return jnp.pad(flat, (0, count * local_width - flat.shape[0])).reshape(count, local_width)
+
+    skip_sums = jnp.dot(gate_sums[1:2], spread_f.T, precision=HIGH)
+    head_rows3 = jnp.concatenate(
+        [jnp.sum(grad_dt_raw, axis=0, keepdims=True), rate_sums[:1] * rates_local, skip_sums]
+    )
+    own_sums = jnp.concatenate(
+        [
+            conv_sums[: CONV + 1, :local_width],
+            gate_sums[:1],
+            jnp.pad(head_rows3, ((0, 0), (0, local_width - LANES))),
+        ]
+    )
+    shared_sums = jnp.concatenate(
+        [rows_of(conv_sums[: CONV + 1, local_width:]), rows_of(grad_norm_mid)]
+    )
+    own_count = own_sums.shape[0]
+    all_sums = sum_all(jnp.concatenate([own_sums, shared_sums]), SEQ, seq_strides)
+    shared_sums = sum_all(all_sums[own_count:], "exp", exp_strides).reshape(-1)
+    own_all = gather_exp(all_sums[None, :own_count], exp_strides)
+    sum_norm_in = sum_all(
+        sum_all(rows_of(grad_norm_in), SEQ, seq_strides), "exp", exp_strides
+    ).reshape(-1)[:model_width]
+    wide = own_all.transpose(1, 0, 2).reshape(own_count, inner_width)
+    head_sums = own_all[:, CONV + 2 :, :head_count].transpose(1, 0, 2).reshape(3, head_total)
+    pair_count = (CONV + 1) * pair_width
+    pair_sums = shared_sums[:pair_count].reshape(CONV + 1, pair_width)
+    pair_rows = -(-pair_count // local_width) * local_width
+    conv_all = jnp.concatenate([wide[: CONV + 1], pair_sums], axis=1)
     return (
         block_output,
         tokens_grad,
-        summed[0],
+        sum_norm_in,
         sum_wz,
         sum_wxdt[:, :local_width],
-        summed[1],
+        sum_wbc.astype(F32),
         sum_wxdt[:, local_width : local_width + head_count],
-        summed[2],
-        summed[3],
-        summed[4],
-        summed[5],
-        summed[6],
-        summed[7],
+        conv_all[:CONV],
+        conv_all[CONV],
+        head_sums[0],
+        head_sums[1],
+        head_sums[2],
+        wide[CONV + 1],
         sum_wout,
-        summed[8],
+        shared_sums[pair_rows : pair_rows + model_width],
         sum_gate_e,
         sum_up_e,
         sum_down_e,
-        pieces[0].T,
-        pieces[1].T,
-        pieces[2],
+        pieces[0].T.astype(F32),
+        pieces[1].T.astype(F32),
+        pieces[2].astype(F32),
     )
 
 
 def solution(mesh):
     placed = (
-        P("seq", None),
+        P(SEQ, None),
         P(),
-        P(("seq", "exp"), None),
-        P(("seq", "exp"), None),
-        P(("seq", "exp"), None),
+        P(ALL, None),
+        P(ALL, None),
+        P(ALL, None),
         P(),
-        P("seq", "exp"),
-        P("seq", "exp"),
+        P(SEQ, "exp"),
+        P(SEQ, "exp"),
         P(),
-        P("seq", "exp"),
+        P(SEQ, "exp"),
         P(),
         P(),
         P(),
         P(),
         P(),
         P(),
-        P("exp", "seq"),
+        P("exp", SEQ),
         P(),
-        P("exp", "seq", None),
-        P("exp", "seq", None),
-        P("exp", None, "seq"),
+        P("exp", SEQ, None),
+        P("exp", SEQ, None),
+        P("exp", None, SEQ),
         P(),
         P(),
         P(),
     )
+    seq_count, exp_count = mesh.devices.shape
+    split = Mesh(
+        mesh.devices.reshape(2, 2, seq_count // 4, exp_count), ("far", "near", "low", "exp")
+    )
     return jax.shard_map(
         per_device,
-        mesh=mesh,
+        mesh=split,
         in_specs=placed,
         out_specs=(
-            P(("seq", "exp"), None),
-            P(("seq", "exp"), None),
+            P(ALL, None),
+            P(ALL, None),
             P(),
-            P("seq", "exp"),
-            P("seq", "exp"),
+            P(SEQ, "exp"),
+            P(SEQ, "exp"),
             P(),
-            P("seq", "exp"),
+            P(SEQ, "exp"),
             P(),
             P(),
             P(),
             P(),
             P(),
             P(),
-            P("exp", "seq"),
+            P("exp", SEQ),
             P(),
-            P("exp", "seq", None),
-            P("exp", "seq", None),
-            P("exp", None, "seq"),
+            P("exp", SEQ, None),
+            P("exp", SEQ, None),
+            P("exp", None, SEQ),
             P(),
             P(),
             P(),

time: 2350 us -> 2030 us (0.86)
  waiting for transfers between devices: 1490 us -> 1140 us
  other arithmetic: 132 us -> 181 us
  local copies, waits for them, and re-layouts: 162 us -> 136 us
  Pallas kernels: 299 us -> 323 us
    ppermute x137 -> x59, waiting for transfers between devices: 1270 us -> 775 us  [swap(): lax.ppermute(block, axis, [(i, i ^ stride) for i in range(lax.axis_size(a...]
    psum x2 -> x0, waiting for transfers between devices: 186 us -> none  [per_device(): lax.psum((grad_norm_in, grad_wbc, placed_conv(conv_sums[:CONV]), placed_c...]
    all_gather x4 -> x5, waiting for transfers between devices: 39.3 us -> 189 us  [the longest x1 106 us: per_device(): lax.all_gather(jnp.concatenate([proj_x, pad_dt, proj_z, proj_out.T], axis...]
    ppermute x2, waiting for transfers between devices: 0.01 us -> 90.6 us  [the longest x1 90.6 us: per_device(): lax.ppermute(tokens[length - 8:], SEQ, [(i, i + 1) for i in range(seq_cou...]
    reduce_scatter x2 -> x3, waiting for transfers between devices: 0.01 us -> 83.4 us  [the longest x1 82.4 us: per_device(): lax.psum_scatter(row_part, GROUP, scatter_dimension=0, tiled=True)]
    convert_element_type x28 -> x25, other arithmetic: 29.3 us -> 65.4 us  [the longest x5 32.3 us: added(): return (one.astype(F32) + two.astype(F32)).astype(BF16)]
    unnamed x380 -> x243, local copies, waits for them, and re-layouts: 73.1 us -> 37.8 us
    ppermute x137 -> x59, starting transfers between devices: 98 us -> 75.5 us  [swap(): lax.ppermute(block, axis, [(i, i ^ stride) for i in range(lax.axis_size(a...]
  transfers between devices with their start and end apart: 148 -> 69, of which waited for: 65 -> 32; matrix products, arithmetic and copies ran while one was open for 16% -> 20% of each run, Pallas kernels for 9% -> 10%
where the time goes in v2:
time: 2030 us; the launch traced here: 2010 us
  waiting for transfers between devices  1140 us (56%)
  Pallas kernels  323 us (16%)
  other arithmetic  181 us (9%)
  matrix products  139 us (7%)
  local copies, waits for them, and re-layouts  136 us (7%)
  starting transfers between devices  79.9 us (4%)
    ppermute x59, waiting for transfers between devices, swap(): lax.ppermute(block, axis, [(i, i ^ stride) for i in range(lax.axis_size(a...  775 us
    all_gather x1, waiting for transfers between devices, per_device(): lax.all_gather(jnp.concatenate([proj_x, pad_dt, proj_z, proj_out.T], axis...  106 us
    ppermute x1, waiting for transfers between devices, per_device(): lax.ppermute(tokens[length - 8:], SEQ, [(i, i + 1) for i in range(seq_cou...  90.6 us
    reduce_scatter x1, waiting for transfers between devices, per_device(): lax.psum_scatter(row_part, GROUP, scatter_dimension=0, tiled=True)  82.4 us
    ppermute x59, starting transfers between devices, swap(): lax.ppermute(block, axis, [(i, i ^ stride) for i in range(lax.axis_size(a...  75.5 us
    all_gather x1, waiting for transfers between devices, gather_states(): gathered = lax.all_gather(packed, SEQ, axis=0).astype(F32)  75 us
    pallas_call x1, Pallas kernels, run_experts(): pl.pallas_call(partial(expert_kernel, len(pieces)), grid_spec=pltpu.Prefe...  71.8 us
    dot_general x7, matrix products, dot_nt(): lax.dot_general(left, right, (((1,), (1,)), ((), ())), preferred_element_...  56.7 us
  transfers between devices with their start and end apart: 69, of which 32 were waited for; matrix products, arithmetic and copies ran while one was open for 20% of the time, Pallas kernels for 10%

profile of v2, /device:TPU:0, one launch (start us, length us, event | category | flops | bytes accessed | tf_op | source)
XLA Modules:
  0.0 2013.6 jit_solution(2302308015058876637)
XLA Ops:
  50.1 90.6 %collective-permute-done.3 = bf16[8,1536]{1,0:T(8,128)(2,1)S(1)} collective-permute-done((bf16[8,1536]{1,0:T(8,128)(2,1)S(1)}, bf16[8,1536]{1,0:T(8,128)(2,1)S(1)}, u32[]{:S(2)}, u32[]{:S(2)}) %collective-permute-start.3) | collective-permute-done | bytes 24608 | tf_op jit(solution)/shard_map/ppermute | solution.py:816
  141.4 106.5 %all-gather.8.cloned.1.call-done = bf16[1536,2432]{1,0:T(8,128)(2,1)} async-done(((bf16[192,2432]{1,0:T(8,128)(2,1)}), bf16[1536,2432]{1,0:T(8,128)(2,1)}) %all-gather.8.cloned.1.call-update) | async-done | bytes 7471120 | tf_op jit(solution)/shard_map/all_gather | solution.py:810
  247.9 9.8 fusion.48.raw_x.raw_x_before
  257.7 7.0 collective-permute-done.2
  268.1 11.7 collective-permute-start.5
  290.3 24.4 %scan_forward.1 = (f32[2048,1024]{1,0:T(8,128)}, bf16[2048,768]{1,0:T(8,128)(2,1)}, bf16[2048,256]{1,0:T(8,128)(2,1)}, f32[2048,768]{1,0:T(8,128)}, f32[2048,128...) custom-call(f32[2048,768]{1,0:T(8,128)} %fusion.48.raw_x.raw_x_before, f32[2048,384]{1,0:T(8,128)} %copy-done.8, ...), custom_call_target="tpu_custom_call" | custom-call | flops 3221225472 | bytes 37748736 | tf_op jit(solution)/shard_map/scan_forward/pallas_call | solution.py:923
  314.7 56.9 %collective-permute-done.4 = bf16[4,192,1536]{2,1,0:T(8,128)(2,1)} collective-permute-done((bf16[4,192,1536]{2,1,0:T(8,128)(2,1)}, bf16[4,192,1536]{2,1,0:T(8,128)(2,1)}, u32[]{:S(2)}, u32[]{:S(2)}) %collective-permute-start.4) | collective-permute-done | bytes 2359328 | tf_op jit(solution)/shard_map/ppermute | solution.py:660
  392.9 9.6 fusion.36.gate
  402.5 75.0 %all-gather.14.cloned.1.call-done = bf16[1152,768]{1,0:T(8,128)(2,1)} async-done(((bf16[144,768]{1,0:T(8,128)(2,1)}), bf16[1152,768]{1,0:T(8,128)(2,1)}) %all-gather.14.cloned.1.call-update) | async-done | bytes 1769488 | tf_op jit(solution)/shard_map/all_gather | solution.py:738
  481.0 55.8 %collective-permute-done.6 = bf16[512,1664]{1,0:T(8,128)(2,1)} collective-permute-done((bf16[512,1664]{1,0:T(8,128)(2,1)}, bf16[512,1664]{1,0:T(8,128)(2,1)}, u32[]{:S(2)}, u32[]{:S(2)}) %collective-permute-start.6) | collective-permute-done | bytes 1703968 | tf_op jit(solution)/shard_map/ppermute | solution.py:660
  539.1 17.7 gate_forward.1
  572.5 31.9 %collective-permute-done.11 = f32[1,512]{1,0:T(1,128)S(1)} collective-permute-done((f32[1,512]{1,0:T(1,128)S(1)}, f32[1,512]{1,0:T(1,128)S(1)}, u32[]{:S(2)}, u32[]{:S(2)}) %collective-permute-start.11) | collective-permute-done | bytes 2080 | tf_op jit(solution)/shard_map/ppermute | solution.py:660
  623.0 67.3 %collective-permute-done.15 = bf16[1024,1664]{1,0:T(8,128)(2,1)} collective-permute-done((bf16[1024,1664]{1,0:T(8,128)(2,1)}, bf16[1024,1664]{1,0:T(8,128)(2,1)}, u32[]{:S(2)}, u32[]{:S(2)}) %collective-permute-start.15) | collective-permute-done | bytes 3407904 | tf_op jit(solution)/shard_map/ppermute | solution.py:660
  748.5 17.8 dispatch.2.grad_got
  766.4 45.9 %collective-permute-done.18.refs_7_ = bf16[8,192,1536]{2,1,0:T(8,128)(2,1)} collective-permute-done((bf16[8,192,1536]{2,1,0:T(8,128)(2,1)}, bf16[8,192,1536]{2,1,0:T(8,128)(2,1)}, u32[]{:S(2)}, u32[]{:S(2)}) %collective-permute-start.18) | collective-permute-done | bytes 4718624 | tf_op jit(solution)/shard_map/ppermute | solution.py:660
  812.3 7.4 all-gather.10.cloned.1.call-done.refs_0_
  826.1 17.0 dispatch.3.got
  847.6 71.8 %experts.1 = (bf16[8,768,512]{2,1,0:T(8,128)(2,1)}, bf16[8,768,1024]{2,1,0:T(8,128)(2,1)}, bf16[8,8,96,1536]{3,2,1,0:T(8,128)(2,1)}, bf16[8,8,96,1536]{3,2,1,0:T(8,128)(2,1)}) custom-call(s32[1]{0:T(128)} %bitcast.36.me, bf16[8,8,96,1536]{3,2,1,0:T(8,128)(2,1)} %dispatch.3.got, bf16[8,8,96,1536]{3,2,1,0:T(8,128)(2,1)} %dispatch.2.grad_got, ...), custom_call_target="tpu_custom_call" | custom-call | flops 57982058496 | bytes 113246208 | tf_op jit(solution)/shard_map/experts/pallas_call | solution.py:503
  919.4 20.1 combine.2
  939.5 43.1 %expert_grads.1 = (bf16[8,192,1536]{2,1,0:T(8,128)(2,1)}, bf16[8,192,1536]{2,1,0:T(8,128)(2,1)}, bf16[8,192,1536]{2,1,0:T(8,128)(2,1)}, bf16[8,192,1536]{2,1,0:T...) custom-call(s32[1]{0:T(128)} %bitcast.36.me, ...), custom_call_target="tpu_custom_call" | custom-call | flops 28991029248 | bytes 75497472 | tf_op jit(solution)/shard_map/expert_grads/pallas_call | solution.py:555
  984.2 6.7 convolution_convert_fusion.2
  991.7 7.0 fusion.29
  999.8 82.4 %reduce-scatter.4.cloned.1.call-done = bf16[512,1536]{1,0:T(8,128)(2,1)} async-done(((bf16[4096,1536]{1,0:T(8,128)(2,1)}), bf16[512,1536]{1,0:T(8,128)(2,1)}) %reduce-scatter.4.cloned.1.call-update) | async-done | bytes 1572880 | tf_op jit(solution)/shard_map/reduce_scatter | solution.py:1107
  1093.2 34.4 %collective-permute-done.19 = bf16[512,1536]{1,0:T(8,128)(2,1)} collective-permute-done((bf16[512,1536]{1,0:T(8,128)(2,1)}, bf16[512,1536]{1,0:T(8,128)(2,1)}, u32[]{:S(2)}, u32[]{:S(2)}) %collective-permute-start.19) | collective-permute-done | bytes 1572896 | tf_op jit(solution)/shard_map/ppermute | solution.py:660
  1127.5 7.6 add_convert_fusion.5
  1135.6 52.4 %collective-permute-done.23 = bf16[8,192,1536]{2,1,0:T(8,128)(2,1)} collective-permute-done((bf16[8,192,1536]{2,1,0:T(8,128)(2,1)}, bf16[8,192,1536]{2,1,0:T(8,128)(2,1)}, u32[]{:S(2)}, u32[]{:S(2)}) %collective-permute-start.23) | collective-permute-done | bytes 4718624 | tf_op jit(solution)/shard_map/ppermute | solution.py:660
  1201.2 17.8 gate_backward.1
  1224.0 118.6 %collective-permute-done.28 = bf16[8,192,1536]{2,1,0:T(8,128)(2,1)S(1)} collective-permute-done((bf16[8,192,1536]{2,1,0:T(8,128)(2,1)}, bf16[8,192,1536]{2,1,0:T(8,128)(2,1)S(1)}, u32[]{:S(2)}, u32[]{:S(2)}) %collective-permute-start.28) | collective-permute-done | bytes 4718624 | tf_op jit(solution)/shard_map/ppermute | solution.py:660
  1348.7 9.8 convolution_convert_fusion
  1367.0 22.6 %collective-permute-done.27 = bf16[8,192,1536]{2,1,0:T(8,128)(2,1)S(1)} collective-permute-done((bf16[8,192,1536]{2,1,0:T(8,128)(2,1)}, bf16[8,192,1536]{2,1,0:T(8,128)(2,1)S(1)}, u32[]{:S(2)}, u32[]{:S(2)}) %collective-permute-start.27) | collective-permute-done | bytes 4718624 | tf_op jit(solution)/shard_map/ppermute | solution.py:660
  1396.6 6.6 copy.169
  1411.0 20.7 %combine.3 = bf16[4096,1536]{1,0:T(8,128)(2,1)} custom-call(bf16[8,8,96,1536]{3,2,1,0:T(8,128)(2,1)} %get-tuple-element.208.refs_0_, bf16[8,512,8]{2,1,0:T(8,128)(2,1)} %get-tuple-element.431.refs_1_, bf16[8,768]{1,0:T(8,128)(2,1)} %fusion.119.refs_2_, f32[1,768]{1,0:T(1,128)} %fusion.143.refs_3_, bf16[8,512,8]{2,1,0:T(8,128)(2,1)} %bitcast.310, ...), custom_call_target="tpu_custom_call" | custom-call | flops 11274289152 | bytes 31457280 | tf_op jit(solution)/shard_map/combine/pallas_call | solution.py:644
  1438.7 10.0 fusion.34
  1451.6 91.9 %collective-permute-done.29 = bf16[4,192,1536]{2,1,0:T(8,128)(2,1)} collective-permute-done((bf16[4,192,1536]{2,1,0:T(8,128)(2,1)}, bf16[4,192,1536]{2,1,0:T(8,128)(2,1)}, u32[]{:S(2)}, u32[]{:S(2)}) %collective-permute-start.29) | collective-permute-done | bytes 2359328 | tf_op jit(solution)/shard_map/ppermute | solution.py:660
  1547.1 53.6 %scan_backward.1 = (bf16[2048,768]{1,0:T(8,128)(2,1)}, bf16[2048,256]{1,0:T(8,128)(2,1)}, f32[2048,128]{1,0:T(8,128)}, f32[8,1024]{1,0:T(8,128)}, f32[8,1024]{1,...) custom-call(f32[2048,1024]{1,0:T(8,128)} %get-tuple-element.218.conv, f32[2048,768]{1,0:T(8,128)} %fusion.48.raw_x.raw_x_before, ...), custom_call_target="tpu_custom_call" | custom-call | flops 8053063680 | bytes 67108864 | tf_op jit(solution)/shard_map/scan_backward/pallas_call | solution.py:1235
  1643.4 9.3 add_convert_fusion.refs_0_
  1652.7 19.9 collective-permute-done.33
  1674.5 109.9 %collective-permute-done.34 = bf16[4,192,1536]{2,1,0:T(8,128)(2,1)} collective-permute-done((bf16[4,192,1536]{2,1,0:T(8,128)(2,1)S(1)}, bf16[4,192,1536]{2,1,0:T(8,128)(2,1)}, u32[]{:S(2)}, u32[]{:S(2)}) %collective-permute-start.34) | collective-permute-done | bytes 2359328 | tf_op jit(solution)/shard_map/ppermute | solution.py:660
  1788.5 9.5 fusion.44
  1798.0 21.4 %fusion.9 = (f32[1536]{0:T(1024)S(1)}, f32[2048]{0:T(1024)S(1)}, f32[2048,1536]{1,0:T(8,128)}) fusion(bf16[2048,1536]{1,0:T(8,128)(2,1)} %param.26, f32[2048]{0:T(1024)S(1)} %copy-done.37, f32[1536]{0:T(1024)S(1)} %copy-done.31, bf16[2048,256]{1,0:T(8,128)(2,1)} %get-tuple-element.234, bf16[1536,256]{1,0:T(8,128)(2,1)S(1)} %copy-done.15, ...), kind=kOutput, calls=%fused_computation.11 | convolution fusion | flops 1642066432 | bytes 58486784 | tf_op jit(solution)/shard_map/dot_general | solution.py:30
  1826.1 19.5 owner_grads.1
  1850.1 10.6 fusion.8
  1862.3 7.8 collective-permute-done.47
  1880.7 8.8 copy.175
  1922.7 13.8 collective-permute-done.51
  1939.3 16.9 collective-permute-done.52
  1962.3 8.4 copy.171
  1990.2 6.6 copy.172
  (602 shorter events, 405.6 us)
Async XLA Ops:
  7.2 240.7 %all-gather.8.cloned.1.call-start = ((), (), s32[]{:S(2)}) async-start(), calls=%async_computation.3 | async-start | bytes 8404992 | tf_op jit(solution)/shard_map/all_gather | solution.py:810
  10.4 467.1 %all-gather.14.cloned.1.call-start = ((), (), s32[]{:S(2)}) async-start(), calls=%async_computation.9 | async-start | bytes 1990656 | tf_op jit(solution)/shard_map/all_gather | solution.py:738
  20.9 245.8 %collective-permute-start.1 = (bf16[8,192,1536]{2,1,0:T(8,128)(2,1)}, bf16[8,192,1536]{2,1,0:T(8,128)(2,1)}, u32[]{:S(2)}, u32[]{:S(2)}) collective-permute-start(bf16[8,192,1536]{2,1,0:T(8,128)(2,1)} %constant_dynamic-slice_fusion.19.refs_0_), channel_id=1, source_target_pairs={{0,8},{4,12},{8,0},{12,4},{16,24},{20,28},{24,16},{28,20},{1,9},{5... | collective-permute-start | bytes 14155784 | tf_op jit(solution)/shard_map/ppermute | solution.py:660
  24.0 242.7 %collective-permute-start = (bf16[8,192,1536]{2,1,0:T(8,128)(2,1)}, bf16[8,192,1536]{2,1,0:T(8,128)(2,1)}, u32[]{:S(2)}, u32[]{:S(2)}) collective-permute-start(bf16[8,192,1536]{2,1,0:T(8,128)(2,1)} %constant_dynamic-slice_fusion.19.refs_0_), channel_id=1, source_target_pairs={{0,4},{4,0},{8,12},{12,8},{16,20},{20,16},{24,28},{28,24},{1,5},{5... | collective-permute-start | bytes 14155784 | tf_op jit(solution)/shard_map/ppermute | solution.py:660
  26.3 114.4 %collective-permute-start.3 = (bf16[8,1536]{1,0:T(8,128)(2,1)S(1)}, bf16[8,1536]{1,0:T(8,128)(2,1)S(1)}, u32[]{:S(2)}, u32[]{:S(2)}) collective-permute-start(bf16[8,1536]{1,0:T(8,128)(2,1)S(1)} %slice.374), channel_id=1, source_target_pairs={{0,4},{4,8},{8,12},{12,16},{16,20},{20,24},{24,28},{1,5},{5,9},{9,... | collective-permute-start | bytes 73736 | tf_op jit(solution)/shard_map/ppermute | solution.py:816
  33.7 231.0 %collective-permute-start.2 = (bf16[4,192,1536]{2,1,0:T(8,128)(2,1)}, bf16[4,192,1536]{2,1,0:T(8,128)(2,1)}, u32[]{:S(2)}, u32[]{:S(2)}) collective-permute-start(bf16[4,192,1536]{2,1,0:T(8,128)(2,1)} %get-tuple-element.417), channel_id=1, source_target_pairs={{0,16},{4,20},{8,24},{12,28},{16,0},{20,4},{24,8},{28,12},{1,17},{... | collective-permute-start | bytes 7077896 | tf_op jit(solution)/shard_map/ppermute | solution.py:660
  266.7 104.8 %collective-permute-start.4 = (bf16[4,192,1536]{2,1,0:T(8,128)(2,1)}, bf16[4,192,1536]{2,1,0:T(8,128)(2,1)}, u32[]{:S(2)}, u32[]{:S(2)}) collective-permute-start(bf16[4,192,1536]{2,1,0:T(8,128)(2,1)} %get-tuple-element.151), channel_id=1, source_target_pairs={{0,16},{4,20},{8,24},{12,28},{16,0},{20,4},{24,8},{28,12},{1,17},{... | collective-permute-start | bytes 7077896 | tf_op jit(solution)/shard_map/ppermute | solution.py:660
  268.1 103.5 %collective-permute-start.5 = (bf16[4,192,1536]{2,1,0:T(8,128)(2,1)}, bf16[4,192,1536]{2,1,0:T(8,128)(2,1)}, u32[]{:S(2)}, u32[]{:S(2)}) collective-permute-start(bf16[4,192,1536]{2,1,0:T(8,128)(2,1)} %collective-permute-done.2), channel_id=1, source_target_pairs={{0,4},{4,0},{8,12},{12,8},{16,20},{20,16},{24,28},{28,24},{1,5},{5... | collective-permute-start | bytes 7077896 | tf_op jit(solution)/shard_map/ppermute | solution.py:660
  378.1 160.9 %collective-permute-start.7 = (bf16[8,192,1536]{2,1,0:T(8,128)(2,1)}, bf16[8,192,1536]{2,1,0:T(8,128)(2,1)}, u32[]{:S(2)}, u32[]{:S(2)}) collective-permute-start(bf16[8,192,1536]{2,1,0:T(8,128)(2,1)} %constant_dynamic-update-slice_fusion.refs_4_), channel_id=1, source_target_pairs={{0,8},{4,12},{8,0},{12,4},{16,24},{20,28},{24,16},{28,20},{1,9},{5... | collective-permute-start | bytes 14155784 | tf_op jit(solution)/shard_map/ppermute | solution.py:660
  378.1 160.9 %collective-permute-start.8 = (bf16[8,192,1536]{2,1,0:T(8,128)(2,1)}, bf16[8,192,1536]{2,1,0:T(8,128)(2,1)}, u32[]{:S(2)}, u32[]{:S(2)}) collective-permute-start(bf16[8,192,1536]{2,1,0:T(8,128)(2,1)} %collective-permute-done.1.refs_2_), channel_id=1, source_target_pairs={{0,4},{4,0},{8,12},{12,8},{16,20},{20,16},{24,28},{28,24},{1,5},{5... | collective-permute-start | bytes 14155784 | tf_op jit(solution)/shard_map/ppermute | solution.py:660
  383.2 436.5 %all-gather.10.cloned.1.call-start = ((), (), s32[]{:S(2)}) async-start(), calls=%async_computation.4 | async-start | bytes 14155776 | tf_op jit(solution)/shard_map/all_gather | solution.py:1039
  387.5 149.3 %collective-permute-start.6 = (bf16[512,1664]{1,0:T(8,128)(2,1)}, bf16[512,1664]{1,0:T(8,128)(2,1)}, u32[]{:S(2)}, u32[]{:S(2)}) collective-permute-start(bf16[512,1664]{1,0:T(8,128)(2,1)} %fusion.41), channel_id=1, source_target_pairs={{0,16},{4,20},{8,24},{12,28},{16,0},{20,4},{24,8},{28,12},{1,17},{... | collective-permute-start | bytes 5111816 | tf_op jit(solution)/shard_map/ppermute | solution.py:660
  560.5 44.0 %collective-permute-start.12 = (bf16[512,1536]{1,0:T(8,128)(2,1)}, bf16[512,1536]{1,0:T(8,128)(2,1)}, u32[]{:S(2)}, u32[]{:S(2)}) collective-permute-start(bf16[512,1536]{1,0:T(8,128)(2,1)} %get-tuple-element.426), channel_id=1, source_target_pairs={{0,1},{1,0},{2,3},{3,2},{4,5},{5,4},{6,7},{7,6},{8,9},{9,8},{10,11... | collective-permute-start | bytes 4718600 | tf_op jit(solution)/shard_map/ppermute | solution.py:660
  567.6 36.8 %collective-permute-start.14 = (bf16[512,1536]{1,0:T(8,128)(2,1)}, bf16[512,1536]{1,0:T(8,128)(2,1)}, u32[]{:S(2)}, u32[]{:S(2)}) collective-permute-start(bf16[512,1536]{1,0:T(8,128)(2,1)} %fusion.26), channel_id=1, source_target_pairs={{0,2},{1,3},{2,0},{3,1},{4,6},{5,7},{6,4},{7,5},{8,10},{9,11},{10,... | collective-permute-start | bytes 4718600 | tf_op jit(solution)/shard_map/ppermute | solution.py:660
  572.0 32.4 %collective-permute-start.11 = (f32[1,512]{1,0:T(1,128)S(1)}, f32[1,512]{1,0:T(1,128)S(1)}, u32[]{:S(2)}, u32[]{:S(2)}) collective-permute-start(f32[1,512]{1,0:T(1,128)S(1)} %fusion.155), channel_id=1, source_target_pairs={{0,2},{1,3},{2,0},{3,1},{4,6},{5,7},{6,4},{7,5},{8,10},{9,11},{10,... | collective-permute-start | bytes 6152 | tf_op jit(solution)/shard_map/ppermute | solution.py:660
  615.1 75.2 %collective-permute-start.15 = (bf16[1024,1664]{1,0:T(8,128)(2,1)}, bf16[1024,1664]{1,0:T(8,128)(2,1)}, u32[]{:S(2)}, u32[]{:S(2)}) collective-permute-start(bf16[1024,1664]{1,0:T(8,128)(2,1)} %pad_maximum_fusion.7), channel_id=1, source_target_pairs={{0,2},{1,3},{2,0},{3,1},{4,6},{5,7},{6,4},{7,5},{8,10},{9,11},{10,... | collective-permute-start | bytes 10223624 | tf_op jit(solution)/shard_map/ppermute | solution.py:660
  616.6 77.7 %collective-permute-start.16 = (bf16[4,192,1536]{2,1,0:T(8,128)(2,1)}, bf16[4,192,1536]{2,1,0:T(8,128)(2,1)}, u32[]{:S(2)}, u32[]{:S(2)}) collective-permute-start(bf16[4,192,1536]{2,1,0:T(8,128)(2,1)} %collective-permute-done.4), channel_id=1, source_target_pairs={{0,4},{4,0},{8,12},{12,8},{16,20},{20,16},{24,28},{28,24},{1,5},{5... | collective-permute-start | bytes 7077896 | tf_op jit(solution)/shard_map/ppermute | solution.py:660
  694.3 387.9 %reduce-scatter.4.cloned.1.call-start = ((), (), s32[]{:S(2)}) async-start(), calls=%async_computation.5 | async-start | bytes 14155776 | tf_op jit(solution)/shard_map/reduce_scatter | solution.py:1107
  704.9 107.3 %collective-permute-start.18 = (bf16[8,192,1536]{2,1,0:T(8,128)(2,1)}, bf16[8,192,1536]{2,1,0:T(8,128)(2,1)}, u32[]{:S(2)}, u32[]{:S(2)}) collective-permute-start(bf16[8,192,1536]{2,1,0:T(8,128)(2,1)} %collective-permute-done.7.refs_6_), channel_id=1, source_target_pairs={{0,4},{4,0},{8,12},{12,8},{16,20},{20,16},{24,28},{28,24},{1,5},{5... | collective-permute-start | bytes 14155784 | tf_op jit(solution)/shard_map/ppermute | solution.py:660
  939.5 282.4 %reduce-scatter.8.cloned.1.call-start = ((), (), s32[]{:S(2)}) async-start(), calls=%async_computation.7 | async-start | bytes 1474560 | tf_op jit(solution)/shard_map/reduce_scatter | solution.py:1142
  982.6 144.9 %collective-permute-start.22 = (bf16[8,192,1536]{2,1,0:T(8,128)(2,1)}, bf16[8,192,1536]{2,1,0:T(8,128)(2,1)}, u32[]{:S(2)}, u32[]{:S(2)}) collective-permute-start(bf16[8,192,1536]{2,1,0:T(8,128)(2,1)} %get-tuple-element.200), channel_id=1, source_target_pairs={{0,4},{4,0},{8,12},{12,8},{16,20},{20,16},{24,28},{28,24},{1,5},{5... | collective-permute-start | bytes 14155784 | tf_op jit(solution)/shard_map/ppermute | solution.py:660
  991.0 197.1 %collective-permute-start.23 = (bf16[8,192,1536]{2,1,0:T(8,128)(2,1)}, bf16[8,192,1536]{2,1,0:T(8,128)(2,1)}, u32[]{:S(2)}, u32[]{:S(2)}) collective-permute-start(bf16[8,192,1536]{2,1,0:T(8,128)(2,1)} %get-tuple-element.202), channel_id=1, source_target_pairs={{0,4},{4,0},{8,12},{12,8},{16,20},{20,16},{24,28},{28,24},{1,5},{5... | collective-permute-start | bytes 14155784 | tf_op jit(solution)/shard_map/ppermute | solution.py:660
  1091.1 36.5 %collective-permute-start.19 = (bf16[512,1536]{1,0:T(8,128)(2,1)}, bf16[512,1536]{1,0:T(8,128)(2,1)}, u32[]{:S(2)}, u32[]{:S(2)}) collective-permute-start(bf16[512,1536]{1,0:T(8,128)(2,1)} %multiply_convert_fusion), channel_id=1, source_target_pairs={{0,2},{1,3},{2,0},{3,1},{4,6},{5,7},{6,4},{7,5},{8,10},{9,11},{10,... | collective-permute-start | bytes 4718600 | tf_op jit(solution)/shard_map/ppermute | solution.py:660
  1092.5 102.9 %collective-permute-start.21 = (bf16[512,1536]{1,0:T(8,128)(2,1)}, bf16[512,1536]{1,0:T(8,128)(2,1)}, u32[]{:S(2)}, u32[]{:S(2)}) collective-permute-start(bf16[512,1536]{1,0:T(8,128)(2,1)} %multiply_convert_fusion), channel_id=1, source_target_pairs={{0,1},{1,0},{2,3},{3,2},{4,5},{5,4},{6,7},{7,6},{8,9},{9,8},{10,11... | collective-permute-start | bytes 4718600 | tf_op jit(solution)/shard_map/ppermute | solution.py:660
  1092.6 43.0 %collective-permute-start.24 = (bf16[1,512]{1,0:T(2,128)(2,1)S(1)}, bf16[1,512]{1,0:T(2,128)(2,1)S(1)}, u32[]{:S(2)}, u32[]{:S(2)}) collective-permute-start(bf16[1,512]{1,0:T(2,128)(2,1)S(1)} %multiply_convert_fusion.6), channel_id=1, source_target_pairs={{0,2},{1,3},{2,0},{3,1},{4,6},{5,7},{6,4},{7,5},{8,10},{9,11},{10,... | collective-permute-start | bytes 3080 | tf_op jit(solution)/shard_map/ppermute | solution.py:660
  1127.5 68.0 %collective-permute-start.20 = (bf16[512,1536]{1,0:T(8,128)(2,1)}, bf16[512,1536]{1,0:T(8,128)(2,1)}, u32[]{:S(2)}, u32[]{:S(2)}) collective-permute-start(bf16[512,1536]{1,0:T(8,128)(2,1)} %collective-permute-done.19), channel_id=1, source_target_pairs={{0,1},{1,0},{2,3},{3,2},{4,5},{5,4},{6,7},{7,6},{8,9},{9,8},{10,11... | collective-permute-start | bytes 4718600 | tf_op jit(solution)/shard_map/ppermute | solution.py:660
  1135.1 58.9 %collective-permute-start.26 = (bf16[1,512]{1,0:T(2,128)(2,1)S(1)}, bf16[1,512]{1,0:T(2,128)(2,1)S(1)}, u32[]{:S(2)}, u32[]{:S(2)}) collective-permute-start(bf16[1,512]{1,0:T(2,128)(2,1)S(1)} %multiply_convert_fusion.6), channel_id=1, source_target_pairs={{0,1},{1,0},{2,3},{3,2},{4,5},{5,4},{6,7},{7,6},{8,9},{9,8},{10,11... | collective-permute-start | bytes 3080 | tf_op jit(solution)/shard_map/ppermute | solution.py:660
  1135.6 58.5 %collective-permute-start.25 = (bf16[1,512]{1,0:T(2,128)(2,1)S(1)}, bf16[1,512]{1,0:T(2,128)(2,1)S(1)}, u32[]{:S(2)}, u32[]{:S(2)}) collective-permute-start(bf16[1,512]{1,0:T(2,128)(2,1)S(1)} %collective-permute-done.24), channel_id=1, source_target_pairs={{0,1},{1,0},{2,3},{3,2},{4,5},{5,4},{6,7},{7,6},{8,9},{9,8},{10,11... | collective-permute-start | bytes 3080 | tf_op jit(solution)/shard_map/ppermute | solution.py:660
  1194.0 254.8 %all-gather.16.cloned.1.call-start = ((), (), s32[]{:S(2)}) async-start(), calls=%async_computation.10 | async-start | bytes 1769472 | tf_op jit(solution)/shard_map/all_gather | solution.py:1212
  1220.7 741.6 %all-gather.12.cloned.1.call-start = ((), (), s32[]{:S(2)}) async-start(), calls=%async_computation.8 | async-start | bytes 9732096 | tf_op jit(solution)/shard_map/all_gather | solution.py:1145
  1221.9 780.5 %reduce-scatter.6.cloned.1.call-start = ((), (), s32[]{:S(2)}) async-start(), calls=%async_computation.6 | async-start | bytes 14155776 | tf_op jit(solution)/shard_map/reduce_scatter | solution.py:1227
  1221.9 120.7 %collective-permute-start.28 = (bf16[8,192,1536]{2,1,0:T(8,128)(2,1)}, bf16[8,192,1536]{2,1,0:T(8,128)(2,1)S(1)}, u32[]{:S(2)}, u32[]{:S(2)}) collective-permute-start(bf16[8,192,1536]{2,1,0:T(8,128)(2,1)} %get-tuple-element.214), channel_id=1, source_target_pairs={{0,4},{4,0},{8,12},{12,8},{16,20},{20,16},{24,28},{28,24},{1,5},{5... | collective-permute-start | bytes 14155784 | tf_op jit(solution)/shard_map/ppermute | solution.py:660
  1223.4 166.1 %collective-permute-start.27 = (bf16[8,192,1536]{2,1,0:T(8,128)(2,1)}, bf16[8,192,1536]{2,1,0:T(8,128)(2,1)S(1)}, u32[]{:S(2)}, u32[]{:S(2)}) collective-permute-start(bf16[8,192,1536]{2,1,0:T(8,128)(2,1)} %add_convert_fusion.4), channel_id=1, source_target_pairs={{0,8},{4,12},{8,0},{12,4},{16,24},{20,28},{24,16},{28,20},{1,9},{5... | collective-permute-start | bytes 14155784 | tf_op jit(solution)/shard_map/ppermute | solution.py:660
  1393.1 207.6 %collective-permute-start.31 = (bf16[8,192,1536]{2,1,0:T(8,128)(2,1)}, bf16[8,192,1536]{2,1,0:T(8,128)(2,1)}, u32[]{:S(2)}, u32[]{:S(2)}) collective-permute-start(bf16[8,192,1536]{2,1,0:T(8,128)(2,1)} %get-tuple-element.229), channel_id=1, source_target_pairs={{0,4},{4,0},{8,12},{12,8},{16,20},{20,16},{24,28},{28,24},{1,5},{5... | collective-permute-start | bytes 14155784 | tf_op jit(solution)/shard_map/ppermute | solution.py:660
  1394.3 206.4 %collective-permute-start.32 = (bf16[8,192,1536]{2,1,0:T(8,128)(2,1)}, bf16[8,192,1536]{2,1,0:T(8,128)(2,1)}, u32[]{:S(2)}, u32[]{:S(2)}) collective-permute-start(bf16[8,192,1536]{2,1,0:T(8,128)(2,1)} %add_convert_fusion.2), channel_id=1, source_target_pairs={{0,8},{4,12},{8,0},{12,4},{16,24},{20,28},{24,16},{28,20},{1,9},{5... | collective-permute-start | bytes 14155784 | tf_op jit(solution)/shard_map/ppermute | solution.py:660
  1406.5 137.0 %collective-permute-start.29 = (bf16[4,192,1536]{2,1,0:T(8,128)(2,1)}, bf16[4,192,1536]{2,1,0:T(8,128)(2,1)}, u32[]{:S(2)}, u32[]{:S(2)}) collective-permute-start(bf16[4,192,1536]{2,1,0:T(8,128)(2,1)} %dynamic-slice_bitcast_fusion), channel_id=1, source_target_pairs={{0,4},{4,0},{8,12},{12,8},{16,20},{20,16},{24,28},{28,24},{1,5},{5... | collective-permute-start | bytes 7077896 | tf_op jit(solution)/shard_map/ppermute | solution.py:660
  1435.1 165.6 %collective-permute-start.30 = (bf16[4,192,1536]{2,1,0:T(8,128)(2,1)}, bf16[4,192,1536]{2,1,0:T(8,128)(2,1)}, u32[]{:S(2)}, u32[]{:S(2)}) collective-permute-start(bf16[4,192,1536]{2,1,0:T(8,128)(2,1)} %slice.427), channel_id=1, source_target_pairs={{0,16},{4,20},{8,24},{12,28},{16,0},{20,4},{24,8},{28,12},{1,17},{... | collective-permute-start | bytes 7077896 | tf_op jit(solution)/shard_map/ppermute | solution.py:660
  1616.7 167.7 %collective-permute-start.34 = (bf16[4,192,1536]{2,1,0:T(8,128)(2,1)S(1)}, bf16[4,192,1536]{2,1,0:T(8,128)(2,1)}, u32[]{:S(2)}, u32[]{:S(2)}) collective-permute-start(bf16[4,192,1536]{2,1,0:T(8,128)(2,1)S(1)} %slice.442), channel_id=1, source_target_pairs={{0,16},{4,20},{8,24},{12,28},{16,0},{20,4},{24,8},{28,12},{1,17},{... | collective-permute-start | bytes 7077896 | tf_op jit(solution)/shard_map/ppermute | solution.py:660
  1633.8 38.8 %collective-permute-start.33 = (bf16[4,192,1152]{2,1,0:T(8,128)(2,1)}, bf16[4,192,1152]{2,1,0:T(8,128)(2,1)}, u32[]{:S(2)}, u32[]{:S(2)}) collective-permute-start(bf16[4,192,1152]{2,1,0:T(8,128)(2,1)} %dynamic-slice_bitcast_fusion.1), channel_id=1, source_target_pairs={{0,4},{4,0},{8,12},{12,8},{16,20},{20,16},{24,28},{28,24},{1,5},{5... | collective-permute-start | bytes 5308424 | tf_op jit(solution)/shard_map/ppermute | solution.py:660
  1635.6 236.6 %collective-permute-start.35 = (f32[8,1536]{1,0:T(8,128)S(1)}, f32[8,1536]{1,0:T(8,128)S(1)}, u32[]{:S(2)}, u32[]{:S(2)}) collective-permute-start(f32[8,1536]{1,0:T(8,128)S(1)} %fusion.107), channel_id=1, source_target_pairs={{4,0},{8,4},{12,8},{16,12},{20,16},{24,20},{28,24},{5,1},{9,5},{13... | collective-permute-start | bytes 147464 | tf_op jit(solution)/shard_map/ppermute | solution.py:1406
  1785.4 62.3 %collective-permute-start.46 = (bf16[2,192,1152]{2,1,0:T(8,128)(2,1)}, bf16[2,192,1152]{2,1,0:T(8,128)(2,1)}, u32[]{:S(2)}, u32[]{:S(2)}) collective-permute-start(bf16[2,192,1152]{2,1,0:T(8,128)(2,1)} %dynamic-slice_bitcast_fusion.7), channel_id=1, source_target_pairs={{0,8},{4,12},{8,0},{12,4},{16,24},{20,28},{24,16},{28,20},{1,9},{5... | collective-permute-start | bytes 2654216 | tf_op jit(solution)/shard_map/ppermute | solution.py:660
  1786.5 105.3 %collective-permute-start.44 = (bf16[2,192,1536]{2,1,0:T(8,128)(2,1)}, bf16[2,192,1536]{2,1,0:T(8,128)(2,1)}, u32[]{:S(2)}, u32[]{:S(2)}) collective-permute-start(bf16[2,192,1536]{2,1,0:T(8,128)(2,1)} %dynamic-slice_bitcast_fusion.6), channel_id=1, source_target_pairs={{0,8},{4,12},{8,0},{12,4},{16,24},{20,28},{24,16},{28,20},{1,9},{5... | collective-permute-start | bytes 3538952 | tf_op jit(solution)/shard_map/ppermute | solution.py:660
  1826.0 19.6 collective-permute-start.40
  1849.1 21.1 %collective-permute-start.47 = (bf16[1,192,1152]{2,1,0:T(8,128)(2,1)S(1)}, bf16[1,192,1152]{2,1,0:T(8,128)(2,1)S(1)}, u32[]{:S(2)}, u32[]{:S(2)}) collective-permute-start(bf16[1,192,1152]{2,1,0:T(8,128)(2,1)S(1)} %dynamic-slice_bitcast_fusion.8), channel_id=1, source_target_pairs={{0,16},{4,20},{8,24},{12,28},{16,0},{20,4},{24,8},{28,12},{1,17},{... | collective-permute-start | bytes 1327112 | tf_op jit(solution)/shard_map/ppermute | solution.py:660
  1879.5 78.0 %collective-permute-start.36 = (bf16[512,1536]{1,0:T(8,128)(2,1)}, bf16[512,1536]{1,0:T(8,128)(2,1)}, u32[]{:S(2)}, u32[]{:S(2)}) collective-permute-start(bf16[512,1536]{1,0:T(8,128)(2,1)} %get-tuple-element.418), channel_id=1, source_target_pairs={{0,1},{1,0},{2,3},{3,2},{4,5},{5,4},{6,7},{7,6},{8,9},{9,8},{10,11... | collective-permute-start | bytes 4718600 | tf_op jit(solution)/shard_map/ppermute | solution.py:660
  1879.5 35.3 %collective-permute-start.37 = (bf16[512,1536]{1,0:T(8,128)(2,1)}, bf16[512,1536]{1,0:T(8,128)(2,1)}, u32[]{:S(2)}, u32[]{:S(2)}) collective-permute-start(bf16[512,1536]{1,0:T(8,128)(2,1)} %get-tuple-element.419), channel_id=1, source_target_pairs={{0,1},{1,0},{2,3},{3,2},{4,5},{5,4},{6,7},{7,6},{8,9},{9,8},{10,11... | collective-permute-start | bytes 4718600 | tf_op jit(solution)/shard_map/ppermute | solution.py:660
  1902.7 34.0 %collective-permute-start.45 = (bf16[1,192,1536]{2,1,0:T(8,128)(2,1)}, bf16[1,192,1536]{2,1,0:T(8,128)(2,1)}, u32[]{:S(2)}, u32[]{:S(2)}) collective-permute-start(bf16[1,192,1536]{2,1,0:T(8,128)(2,1)} %constant_dynamic-slice_fusion.1), channel_id=1, source_target_pairs={{0,16},{4,20},{8,24},{12,28},{16,0},{20,4},{24,8},{28,12},{1,17},{... | collective-permute-start | bytes 1769480 | tf_op jit(solution)/shard_map/ppermute | solution.py:660
  1918.2 39.3 %collective-permute-start.38 = (bf16[512,1536]{1,0:T(8,128)(2,1)}, bf16[512,1536]{1,0:T(8,128)(2,1)}, u32[]{:S(2)}, u32[]{:S(2)}) collective-permute-start(bf16[512,1536]{1,0:T(8,128)(2,1)} %fusion.24), channel_id=1, source_target_pairs={{0,2},{1,3},{2,0},{3,1},{4,6},{5,7},{6,4},{7,5},{8,10},{9,11},{10,... | collective-permute-start | bytes 4718600 | tf_op jit(solution)/shard_map/ppermute | solution.py:660
  (125 other events, 4362.7 us)
Sparse Core Ops, SparseCore 0:
  10.8 237.0 all-gather.7
  383.4 94.1 all-gather.13
  694.5 125.2 all-gather.9
  939.6 142.5 reduce-scatter.3
  1194.1 27.6 reduce-scatter.7
  1223.9 58.0 all-gather.15
  1284.9 105.8 all-gather.11
  1546.6 235.0 reduce-scatter.5

commit v3 on v2

--- a/solution.py
+++ b/solution.py
@@ -1220,9 +1220,7 @@
     far_back = [swap(third_sum[:middle], SEQ, far_z)]
     low_sent = swap(known[1], SEQ, 1)
     sent, sent_left = scatter_step(sent, small_first[0], None)
-    grad_y, state_grad, out_part, sent = lax.optimization_barrier(
-        (grad_y, state_grad, out_part, sent)
-    )
+    grad_y, state_grad, out_part = lax.optimization_barrier((grad_y, state_grad, out_part))
     near_sent = swap(fourth_sum, SEQ, low_z)
     routed = lax.psum_scatter(out_part, GROUP, scatter_dimension=0, tiled=True).astype(F32)
     passed = jnp.concatenate([jnp.ones((1, LANES), F32), reach[SPAN - 1 : length - 1 : SPAN]])
@@ -1320,6 +1318,7 @@
         third_sum,
         low_sent,
         near_sent,
+        sent,
     ) = lax.optimization_barrier(
         (
             grad_x,
@@ -1333,6 +1332,7 @@
             third_sum,
             low_sent,
             near_sent,
+            sent,
         )
     )
     if middle < experts_half:
@@ -1360,10 +1360,9 @@
         ],
         axis=1,
     ).astype(BF16)
+    grad_late, far_back = lax.optimization_barrier((grad_late, far_back))
     late_sum, late_left = scatter_step(grad_late, small_first[0], None)
-    grad_x, late_sum, sent, far_back = lax.optimization_barrier(
-        (grad_x, late_sum, sent, far_back)
-    )
+    grad_x, late_sum = lax.optimization_barrier((grad_x, late_sum))
     for stride in small_first[1:]:
         sent, sent_left = scatter_step(sent, stride, sent_left)
     sent = sent.astype(F32)

time: 2030 us -> 2010 us (level)
  waiting for transfers between devices: 1140 us -> 1100 us
    ppermute x59, waiting for transfers between devices: 775 us -> 737 us  [swap(): lax.ppermute(block, axis, [(i, i ^ stride) for i in range(lax.axis_size(a...]
  transfers between devices with their start and end apart: 69 -> 69, of which waited for: 32 -> 33; matrix products, arithmetic and copies ran while one was open for 20% -> 21% of each run, Pallas kernels for 10% -> 10%
where the time goes in v3:
time: 2010 us; the launch traced here: 1990 us
  waiting for transfers between devices  1100 us (55%)
  Pallas kernels  324 us (16%)
  other arithmetic  181 us (9%)
  local copies, waits for them, and re-layouts  145 us (7%)
  matrix products  139 us (7%)
  starting transfers between devices  88.8 us (4%)
    ppermute x59, waiting for transfers between devices, swap(): lax.ppermute(block, axis, [(i, i ^ stride) for i in range(lax.axis_size(a...  737 us
    all_gather x1, waiting for transfers between devices, per_device(): lax.all_gather(jnp.concatenate([proj_x, pad_dt, proj_z, proj_out.T], axis...  106 us
    ppermute x1, waiting for transfers between devices, per_device(): lax.ppermute(tokens[length - 8:], SEQ, [(i, i + 1) for i in range(seq_cou...  90.7 us
    ppermute x59, starting transfers between devices, swap(): lax.ppermute(block, axis, [(i, i ^ stride) for i in range(lax.axis_size(a...  84.6 us
    reduce_scatter x1, waiting for transfers between devices, per_device(): lax.psum_scatter(row_part, GROUP, scatter_dimension=0, tiled=True)  82.4 us
    all_gather x1, waiting for transfers between devices, gather_states(): gathered = lax.all_gather(packed, SEQ, axis=0).astype(F32)  75 us
    pallas_call x1, Pallas kernels, run_experts(): pl.pallas_call(partial(expert_kernel, len(pieces)), grid_spec=pltpu.Prefe...  71.8 us
    dot_general x7, matrix products, dot_nt(): lax.dot_general(left, right, (((1,), (1,)), ((), ())), preferred_element_...  57.6 us
  transfers between devices with their start and end apart: 69, of which 33 were waited for; matrix products, arithmetic and copies ran while one was open for 21% of the time, Pallas kernels for 10%

profile of v3, /device:TPU:0, one launch (start us, length us, event | category | flops | bytes accessed | tf_op | source)
XLA Modules:
  0.0 1993.0 jit_solution(13064877459683191090)
XLA Ops:
  50.1 90.7 %collective-permute-done.3 = bf16[8,1536]{1,0:T(8,128)(2,1)S(1)} collective-permute-done((bf16[8,1536]{1,0:T(8,128)(2,1)S(1)}, bf16[8,1536]{1,0:T(8,128)(2,1)S(1)}, u32[]{:S(2)}, u32[]{:S(2)}) %collective-permute-start.3) | collective-permute-done | bytes 24608 | tf_op jit(solution)/shard_map/ppermute | solution.py:816
  141.4 106.5 %all-gather.8.cloned.1.call-done = bf16[1536,2432]{1,0:T(8,128)(2,1)} async-done(((bf16[192,2432]{1,0:T(8,128)(2,1)}), bf16[1536,2432]{1,0:T(8,128)(2,1)}) %all-gather.8.cloned.1.call-update) | async-done | bytes 7471120 | tf_op jit(solution)/shard_map/all_gather | solution.py:810
  247.9 9.8 fusion.48.raw_x.raw_x_before
  257.7 7.0 collective-permute-done.2
  268.1 11.7 collective-permute-start.5
  290.3 24.4 %scan_forward.1 = (f32[2048,1024]{1,0:T(8,128)}, bf16[2048,768]{1,0:T(8,128)(2,1)}, bf16[2048,256]{1,0:T(8,128)(2,1)}, f32[2048,768]{1,0:T(8,128)}, f32[2048,128...) custom-call(f32[2048,768]{1,0:T(8,128)} %fusion.48.raw_x.raw_x_before, f32[2048,384]{1,0:T(8,128)} %copy-done.8, ...), custom_call_target="tpu_custom_call" | custom-call | flops 3221225472 | bytes 37748736 | tf_op jit(solution)/shard_map/scan_forward/pallas_call | solution.py:923
  314.7 56.9 %collective-permute-done.4 = bf16[4,192,1536]{2,1,0:T(8,128)(2,1)} collective-permute-done((bf16[4,192,1536]{2,1,0:T(8,128)(2,1)}, bf16[4,192,1536]{2,1,0:T(8,128)(2,1)}, u32[]{:S(2)}, u32[]{:S(2)}) %collective-permute-start.4) | collective-permute-done | bytes 2359328 | tf_op jit(solution)/shard_map/ppermute | solution.py:660
  392.9 9.6 fusion.36.gate
  402.5 75.0 %all-gather.14.cloned.1.call-done = bf16[1152,768]{1,0:T(8,128)(2,1)} async-done(((bf16[144,768]{1,0:T(8,128)(2,1)}), bf16[1152,768]{1,0:T(8,128)(2,1)}) %all-gather.14.cloned.1.call-update) | async-done | bytes 1769488 | tf_op jit(solution)/shard_map/all_gather | solution.py:738
  481.0 55.8 %collective-permute-done.6 = bf16[512,1664]{1,0:T(8,128)(2,1)} collective-permute-done((bf16[512,1664]{1,0:T(8,128)(2,1)}, bf16[512,1664]{1,0:T(8,128)(2,1)}, u32[]{:S(2)}, u32[]{:S(2)}) %collective-permute-start.6) | collective-permute-done | bytes 1703968 | tf_op jit(solution)/shard_map/ppermute | solution.py:660
  539.1 17.7 gate_forward.1
  572.6 31.9 %collective-permute-done.11 = f32[1,512]{1,0:T(1,128)S(1)} collective-permute-done((f32[1,512]{1,0:T(1,128)S(1)}, f32[1,512]{1,0:T(1,128)S(1)}, u32[]{:S(2)}, u32[]{:S(2)}) %collective-permute-start.11) | collective-permute-done | bytes 2080 | tf_op jit(solution)/shard_map/ppermute | solution.py:660
  623.0 67.4 %collective-permute-done.15 = bf16[1024,1664]{1,0:T(8,128)(2,1)} collective-permute-done((bf16[1024,1664]{1,0:T(8,128)(2,1)}, bf16[1024,1664]{1,0:T(8,128)(2,1)}, u32[]{:S(2)}, u32[]{:S(2)}) %collective-permute-start.15) | collective-permute-done | bytes 3407904 | tf_op jit(solution)/shard_map/ppermute | solution.py:660
  748.5 17.9 dispatch.2.grad_got
  766.4 45.8 %collective-permute-done.18.refs_7_ = bf16[8,192,1536]{2,1,0:T(8,128)(2,1)} collective-permute-done((bf16[8,192,1536]{2,1,0:T(8,128)(2,1)}, bf16[8,192,1536]{2,1,0:T(8,128)(2,1)}, u32[]{:S(2)}, u32[]{:S(2)}) %collective-permute-start.18) | collective-permute-done | bytes 4718624 | tf_op jit(solution)/shard_map/ppermute | solution.py:660
  812.2 7.5 all-gather.10.cloned.1.call-done.refs_0_
  826.2 17.0 dispatch.3.got
  847.6 71.8 %experts.1 = (bf16[8,768,512]{2,1,0:T(8,128)(2,1)}, bf16[8,768,1024]{2,1,0:T(8,128)(2,1)}, bf16[8,8,96,1536]{3,2,1,0:T(8,128)(2,1)}, bf16[8,8,96,1536]{3,2,1,0:T(8,128)(2,1)}) custom-call(s32[1]{0:T(128)} %bitcast.36.me, bf16[8,8,96,1536]{3,2,1,0:T(8,128)(2,1)} %dispatch.3.got, bf16[8,8,96,1536]{3,2,1,0:T(8,128)(2,1)} %dispatch.2.grad_got, ...), custom_call_target="tpu_custom_call" | custom-call | flops 57982058496 | bytes 113246208 | tf_op jit(solution)/shard_map/experts/pallas_call | solution.py:503
  919.4 20.1 %combine.2 = bf16[4096,1536]{1,0:T(8,128)(2,1)} custom-call(bf16[8,8,96,1536]{3,2,1,0:T(8,128)(2,1)} %get-tuple-element.191.refs_0_, bf16[8,512,8]{2,1,0:T(8,128)(2,1)} %get-tuple-element.431.refs_1_, bf16[8,768]{1,0:T(8,128)(2,1)} %fusion.119.refs_2_, f32[1,768]{1,0:T(1,128)} %fusion.143.refs_3_, bf16[4096,256]{1,0:T(8,128)(2,1)} %pad_maximum_fusion.8.refs_4_, ...), custom_call_target="tpu_custom_call" | custom-call | flops 12884901888 | bytes 31457280 | tf_op jit(solution)/shard_map/combine/pallas_call | solution.py:644
  939.6 43.0 %expert_grads.1 = (bf16[8,192,1536]{2,1,0:T(8,128)(2,1)}, bf16[8,192,1536]{2,1,0:T(8,128)(2,1)}, bf16[8,192,1536]{2,1,0:T(8,128)(2,1)}, bf16[8,192,1536]{2,1,0:T...) custom-call(s32[1]{0:T(128)} %bitcast.36.me, ...), custom_call_target="tpu_custom_call" | custom-call | flops 28991029248 | bytes 75497472 | tf_op jit(solution)/shard_map/expert_grads/pallas_call | solution.py:555
  984.3 6.7 convolution_convert_fusion.2
  991.7 7.0 fusion.29
  999.8 82.4 %reduce-scatter.4.cloned.1.call-done = bf16[512,1536]{1,0:T(8,128)(2,1)} async-done(((bf16[4096,1536]{1,0:T(8,128)(2,1)}), bf16[512,1536]{1,0:T(8,128)(2,1)}) %reduce-scatter.4.cloned.1.call-update) | async-done | bytes 1572880 | tf_op jit(solution)/shard_map/reduce_scatter | solution.py:1107
  1093.3 34.4 %collective-permute-done.19 = bf16[512,1536]{1,0:T(8,128)(2,1)} collective-permute-done((bf16[512,1536]{1,0:T(8,128)(2,1)}, bf16[512,1536]{1,0:T(8,128)(2,1)}, u32[]{:S(2)}, u32[]{:S(2)}) %collective-permute-start.19) | collective-permute-done | bytes 1572896 | tf_op jit(solution)/shard_map/ppermute | solution.py:660
  1127.7 7.5 add_convert_fusion.5
  1135.7 52.4 %collective-permute-done.23 = bf16[8,192,1536]{2,1,0:T(8,128)(2,1)} collective-permute-done((bf16[8,192,1536]{2,1,0:T(8,128)(2,1)}, bf16[8,192,1536]{2,1,0:T(8,128)(2,1)}, u32[]{:S(2)}, u32[]{:S(2)}) %collective-permute-start.23) | collective-permute-done | bytes 4718624 | tf_op jit(solution)/shard_map/ppermute | solution.py:660
  1201.3 17.8 gate_backward.1
  1224.2 118.6 %collective-permute-done.28 = bf16[8,192,1536]{2,1,0:T(8,128)(2,1)S(1)} collective-permute-done((bf16[8,192,1536]{2,1,0:T(8,128)(2,1)}, bf16[8,192,1536]{2,1,0:T(8,128)(2,1)S(1)}, u32[]{:S(2)}, u32[]{:S(2)}) %collective-permute-start.28) | collective-permute-done | bytes 4718624 | tf_op jit(solution)/shard_map/ppermute | solution.py:660
  1348.8 10.1 convolution_convert_fusion
  1367.3 22.3 %collective-permute-done.27 = bf16[8,192,1536]{2,1,0:T(8,128)(2,1)S(1)} collective-permute-done((bf16[8,192,1536]{2,1,0:T(8,128)(2,1)}, bf16[8,192,1536]{2,1,0:T(8,128)(2,1)S(1)}, u32[]{:S(2)}, u32[]{:S(2)}) %collective-permute-start.27) | collective-permute-done | bytes 4718624 | tf_op jit(solution)/shard_map/ppermute | solution.py:660
  1400.5 6.6 copy.174
  1411.2 20.7 %combine.3 = bf16[4096,1536]{1,0:T(8,128)(2,1)} custom-call(bf16[8,8,96,1536]{3,2,1,0:T(8,128)(2,1)} %get-tuple-element.208.refs_0_, bf16[8,512,8]{2,1,0:T(8,128)(2,1)} %get-tuple-element.431.refs_1_, bf16[8,768]{1,0:T(8,128)(2,1)} %fusion.119.refs_2_, f32[1,768]{1,0:T(1,128)} %fusion.143.refs_3_, bf16[8,512,8]{2,1,0:T(8,128)(2,1)} %bitcast.307, ...), custom_call_target="tpu_custom_call" | custom-call | flops 11274289152 | bytes 31457280 | tf_op jit(solution)/shard_map/combine/pallas_call | solution.py:644
  1438.9 9.8 fusion.34
  1452.2 53.3 %scan_backward.1 = (bf16[2048,768]{1,0:T(8,128)(2,1)}, bf16[2048,256]{1,0:T(8,128)(2,1)}, f32[2048,128]{1,0:T(8,128)}, f32[8,1024]{1,0:T(8,128)}, f32[8,1024]{1,...) custom-call(f32[2048,1024]{1,0:T(8,128)} %get-tuple-element.211.conv, f32[2048,768]{1,0:T(8,128)} %fusion.48.raw_x.raw_x_before, ...), custom_call_target="tpu_custom_call" | custom-call | flops 8053063680 | bytes 67108864 | tf_op jit(solution)/shard_map/scan_backward/pallas_call | solution.py:1233
  1505.5 38.0 %collective-permute-done.32 = bf16[4,192,1536]{2,1,0:T(8,128)(2,1)} collective-permute-done((bf16[4,192,1536]{2,1,0:T(8,128)(2,1)}, bf16[4,192,1536]{2,1,0:T(8,128)(2,1)}, u32[]{:S(2)}, u32[]{:S(2)}) %collective-permute-start.32) | collective-permute-done | bytes 2359328 | tf_op jit(solution)/shard_map/ppermute | solution.py:660
  1546.6 21.5 %collective-permute-done.29 = bf16[4,192,1536]{2,1,0:T(8,128)(2,1)} collective-permute-done((bf16[4,192,1536]{2,1,0:T(8,128)(2,1)}, bf16[4,192,1536]{2,1,0:T(8,128)(2,1)}, u32[]{:S(2)}, u32[]{:S(2)}) %collective-permute-start.29) | collective-permute-done | bytes 2359328 | tf_op jit(solution)/shard_map/ppermute | solution.py:660
  1584.5 6.7 collective-permute-start.44
  1607.2 135.1 %collective-permute-done.33 = bf16[4,192,1536]{2,1,0:T(8,128)(2,1)} collective-permute-done((bf16[4,192,1536]{2,1,0:T(8,128)(2,1)S(1)}, bf16[4,192,1536]{2,1,0:T(8,128)(2,1)}, u32[]{:S(2)}, u32[]{:S(2)}) %collective-permute-start.33) | collective-permute-done | bytes 2359328 | tf_op jit(solution)/shard_map/ppermute | solution.py:660
  1751.5 9.3 add_convert_fusion.refs_0_
  1760.8 7.2 fusion.91
  1776.4 19.8 owner_grads.1
  1802.2 9.5 fusion.44
  1811.7 21.6 %fusion.9 = (f32[1536]{0:T(1024)S(1)}, f32[2048]{0:T(1024)S(1)}, f32[2048,1536]{1,0:T(8,128)}) fusion(bf16[2048,1536]{1,0:T(8,128)(2,1)} %param.26, f32[2048]{0:T(1024)S(1)} %copy-done.39, f32[1536]{0:T(1024)S(1)} %copy-done.33, bf16[2048,256]{1,0:T(8,128)(2,1)} %get-tuple-element.234, bf16[1536,256]{1,0:T(8,128)(2,1)S(1)} %copy-done.16, ...), kind=kOutput, calls=%fused_computation.11 | convolution fusion | flops 1642066432 | bytes 58486784 | tf_op jit(solution)/shard_map/dot_general | solution.py:30
  1836.2 10.6 fusion.8
  1879.5 8.5 copy.180
  1916.5 16.6 collective-permute-done.52
  1941.9 8.4 copy.176
  1959.5 6.6 copy.178
  (604 shorter events, 420.2 us)
Async XLA Ops:
  7.2 240.7 %all-gather.8.cloned.1.call-start = ((), (), s32[]{:S(2)}) async-start(), calls=%async_computation.3 | async-start | bytes 8404992 | tf_op jit(solution)/shard_map/all_gather | solution.py:810
  10.4 467.1 %all-gather.14.cloned.1.call-start = ((), (), s32[]{:S(2)}) async-start(), calls=%async_computation.9 | async-start | bytes 1990656 | tf_op jit(solution)/shard_map/all_gather | solution.py:738
  20.9 245.8 %collective-permute-start.1 = (bf16[8,192,1536]{2,1,0:T(8,128)(2,1)}, bf16[8,192,1536]{2,1,0:T(8,128)(2,1)}, u32[]{:S(2)}, u32[]{:S(2)}) collective-permute-start(bf16[8,192,1536]{2,1,0:T(8,128)(2,1)} %constant_dynamic-slice_fusion.19.refs_0_), channel_id=1, source_target_pairs={{0,8},{4,12},{8,0},{12,4},{16,24},{20,28},{24,16},{28,20},{1,9},{5... | collective-permute-start | bytes 14155784 | tf_op jit(solution)/shard_map/ppermute | solution.py:660
  24.0 242.7 %collective-permute-start = (bf16[8,192,1536]{2,1,0:T(8,128)(2,1)}, bf16[8,192,1536]{2,1,0:T(8,128)(2,1)}, u32[]{:S(2)}, u32[]{:S(2)}) collective-permute-start(bf16[8,192,1536]{2,1,0:T(8,128)(2,1)} %constant_dynamic-slice_fusion.19.refs_0_), channel_id=1, source_target_pairs={{0,4},{4,0},{8,12},{12,8},{16,20},{20,16},{24,28},{28,24},{1,5},{5... | collective-permute-start | bytes 14155784 | tf_op jit(solution)/shard_map/ppermute | solution.py:660
  26.3 114.4 %collective-permute-start.3 = (bf16[8,1536]{1,0:T(8,128)(2,1)S(1)}, bf16[8,1536]{1,0:T(8,128)(2,1)S(1)}, u32[]{:S(2)}, u32[]{:S(2)}) collective-permute-start(bf16[8,1536]{1,0:T(8,128)(2,1)S(1)} %slice.374), channel_id=1, source_target_pairs={{0,4},{4,8},{8,12},{12,16},{16,20},{20,24},{24,28},{1,5},{5,9},{9,... | collective-permute-start | bytes 73736 | tf_op jit(solution)/shard_map/ppermute | solution.py:816
  33.7 231.0 %collective-permute-start.2 = (bf16[4,192,1536]{2,1,0:T(8,128)(2,1)}, bf16[4,192,1536]{2,1,0:T(8,128)(2,1)}, u32[]{:S(2)}, u32[]{:S(2)}) collective-permute-start(bf16[4,192,1536]{2,1,0:T(8,128)(2,1)} %get-tuple-element.417), channel_id=1, source_target_pairs={{0,16},{4,20},{8,24},{12,28},{16,0},{20,4},{24,8},{28,12},{1,17},{... | collective-permute-start | bytes 7077896 | tf_op jit(solution)/shard_map/ppermute | solution.py:660
  266.7 104.8 %collective-permute-start.4 = (bf16[4,192,1536]{2,1,0:T(8,128)(2,1)}, bf16[4,192,1536]{2,1,0:T(8,128)(2,1)}, u32[]{:S(2)}, u32[]{:S(2)}) collective-permute-start(bf16[4,192,1536]{2,1,0:T(8,128)(2,1)} %get-tuple-element.151), channel_id=1, source_target_pairs={{0,16},{4,20},{8,24},{12,28},{16,0},{20,4},{24,8},{28,12},{1,17},{... | collective-permute-start | bytes 7077896 | tf_op jit(solution)/shard_map/ppermute | solution.py:660
  268.1 103.5 %collective-permute-start.5 = (bf16[4,192,1536]{2,1,0:T(8,128)(2,1)}, bf16[4,192,1536]{2,1,0:T(8,128)(2,1)}, u32[]{:S(2)}, u32[]{:S(2)}) collective-permute-start(bf16[4,192,1536]{2,1,0:T(8,128)(2,1)} %collective-permute-done.2), channel_id=1, source_target_pairs={{0,4},{4,0},{8,12},{12,8},{16,20},{20,16},{24,28},{28,24},{1,5},{5... | collective-permute-start | bytes 7077896 | tf_op jit(solution)/shard_map/ppermute | solution.py:660
  378.1 160.9 %collective-permute-start.7 = (bf16[8,192,1536]{2,1,0:T(8,128)(2,1)}, bf16[8,192,1536]{2,1,0:T(8,128)(2,1)}, u32[]{:S(2)}, u32[]{:S(2)}) collective-permute-start(bf16[8,192,1536]{2,1,0:T(8,128)(2,1)} %constant_dynamic-update-slice_fusion.refs_4_), channel_id=1, source_target_pairs={{0,8},{4,12},{8,0},{12,4},{16,24},{20,28},{24,16},{28,20},{1,9},{5... | collective-permute-start | bytes 14155784 | tf_op jit(solution)/shard_map/ppermute | solution.py:660
  378.1 160.9 %collective-permute-start.8 = (bf16[8,192,1536]{2,1,0:T(8,128)(2,1)}, bf16[8,192,1536]{2,1,0:T(8,128)(2,1)}, u32[]{:S(2)}, u32[]{:S(2)}) collective-permute-start(bf16[8,192,1536]{2,1,0:T(8,128)(2,1)} %collective-permute-done.1.refs_2_), channel_id=1, source_target_pairs={{0,4},{4,0},{8,12},{12,8},{16,20},{20,16},{24,28},{28,24},{1,5},{5... | collective-permute-start | bytes 14155784 | tf_op jit(solution)/shard_map/ppermute | solution.py:660
  383.2 436.6 %all-gather.10.cloned.1.call-start = ((), (), s32[]{:S(2)}) async-start(), calls=%async_computation.4 | async-start | bytes 14155776 | tf_op jit(solution)/shard_map/all_gather | solution.py:1039
  387.5 149.3 %collective-permute-start.6 = (bf16[512,1664]{1,0:T(8,128)(2,1)}, bf16[512,1664]{1,0:T(8,128)(2,1)}, u32[]{:S(2)}, u32[]{:S(2)}) collective-permute-start(bf16[512,1664]{1,0:T(8,128)(2,1)} %fusion.41), channel_id=1, source_target_pairs={{0,16},{4,20},{8,24},{12,28},{16,0},{20,4},{24,8},{28,12},{1,17},{... | collective-permute-start | bytes 5111816 | tf_op jit(solution)/shard_map/ppermute | solution.py:660
  560.5 44.0 %collective-permute-start.12 = (bf16[512,1536]{1,0:T(8,128)(2,1)}, bf16[512,1536]{1,0:T(8,128)(2,1)}, u32[]{:S(2)}, u32[]{:S(2)}) collective-permute-start(bf16[512,1536]{1,0:T(8,128)(2,1)} %get-tuple-element.426), channel_id=1, source_target_pairs={{0,1},{1,0},{2,3},{3,2},{4,5},{5,4},{6,7},{7,6},{8,9},{9,8},{10,11... | collective-permute-start | bytes 4718600 | tf_op jit(solution)/shard_map/ppermute | solution.py:660
  567.7 36.8 %collective-permute-start.14 = (bf16[512,1536]{1,0:T(8,128)(2,1)}, bf16[512,1536]{1,0:T(8,128)(2,1)}, u32[]{:S(2)}, u32[]{:S(2)}) collective-permute-start(bf16[512,1536]{1,0:T(8,128)(2,1)} %fusion.26), channel_id=1, source_target_pairs={{0,2},{1,3},{2,0},{3,1},{4,6},{5,7},{6,4},{7,5},{8,10},{9,11},{10,... | collective-permute-start | bytes 4718600 | tf_op jit(solution)/shard_map/ppermute | solution.py:660
  572.0 32.4 %collective-permute-start.11 = (f32[1,512]{1,0:T(1,128)S(1)}, f32[1,512]{1,0:T(1,128)S(1)}, u32[]{:S(2)}, u32[]{:S(2)}) collective-permute-start(f32[1,512]{1,0:T(1,128)S(1)} %fusion.155), channel_id=1, source_target_pairs={{0,2},{1,3},{2,0},{3,1},{4,6},{5,7},{6,4},{7,5},{8,10},{9,11},{10,... | collective-permute-start | bytes 6152 | tf_op jit(solution)/shard_map/ppermute | solution.py:660
  615.2 75.2 %collective-permute-start.15 = (bf16[1024,1664]{1,0:T(8,128)(2,1)}, bf16[1024,1664]{1,0:T(8,128)(2,1)}, u32[]{:S(2)}, u32[]{:S(2)}) collective-permute-start(bf16[1024,1664]{1,0:T(8,128)(2,1)} %pad_maximum_fusion.7), channel_id=1, source_target_pairs={{0,2},{1,3},{2,0},{3,1},{4,6},{5,7},{6,4},{7,5},{8,10},{9,11},{10,... | collective-permute-start | bytes 10223624 | tf_op jit(solution)/shard_map/ppermute | solution.py:660
  616.7 77.7 %collective-permute-start.16 = (bf16[4,192,1536]{2,1,0:T(8,128)(2,1)}, bf16[4,192,1536]{2,1,0:T(8,128)(2,1)}, u32[]{:S(2)}, u32[]{:S(2)}) collective-permute-start(bf16[4,192,1536]{2,1,0:T(8,128)(2,1)} %collective-permute-done.4), channel_id=1, source_target_pairs={{0,4},{4,0},{8,12},{12,8},{16,20},{20,16},{24,28},{28,24},{1,5},{5... | collective-permute-start | bytes 7077896 | tf_op jit(solution)/shard_map/ppermute | solution.py:660
  694.4 387.9 %reduce-scatter.4.cloned.1.call-start = ((), (), s32[]{:S(2)}) async-start(), calls=%async_computation.5 | async-start | bytes 14155776 | tf_op jit(solution)/shard_map/reduce_scatter | solution.py:1107
  705.0 107.2 %collective-permute-start.18 = (bf16[8,192,1536]{2,1,0:T(8,128)(2,1)}, bf16[8,192,1536]{2,1,0:T(8,128)(2,1)}, u32[]{:S(2)}, u32[]{:S(2)}) collective-permute-start(bf16[8,192,1536]{2,1,0:T(8,128)(2,1)} %collective-permute-done.7.refs_6_), channel_id=1, source_target_pairs={{0,4},{4,0},{8,12},{12,8},{16,20},{20,16},{24,28},{28,24},{1,5},{5... | collective-permute-start | bytes 14155784 | tf_op jit(solution)/shard_map/ppermute | solution.py:660
  939.5 282.4 %reduce-scatter.8.cloned.1.call-start = ((), (), s32[]{:S(2)}) async-start(), calls=%async_computation.7 | async-start | bytes 1474560 | tf_op jit(solution)/shard_map/reduce_scatter | solution.py:1142
  982.6 145.1 %collective-permute-start.22 = (bf16[8,192,1536]{2,1,0:T(8,128)(2,1)}, bf16[8,192,1536]{2,1,0:T(8,128)(2,1)}, u32[]{:S(2)}, u32[]{:S(2)}) collective-permute-start(bf16[8,192,1536]{2,1,0:T(8,128)(2,1)} %get-tuple-element.200), channel_id=1, source_target_pairs={{0,4},{4,0},{8,12},{12,8},{16,20},{20,16},{24,28},{28,24},{1,5},{5... | collective-permute-start | bytes 14155784 | tf_op jit(solution)/shard_map/ppermute | solution.py:660
  991.0 197.1 %collective-permute-start.23 = (bf16[8,192,1536]{2,1,0:T(8,128)(2,1)}, bf16[8,192,1536]{2,1,0:T(8,128)(2,1)}, u32[]{:S(2)}, u32[]{:S(2)}) collective-permute-start(bf16[8,192,1536]{2,1,0:T(8,128)(2,1)} %get-tuple-element.202), channel_id=1, source_target_pairs={{0,4},{4,0},{8,12},{12,8},{16,20},{20,16},{24,28},{28,24},{1,5},{5... | collective-permute-start | bytes 14155784 | tf_op jit(solution)/shard_map/ppermute | solution.py:660
  1091.2 36.5 %collective-permute-start.19 = (bf16[512,1536]{1,0:T(8,128)(2,1)}, bf16[512,1536]{1,0:T(8,128)(2,1)}, u32[]{:S(2)}, u32[]{:S(2)}) collective-permute-start(bf16[512,1536]{1,0:T(8,128)(2,1)} %multiply_convert_fusion), channel_id=1, source_target_pairs={{0,2},{1,3},{2,0},{3,1},{4,6},{5,7},{6,4},{7,5},{8,10},{9,11},{10,... | collective-permute-start | bytes 4718600 | tf_op jit(solution)/shard_map/ppermute | solution.py:660
  1092.6 103.0 %collective-permute-start.21 = (bf16[512,1536]{1,0:T(8,128)(2,1)}, bf16[512,1536]{1,0:T(8,128)(2,1)}, u32[]{:S(2)}, u32[]{:S(2)}) collective-permute-start(bf16[512,1536]{1,0:T(8,128)(2,1)} %multiply_convert_fusion), channel_id=1, source_target_pairs={{0,1},{1,0},{2,3},{3,2},{4,5},{5,4},{6,7},{7,6},{8,9},{9,8},{10,11... | collective-permute-start | bytes 4718600 | tf_op jit(solution)/shard_map/ppermute | solution.py:660
  1092.6 43.0 %collective-permute-start.24 = (bf16[1,512]{1,0:T(2,128)(2,1)S(1)}, bf16[1,512]{1,0:T(2,128)(2,1)S(1)}, u32[]{:S(2)}, u32[]{:S(2)}) collective-permute-start(bf16[1,512]{1,0:T(2,128)(2,1)S(1)} %multiply_convert_fusion.6), channel_id=1, source_target_pairs={{0,2},{1,3},{2,0},{3,1},{4,6},{5,7},{6,4},{7,5},{8,10},{9,11},{10,... | collective-permute-start | bytes 3080 | tf_op jit(solution)/shard_map/ppermute | solution.py:660
  1127.6 68.0 %collective-permute-start.20 = (bf16[512,1536]{1,0:T(8,128)(2,1)}, bf16[512,1536]{1,0:T(8,128)(2,1)}, u32[]{:S(2)}, u32[]{:S(2)}) collective-permute-start(bf16[512,1536]{1,0:T(8,128)(2,1)} %collective-permute-done.19), channel_id=1, source_target_pairs={{0,1},{1,0},{2,3},{3,2},{4,5},{5,4},{6,7},{7,6},{8,9},{9,8},{10,11... | collective-permute-start | bytes 4718600 | tf_op jit(solution)/shard_map/ppermute | solution.py:660
  1135.1 59.0 %collective-permute-start.26 = (bf16[1,512]{1,0:T(2,128)(2,1)S(1)}, bf16[1,512]{1,0:T(2,128)(2,1)S(1)}, u32[]{:S(2)}, u32[]{:S(2)}) collective-permute-start(bf16[1,512]{1,0:T(2,128)(2,1)S(1)} %multiply_convert_fusion.6), channel_id=1, source_target_pairs={{0,1},{1,0},{2,3},{3,2},{4,5},{5,4},{6,7},{7,6},{8,9},{9,8},{10,11... | collective-permute-start | bytes 3080 | tf_op jit(solution)/shard_map/ppermute | solution.py:660
  1135.6 58.6 %collective-permute-start.25 = (bf16[1,512]{1,0:T(2,128)(2,1)S(1)}, bf16[1,512]{1,0:T(2,128)(2,1)S(1)}, u32[]{:S(2)}, u32[]{:S(2)}) collective-permute-start(bf16[1,512]{1,0:T(2,128)(2,1)S(1)} %collective-permute-done.24), channel_id=1, source_target_pairs={{0,1},{1,0},{2,3},{3,2},{4,5},{5,4},{6,7},{7,6},{8,9},{9,8},{10,11... | collective-permute-start | bytes 3080 | tf_op jit(solution)/shard_map/ppermute | solution.py:660
  1194.1 254.7 %all-gather.16.cloned.1.call-start = ((), (), s32[]{:S(2)}) async-start(), calls=%async_computation.10 | async-start | bytes 1769472 | tf_op jit(solution)/shard_map/all_gather | solution.py:1212
  1220.9 721.1 %all-gather.12.cloned.1.call-start = ((), (), s32[]{:S(2)}) async-start(), calls=%async_computation.8 | async-start | bytes 9732096 | tf_op jit(solution)/shard_map/all_gather | solution.py:1145
  1222.0 760.0 %reduce-scatter.6.cloned.1.call-start = ((), (), s32[]{:S(2)}) async-start(), calls=%async_computation.6 | async-start | bytes 14155776 | tf_op jit(solution)/shard_map/reduce_scatter | solution.py:1225
  1222.0 120.7 %collective-permute-start.28 = (bf16[8,192,1536]{2,1,0:T(8,128)(2,1)}, bf16[8,192,1536]{2,1,0:T(8,128)(2,1)S(1)}, u32[]{:S(2)}, u32[]{:S(2)}) collective-permute-start(bf16[8,192,1536]{2,1,0:T(8,128)(2,1)} %get-tuple-element.225), channel_id=1, source_target_pairs={{0,4},{4,0},{8,12},{12,8},{16,20},{20,16},{24,28},{28,24},{1,5},{5... | collective-permute-start | bytes 14155784 | tf_op jit(solution)/shard_map/ppermute | solution.py:660
  1223.6 166.1 %collective-permute-start.27 = (bf16[8,192,1536]{2,1,0:T(8,128)(2,1)}, bf16[8,192,1536]{2,1,0:T(8,128)(2,1)S(1)}, u32[]{:S(2)}, u32[]{:S(2)}) collective-permute-start(bf16[8,192,1536]{2,1,0:T(8,128)(2,1)} %add_convert_fusion.4), channel_id=1, source_target_pairs={{0,8},{4,12},{8,0},{12,4},{16,24},{20,28},{24,16},{28,20},{1,9},{5... | collective-permute-start | bytes 14155784 | tf_op jit(solution)/shard_map/ppermute | solution.py:660
  1393.2 174.9 %collective-permute-start.30 = (bf16[8,192,1536]{2,1,0:T(8,128)(2,1)}, bf16[8,192,1536]{2,1,0:T(8,128)(2,1)}, u32[]{:S(2)}, u32[]{:S(2)}) collective-permute-start(bf16[8,192,1536]{2,1,0:T(8,128)(2,1)} %get-tuple-element.228), channel_id=1, source_target_pairs={{0,4},{4,0},{8,12},{12,8},{16,20},{20,16},{24,28},{28,24},{1,5},{5... | collective-permute-start | bytes 14155784 | tf_op jit(solution)/shard_map/ppermute | solution.py:660
  1394.5 173.7 %collective-permute-start.31 = (bf16[8,192,1536]{2,1,0:T(8,128)(2,1)}, bf16[8,192,1536]{2,1,0:T(8,128)(2,1)}, u32[]{:S(2)}, u32[]{:S(2)}) collective-permute-start(bf16[8,192,1536]{2,1,0:T(8,128)(2,1)} %add_convert_fusion.2), channel_id=1, source_target_pairs={{0,8},{4,12},{8,0},{12,4},{16,24},{20,28},{24,16},{28,20},{1,9},{5... | collective-permute-start | bytes 14155784 | tf_op jit(solution)/shard_map/ppermute | solution.py:660
  1410.4 133.2 %collective-permute-start.32 = (bf16[4,192,1536]{2,1,0:T(8,128)(2,1)}, bf16[4,192,1536]{2,1,0:T(8,128)(2,1)}, u32[]{:S(2)}, u32[]{:S(2)}) collective-permute-start(bf16[4,192,1536]{2,1,0:T(8,128)(2,1)} %dynamic-slice_bitcast_fusion), channel_id=1, source_target_pairs={{0,4},{4,0},{8,12},{12,8},{16,20},{20,16},{24,28},{28,24},{1,5},{5... | collective-permute-start | bytes 7077896 | tf_op jit(solution)/shard_map/ppermute | solution.py:660
  1435.3 132.9 %collective-permute-start.29 = (bf16[4,192,1536]{2,1,0:T(8,128)(2,1)}, bf16[4,192,1536]{2,1,0:T(8,128)(2,1)}, u32[]{:S(2)}, u32[]{:S(2)}) collective-permute-start(bf16[4,192,1536]{2,1,0:T(8,128)(2,1)} %slice.427), channel_id=1, source_target_pairs={{0,16},{4,20},{8,24},{12,28},{16,0},{20,4},{24,8},{28,12},{1,17},{... | collective-permute-start | bytes 7077896 | tf_op jit(solution)/shard_map/ppermute | solution.py:660
  1575.3 281.9 %collective-permute-start.35 = (f32[8,1536]{1,0:T(8,128)S(1)}, f32[8,1536]{1,0:T(8,128)S(1)}, u32[]{:S(2)}, u32[]{:S(2)}) collective-permute-start(f32[8,1536]{1,0:T(8,128)S(1)} %fusion.107), channel_id=1, source_target_pairs={{4,0},{8,4},{12,8},{16,12},{20,16},{24,20},{28,24},{5,1},{9,5},{13... | collective-permute-start | bytes 147464 | tf_op jit(solution)/shard_map/ppermute | solution.py:1405
  1584.5 183.5 %collective-permute-start.44 = (bf16[2,192,1536]{2,1,0:T(8,128)(2,1)}, bf16[2,192,1536]{2,1,0:T(8,128)(2,1)}, u32[]{:S(2)}, u32[]{:S(2)}) collective-permute-start(bf16[2,192,1536]{2,1,0:T(8,128)(2,1)} %dynamic-slice_bitcast_fusion.6), channel_id=1, source_target_pairs={{0,8},{4,12},{8,0},{12,4},{16,24},{20,28},{24,16},{28,20},{1,9},{5... | collective-permute-start | bytes 3538952 | tf_op jit(solution)/shard_map/ppermute | solution.py:660
  1591.3 150.9 %collective-permute-start.33 = (bf16[4,192,1536]{2,1,0:T(8,128)(2,1)S(1)}, bf16[4,192,1536]{2,1,0:T(8,128)(2,1)}, u32[]{:S(2)}, u32[]{:S(2)}) collective-permute-start(bf16[4,192,1536]{2,1,0:T(8,128)(2,1)S(1)} %slice.442), channel_id=1, source_target_pairs={{0,16},{4,20},{8,24},{12,28},{16,0},{20,4},{24,8},{28,12},{1,17},{... | collective-permute-start | bytes 7077896 | tf_op jit(solution)/shard_map/ppermute | solution.py:660
  1750.8 45.4 %collective-permute-start.34 = (bf16[4,192,1152]{2,1,0:T(8,128)(2,1)}, bf16[4,192,1152]{2,1,0:T(8,128)(2,1)}, u32[]{:S(2)}, u32[]{:S(2)}) collective-permute-start(bf16[4,192,1152]{2,1,0:T(8,128)(2,1)} %dynamic-slice_bitcast_fusion.1), channel_id=1, source_target_pairs={{0,4},{4,0},{8,12},{12,8},{16,20},{20,16},{24,28},{28,24},{1,5},{5... | collective-permute-start | bytes 5308424 | tf_op jit(solution)/shard_map/ppermute | solution.py:660
  1771.4 97.7 %collective-permute-start.45 = (bf16[1,192,1536]{2,1,0:T(8,128)(2,1)}, bf16[1,192,1536]{2,1,0:T(8,128)(2,1)}, u32[]{:S(2)}, u32[]{:S(2)}) collective-permute-start(bf16[1,192,1536]{2,1,0:T(8,128)(2,1)} %constant_dynamic-slice_fusion.1), channel_id=1, source_target_pairs={{0,16},{4,20},{8,24},{12,28},{16,0},{20,4},{24,8},{28,12},{1,17},{... | collective-permute-start | bytes 1769480 | tf_op jit(solution)/shard_map/ppermute | solution.py:660
  1799.2 34.4 %collective-permute-start.46 = (bf16[2,192,1152]{2,1,0:T(8,128)(2,1)}, bf16[2,192,1152]{2,1,0:T(8,128)(2,1)}, u32[]{:S(2)}, u32[]{:S(2)}) collective-permute-start(bf16[2,192,1152]{2,1,0:T(8,128)(2,1)} %dynamic-slice_bitcast_fusion.7), channel_id=1, source_target_pairs={{0,8},{4,12},{8,0},{12,4},{16,24},{20,28},{24,16},{28,20},{1,9},{5... | collective-permute-start | bytes 2654216 | tf_op jit(solution)/shard_map/ppermute | solution.py:660
  1835.1 19.0 collective-permute-start.47
  1865.5 31.2 %collective-permute-start.37 = (bf16[512,1536]{1,0:T(8,128)(2,1)}, bf16[512,1536]{1,0:T(8,128)(2,1)}, u32[]{:S(2)}, u32[]{:S(2)}) collective-permute-start(bf16[512,1536]{1,0:T(8,128)(2,1)} %get-tuple-element.419), channel_id=1, source_target_pairs={{0,1},{1,0},{2,3},{3,2},{4,5},{5,4},{6,7},{7,6},{8,9},{9,8},{10,11... | collective-permute-start | bytes 4718600 | tf_op jit(solution)/shard_map/ppermute | solution.py:660
  1878.4 56.1 %collective-permute-start.36 = (bf16[512,1536]{1,0:T(8,128)(2,1)}, bf16[512,1536]{1,0:T(8,128)(2,1)}, u32[]{:S(2)}, u32[]{:S(2)}) collective-permute-start(bf16[512,1536]{1,0:T(8,128)(2,1)} %get-tuple-element.418), channel_id=1, source_target_pairs={{0,1},{1,0},{2,3},{3,2},{4,5},{5,4},{6,7},{7,6},{8,9},{9,8},{10,11... | collective-permute-start | bytes 4718600 | tf_op jit(solution)/shard_map/ppermute | solution.py:660
  1900.1 37.1 %collective-permute-start.38 = (bf16[512,1536]{1,0:T(8,128)(2,1)}, bf16[512,1536]{1,0:T(8,128)(2,1)}, u32[]{:S(2)}, u32[]{:S(2)}) collective-permute-start(bf16[512,1536]{1,0:T(8,128)(2,1)} %fusion.24), channel_id=1, source_target_pairs={{0,2},{1,3},{2,0},{3,1},{4,6},{5,7},{6,4},{7,5},{8,10},{9,11},{10,... | collective-permute-start | bytes 4718600 | tf_op jit(solution)/shard_map/ppermute | solution.py:660
  1914.2 19.0 collective-permute-start.52
  (126 other events, 4346.4 us)
Sparse Core Ops, SparseCore 0:
  10.8 237.0 all-gather.7
  383.3 94.1 all-gather.13
  694.5 125.2 all-gather.9
  939.7 142.5 reduce-scatter.3
  1194.2 27.6 reduce-scatter.7
  1224.0 58.0 all-gather.15
  1285.0 105.8 all-gather.11
  1451.7 282.8 reduce-scatter.5
